TPU v7x, 32 devices: a whole 2x2x4 slice. The times are simulated.
32 devices in a mesh: wall: 2 (over x), stream: 4 (over y, core), span: 4 (over z).
Axes of the slice: x: 2, y: 2, z: 4, core: 2. Of those that a mesh axis runs over, the one named last changes fastest.
Arguments:
- potential: float32 [64, 64, 512], P('wall', 'span', 'stream'), may hold values from -1.2 to 1.2
- concentration: float32 [3, 64, 64, 512], P(None, 'wall', 'span', 'stream'), may hold values from 0.2 to 3
- permittivity: float32 [64, 64, 512], P('wall', 'span', 'stream'), may hold values from 0.5 to 2
- fixed_charge: float32 [64, 64, 512], P('wall', 'span', 'stream'), may hold values from -6 to 6
Outputs:
- update: float32 [4, 64, 64, 512], P(None, 'wall', 'span', 'stream')
All inputs are finite; a program needn't handle non-finite values.
Results may differ from a plain program's by a relative error of at most 0.0003.
Values sent between devices are 32-bit elements; how exact they have to be, the bound alone decides.
No kernel may reach another device: no remote copies, remote signals or barrier semaphores. Data moves between devices by JAX's collectives and lax.ppermute only.
A program may use at most 128 MiB of HBM per device.

v0:
```python
import jax
import jax.numpy as jnp
from jax import lax
from jax.sharding import PartitionSpec as P

VALENCE = (1.0, -1.0, 2.0)
MOBILITY = (1.0, 1.5, 0.7)
PLANE_WEIGHT = 0.01


def with_halo(block, sides, width, periodic):
    for axis, dim in sides:
        count = lax.axis_size(axis)
        forward = [(i, i + 1) for i in range(count - 1)]
        if periodic:
            forward.append((count - 1, 0))
        backward = [(target, source) for source, target in forward]
        low = lax.ppermute(
            lax.slice_in_dim(block, block.shape[dim] - width, None, axis=dim), axis, forward
        )
        high = lax.ppermute(lax.slice_in_dim(block, 0, width, axis=dim), axis, backward)
        block = jnp.concatenate([low, block, high], axis=dim)
    return block


def bernoulli(values):
    near_zero = jnp.abs(values) < 0.001
    safe_values = jnp.where(near_zero, 1.0, values)
    series = 1.0 - 0.5 * values + values * values / 12.0
    return jnp.where(near_zero, series, safe_values / jnp.expm1(safe_values))


def block_mul(left_block, right_block):
    return jnp.sum(left_block[:, :, None] * right_block[None, :, :], axis=1)


def invert_small(matrix):
    order_size = matrix.shape[0]
    left_rows = [[matrix[i, j] for j in range(order_size)] for i in range(order_size)]
    blank_entry = jnp.zeros_like(matrix[0, 0])
    right_rows = [
        [blank_entry + (1.0 if i == j else 0.0) for j in range(order_size)]
        for i in range(order_size)
    ]
    for k in range(order_size):
        pivot_inv = 1.0 / left_rows[k][k]
        left_rows[k] = [v * pivot_inv for v in left_rows[k]]
        right_rows[k] = [v * pivot_inv for v in right_rows[k]]
        for i in range(order_size):
            if i != k:
                factor = left_rows[i][k]
                left_rows[i] = [a - factor * b for a, b in zip(left_rows[i], left_rows[k])]
                right_rows[i] = [a - factor * b for a, b in zip(right_rows[i], right_rows[k])]
    return jnp.stack([jnp.stack(r, 0) for r in right_rows], 0)


def block_thomas(lower, diagonal, upper, right_side):

    def forward(carried, row_blocks):
        coupled_prev, solved_prev = carried
        lower_row, diag_row, upper_row, side_row = row_blocks
        reduced = diag_row - block_mul(lower_row, coupled_prev)
        inverse = invert_small(reduced)
        coupled = block_mul(inverse, upper_row)
        solved = block_mul(inverse, side_row - block_mul(lower_row, solved_prev))
        return ((coupled, solved), (coupled, solved))

    initial = (jnp.zeros_like(diagonal[0]), jnp.zeros_like(right_side[0]))
    ignored_end, (coupled_all, solved_all) = lax.scan(
        forward, initial, (lower, diagonal, upper, right_side)
    )

    def backward(following, row_blocks):
        coupled, solved = row_blocks
        current = solved - block_mul(coupled, following)
        return (current, current)

    ignored_start, result = lax.scan(
        backward, jnp.zeros_like(right_side[0]), (coupled_all, solved_all), reverse=True
    )
    return result


def stack_blocks(entries):
    stacked = jnp.stack([jnp.stack([e for e in r], 0) for r in entries], 0)
    return jnp.moveaxis(stacked, 2, 0)


def assemble(center, neighbours, fixed_charge):
    potential, concentration, permittivity = center
    blank_entry = jnp.zeros_like(potential)
    charge = fixed_charge
    for k in range(3):
        charge = charge + VALENCE[k] * concentration[k]
    residual = [-charge, blank_entry, blank_entry, blank_entry]
    jacobian = [[blank_entry] * 4 for i in range(4)]
    lower = [[blank_entry] * 4 for i in range(4)]
    upper = [[blank_entry] * 4 for i in range(4)]
    for k in range(3):
        jacobian[0][k + 1] = blank_entry - VALENCE[k]
    for nearby, inside, weight, position in neighbours:
        near_potential, near_conc, near_perm = nearby
        harmonic = 2.0 * permittivity * near_perm / (permittivity + near_perm)
        face_perm = weight * (inside * harmonic + (1.0 - inside) * permittivity)
        residual[0] = residual[0] + face_perm * (potential - near_potential)
        jacobian[0][0] = jacobian[0][0] + face_perm
        offdiag = lower if position == "lower" else upper if position == "upper" else None
        if offdiag is not None:
            offdiag[0][0] = -inside * face_perm
        for k in range(3):
            drift = VALENCE[k] * (near_potential - potential)
            face_coef = inside * weight * MOBILITY[k]
            weight_out = bernoulli(drift)
            weight_in = bernoulli(-drift)
            mean_conc = 0.5 * (concentration[k] + near_conc[k])
            residual[k + 1] = residual[k + 1] + face_coef * (
                weight_out * concentration[k] - weight_in * near_conc[k]
            )
            jacobian[k + 1][k + 1] = jacobian[k + 1][k + 1] + face_coef * weight_out
            jacobian[k + 1][0] = jacobian[k + 1][0] + face_coef * VALENCE[k] * mean_conc
            if offdiag is not None:
                offdiag[k + 1][k + 1] = -face_coef * weight_in
                offdiag[k + 1][0] = -face_coef * VALENCE[k] * mean_conc
    residual_all = jnp.moveaxis(jnp.stack([e for e in residual], 0), 1, 0)
    return (residual_all, stack_blocks(jacobian), stack_blocks(lower), stack_blocks(upper))


def split_fields(block):
    return (block[0], block[1:4], block[4])


def partition_forward(previous_vec, previous_map, first_tip, last_tip):
    identity = jnp.eye(4, dtype=first_tip.dtype).reshape((4, 4) + (1,) * (first_tip.ndim - 2))
    start_vec = first_tip[:, 0:1]
    start_left = first_tip[:, 1:5]
    start_right = first_tip[:, 5:9]
    end_vec = last_tip[:, 0:1]
    end_left = last_tip[:, 1:5]
    end_right = last_tip[:, 5:9]
    schur_block = identity - block_mul(start_left, previous_map)
    inverse = invert_small(schur_block)
    offset = block_mul(inverse, start_vec + block_mul(start_left, previous_vec))
    reach_map = block_mul(inverse, start_right)
    next_vec = end_vec + block_mul(end_left, previous_vec + block_mul(previous_map, offset))
    next_map = block_mul(end_left, block_mul(previous_map, reach_map)) + end_right
    return (next_vec, next_map, offset, reach_map)


def reduced_sweep(every_tip, zero_vec, zero_map):

    def sweep_forward(carried, tip_pair):
        previous_vec, previous_map = carried
        next_vec, next_map, offset, reach_map = partition_forward(
            previous_vec, previous_map, tip_pair[0], tip_pair[1]
        )
        return ((next_vec, next_map), (previous_vec, previous_map, offset, reach_map))

    ignored_e, (vec_all, map_all, offset_all, reach_all) = lax.scan(
        sweep_forward, (zero_vec, zero_map), every_tip
    )

    def sweep_backward(right_value, pieces):
        offset, reach_map = pieces
        return (offset + block_mul(reach_map, right_value), right_value)

    ignored_f, right_all = lax.scan(sweep_backward, zero_vec, (offset_all, reach_all), reverse=True)
    return (vec_all, map_all, offset_all, reach_all, right_all)


def on_device(potential, concentration, permittivity, fixed_charge):
    cells_wall = potential.shape[0]
    stacked = jnp.concatenate([potential[None], concentration, permittivity[None]], 0)
    walled = with_halo(stacked, (("wall", 1),), 1, False)
    planed = with_halo(stacked, (("stream", 3), ("span", 2)), 1, True)
    center = split_fields(stacked)
    wall_index = lax.axis_index("wall")
    global_row = wall_index * cells_wall + jnp.arange(cells_wall, dtype=jnp.int32)
    line_length = lax.axis_size("wall") * cells_wall
    inside_lower = (global_row > 0).astype(jnp.float32)[:, None, None]
    inside_upper = (global_row < line_length - 1).astype(jnp.float32)[:, None, None]
    neighbours = [
        (split_fields(walled[:, :-2]), inside_lower, 1.0, "lower"),
        (split_fields(walled[:, 2:]), inside_upper, 1.0, "upper"),
        (split_fields(planed[:, :, :-2, 1:-1]), 1.0, PLANE_WEIGHT, "plane"),
        (split_fields(planed[:, :, 2:, 1:-1]), 1.0, PLANE_WEIGHT, "plane"),
        (split_fields(planed[:, :, 1:-1, :-2]), 1.0, PLANE_WEIGHT, "plane"),
        (split_fields(planed[:, :, 1:-1, 2:]), 1.0, PLANE_WEIGHT, "plane"),
    ]
    residual, diagonal, lower, upper = assemble(center, neighbours, fixed_charge)
    row_ids = jnp.arange(cells_wall, dtype=jnp.int32)
    first_mask = (row_ids == 0).astype(jnp.float32)[:, None, None, None, None]
    last_mask = (row_ids == cells_wall - 1).astype(jnp.float32)[:, None, None, None, None]
    right_side = jnp.concatenate(
        [-residual[:, :, None], -lower * first_mask, -upper * last_mask], 2
    )
    solved = block_thomas(lower, diagonal, upper, right_side)
    first_tip = solved[0]
    last_tip = solved[-1]
    lines_shape = first_tip.shape[2:]
    zero_vec = jnp.zeros((4, 1) + lines_shape, jnp.float32)
    zero_map = jnp.zeros((4, 4) + lines_shape, jnp.float32)
    line_tips = jnp.stack([first_tip, last_tip], 0)[None]
    every_tip = lax.all_gather(line_tips, "wall", axis=0, tiled=True)
    vec_all, map_all, offset_all, reach_all, right_all = reduced_sweep(
        every_tip, zero_vec, zero_map
    )

    def choose_own(stacked_all):
        return lax.dynamic_index_in_dim(stacked_all, wall_index, 0, False)

    previous_vec = choose_own(vec_all)
    previous_map = choose_own(map_all)
    offset = choose_own(offset_all)
    reach_map = choose_own(reach_all)
    right_value = choose_own(right_all)
    local_first = offset + block_mul(reach_map, right_value)
    left_value = previous_vec + block_mul(previous_map, local_first)
    update = solved[:, :, 0]
    update = update + jnp.sum(solved[:, :, 1:5] * left_value[None, None, :, 0], axis=2)
    update = update + jnp.sum(solved[:, :, 5:9] * right_value[None, None, :, 0], axis=2)
    return jnp.moveaxis(update, 1, 0)


def solution(mesh):
    return jax.shard_map(
        on_device,
        mesh=mesh,
        in_specs=(
            P("wall", "span", "stream"),
            P(None, "wall", "span", "stream"),
            P("wall", "span", "stream"),
            P("wall", "span", "stream"),
        ),
        out_specs=P(None, "wall", "span", "stream"),
        check_vma=False,
    )
```

profile of v0, /device:TPU:0, one launch (start us, length us, event | category | flops | bytes accessed | tf_op | source)
XLA Modules:
  0.0 408.1 jit_solution(15611558827790788416)
XLA Ops:
  9.5 1.9 copy.103
  12.5 2.0 collective-permute-start.3
  15.1 4.2 %collective-permute-start = (f32[5,1,16,128]{3,2,1,0:T(8,128)}, f32[5,1,16,128]{3,2,1,0:T(8,128)S(1)}, u32[]{:S(2)}, u32[]{:S(2)}) collective-permute-start(f32[5,1,16,128]{3,2,1,0:T(8,128)} %get-tuple-element.649), channel_id=1, source_target_pairs={{0,16},{1,17},{2,18},{3,19},{4,20},{5,21},{6,22},{7,23},{8,24},{9,... | collective-permute-start | bytes 122888 | tf_op jit(solution)/shard_map/ppermute | solution.py:18
  29.5 2.9 pad_maximum_fusion.59
  33.9 2.2 collective-permute-start.5
  36.9 4.7 %collective-permute-done.4 = f32[5,32,1,130]{3,2,1,0:T(1,128)} collective-permute-done((f32[5,32,1,130]{3,2,1,0:T(1,128)}, f32[5,32,1,130]{3,2,1,0:T(1,128)}, u32[]{:S(2)}, u32[]{:S(2)}) %collective-permute-start.4) | collective-permute-done | bytes 83232 | tf_op jit(solution)/shard_map/ppermute | solution.py:18
  43.2 4.1 %fusion.198 = (f32[1,32,16,128]{3,2,1,0:T(8,128)S(1)}, f32[32,16,128]{2,1,0:T(8,128)S(1)}, f32[32,16,128]{2,1,0:T(8,128)S(1)}, f32[32,16,128]{2,1,0:T(8,128)S(1)...) fusion(f32[32,16,128]{2,1,0:T(8,128)} %param.15, ...), kind=kLoop, calls=%fused_computation.459 | loop fusion | flops 6684672 | bytes 9162496 | tf_op jit(solution)/shard_map/stack | solution.py:124
  47.6 3.5 fusion.200
  51.2 4.2 %multiply_bitcast_fusion.2 = (f32[1,32,16,128]{3,2,1,0:T(8,128)S(1)}, f32[1,32,16,128]{3,2,1,0:T(8,128)S(1)}, f32[1,32,16,128]{3,2,1,0:T(8,128)S(1)}, f32[1,32,1...) fusion(f32[32]{0:T(128)S(1)} %copy-done.9, ...), kind=kLoop, calls=%fused_computation.491 | loop fusion | flops 18284544 | bytes 3933696 | tf_op jit(solution)/shard_map/stack | solution.py:85
  55.4 3.5 fusion.202
  59.5 3.4 fusion.201
  64.3 2.5 maximum_bitcast_fusion.6
  67.3 2.4 maximum_bitcast_fusion.5
  70.6 2.4 maximum_bitcast_fusion.4
  73.0 4.2 %pad_maximum_fusion.6 = f32[32,4,9,16,128]{4,3,2,1,0:T(8,128)} fusion(f32[1,32,16,128]{3,2,1,0:T(8,128)S(1)} %get-tuple-element.580, f32[1,32,16,128]{3,2,1,0:T(8,128)S(1)} %get-tuple-element.573, f32[1,32,16,128]{3,2,1,0:T(8,128)S(1)} %get-tuple-element.560, f32[1,32,16,128]{3,2,1,0:T(8,128)S(1)} %get-tuple-element.547, ...), kind=kLoop, calls=%fused_computation.207 | loop fusion | flops 5767168 | bytes 18874368 | tf_op jit(solution)/shard_map/concatenate | solution.py:193
  77.2 4.7 %broadcast.1638.clone = f32[32,4,9,16,128]{4,3,2,1,0:T(8,128)} broadcast(f32[]{:T(128)} %constant.268.clone.1), dimensions={} | broadcast | bytes 9437188 | tf_op jit(solution)/shard_map/broadcast.35
  82.0 156.0 %while.71 = (s32[]{:T(128)}, f32[4,4,16,128]{3,2,1,0:T(8,128)S(1)}, f32[4,9,16,128]{3,2,1,0:T(8,128)S(1)}, f32[32,4,4,16,128]{4,3,2,1,0:T(8,128)}, f32[32,4,9,16...) while((s32[]{:T(128)}, f32[4,4,16,128]{3,2,1,0:T(8,128)S(1)}, ...), condition=%wide.region_5.6_spmd, body=%wide.region_0.5_spmd.sunk | while | flops 2105346 | bytes 6218865 | solution.py:69
  238.0 4.8 %broadcast.1638 = f32[32,4,9,16,128]{4,3,2,1,0:T(8,128)} broadcast(f32[]{:T(128)} %constant.268.clone.1), dimensions={} | broadcast | bytes 9437188 | tf_op jit(solution)/shard_map/broadcast.35
  242.7 121.7 %while.72 = (s32[]{:T(128)}, f32[4,9,16,128]{3,2,1,0:T(8,128)S(1)}, f32[32,4,9,16,128]{4,3,2,1,0:T(8,128)}, f32[32,4,9,16,128]{4,3,2,1,0:T(8,128)}, f32[32,4,4,1...) while((s32[]{:T(128)}, f32[4,9,16,128]{3,2,1,0:T(8,128)S(1)}, ...), condition=%wide.region_8.9_spmd.clone, body=%wide.region_6.8_spmd.clone.sunk | while | flops 737284 | bytes 3342455 | solution.py:78
  259.0 1.8 fusion.260
  262.9 1.8 fusion.260
  366.4 22.9 %all-gather.3.cloned.1.call-done = f32[4,4,9,16,128]{4,3,2,1,0:T(8,128)} async-done(((f32[2,4,9,16,128]{4,3,2,1,0:T(8,128)}), f32[4,4,9,16,128]{4,3,2,1,0:T(8,128)}) %all-gather.3.cloned.1.call-update) | async-done | bytes 1179664 | tf_op jit(solution)/shard_map/all_gather | solution.py:203
  389.3 3.8 while.73
  393.5 5.2 %multiply_reduce_fusion.13 = (f32[32,4,16,128]{3,2,1,0:T(8,128)S(1)}, f32[32,4,16,128]{3,2,1,0:T(8,128)S(1)}) fusion(f32[32,4,9,16,128]{4,3,2,1,0:T(8,128)} %get-tuple-element.306, f32[4,16,128]{2,1,0:T(8,128)S(1)} %bitcast_add_fusion.4, f32[4,16,128]{2,1,0:T(8,128)S(1)} %dynamic-slice_bitcast_fusion.5), kind=kLoop, calls=%fused_computation.212 | loop fusion | flops 3670016 | bytes 10551296 | tf_op jit(solution)/shard_map/reduce_sum | solution.py:219
  (981 shorter events, 300.2 us)
Async XLA Ops:
  6.5 382.8 %all-gather.3.cloned.1.call-start = ((), (), s32[]{:S(2)}) async-start(), calls=%async_computation | async-start | bytes 1769472 | tf_op jit(solution)/shard_map/all_gather | solution.py:203
  7.9 6.5 %copy-start = (f32[3,32,16,128]{3,2,1,0:T(8,128)S(1)}, f32[3,32,16,128]{3,2,1,0:T(8,128)}, u32[]{:S(2)}) copy-start(f32[3,32,16,128]{3,2,1,0:T(8,128)} %param.13) | copy-start | bytes 2359300
  7.9 6.5 %copy-start.1 = (f32[32,16,128]{2,1,0:T(8,128)S(1)}, f32[32,16,128]{2,1,0:T(8,128)}, u32[]{:S(2)}) copy-start(f32[32,16,128]{2,1,0:T(8,128)} %param.12) | copy-start | bytes 786436
  8.0 6.5 %copy-start.3 = (f32[32,16,128]{2,1,0:T(8,128)S(1)}, f32[32,16,128]{2,1,0:T(8,128)}, u32[]{:S(2)}) copy-start(f32[32,16,128]{2,1,0:T(8,128)} %param.14) | copy-start | bytes 786436
  11.4 16.0 %collective-permute-start.2 = (f32[5,32,16,1]{1,2,3,0:T(8,128)S(1)}, f32[5,32,16,1]{1,2,3,0:T(8,128)S(1)}, u32[]{:S(2)}, u32[]{:S(2)}) collective-permute-start(f32[5,32,16,1]{1,2,3,0:T(8,128)S(1)} %copy.103), channel_id=1, source_target_pairs={{0,4},{4,8},{8,12},{12,0},{1,5},{5,9},{9,13},{13,1},{2,6},{6,10},{... | collective-permute-start | bytes 30728 | tf_op jit(solution)/shard_map/ppermute | solution.py:18
  12.5 15.6 %collective-permute-start.3 = (f32[5,32,16,1]{1,2,3,0:T(8,128)S(1)}, f32[5,32,16,1]{1,2,3,0:T(8,128)}, u32[]{:S(2)}, u32[]{:S(2)}) collective-permute-start(f32[5,32,16,1]{1,2,3,0:T(8,128)S(1)} %copy.104), channel_id=1, source_target_pairs={{4,0},{8,4},{12,8},{0,12},{5,1},{9,5},{13,9},{1,13},{6,2},{10,6},{... | collective-permute-start | bytes 30728 | tf_op jit(solution)/shard_map/ppermute | solution.py:21
  15.1 21.8 %collective-permute-start = (f32[5,1,16,128]{3,2,1,0:T(8,128)}, f32[5,1,16,128]{3,2,1,0:T(8,128)S(1)}, u32[]{:S(2)}, u32[]{:S(2)}) collective-permute-start(f32[5,1,16,128]{3,2,1,0:T(8,128)} %get-tuple-element.649), channel_id=1, source_target_pairs={{0,16},{1,17},{2,18},{3,19},{4,20},{5,21},{6,22},{7,23},{8,24},{9,... | collective-permute-start | bytes 122888 | tf_op jit(solution)/shard_map/ppermute | solution.py:18
  19.3 17.7 %collective-permute-start.1 = (f32[5,1,16,128]{3,2,1,0:T(8,128)S(1)}, f32[5,1,16,128]{3,2,1,0:T(8,128)S(1)}, u32[]{:S(2)}, u32[]{:S(2)}) collective-permute-start(f32[5,1,16,128]{3,2,1,0:T(8,128)S(1)} %get-tuple-element.650), channel_id=1, source_target_pairs={{16,0},{17,1},{18,2},{19,3},{20,4},{21,5},{22,6},{23,7},{24,8},{25... | collective-permute-start | bytes 122888 | tf_op jit(solution)/shard_map/ppermute | solution.py:21
  32.3 9.3 %collective-permute-start.4 = (f32[5,32,1,130]{3,2,1,0:T(1,128)}, f32[5,32,1,130]{3,2,1,0:T(1,128)}, u32[]{:S(2)}, u32[]{:S(2)}) collective-permute-start(f32[5,32,1,130]{3,2,1,0:T(1,128)} %get-tuple-element.643), channel_id=1, source_target_pairs={{0,1},{1,2},{2,3},{3,0},{4,5},{5,6},{6,7},{7,4},{8,9},{9,10},{10,1... | collective-permute-start | bytes 249608 | tf_op jit(solution)/shard_map/ppermute | solution.py:18
  33.9 9.3 %collective-permute-start.5 = (f32[5,32,1,130]{3,2,1,0:T(1,128)}, f32[5,32,1,130]{3,2,1,0:T(1,128)}, u32[]{:S(2)}, u32[]{:S(2)}) collective-permute-start(f32[5,32,1,130]{3,2,1,0:T(1,128)} %get-tuple-element.642), channel_id=1, source_target_pairs={{1,0},{2,1},{3,2},{0,3},{5,4},{6,5},{7,6},{4,7},{9,8},{10,9},{11,1... | collective-permute-start | bytes 249608 | tf_op jit(solution)/shard_map/ppermute | solution.py:21
  43.2 4.1 %copy-start.8 = (f32[32]{0:T(128)S(1)}, f32[32]{0:T(128)}, u32[]{:S(2)}) copy-start(f32[32]{0:T(128)} %get-tuple-element.690) | copy-start | bytes 388
  43.2 4.1 %copy-start.9 = (f32[32]{0:T(128)S(1)}, f32[32]{0:T(128)}, u32[]{:S(2)}) copy-start(f32[32]{0:T(128)} %get-tuple-element.700) | copy-start | bytes 388
  43.2 4.3 %copy-start.2 = (f32[32,16,128]{2,1,0:T(8,128)S(1)}, f32[32,16,128]{2,1,0:T(8,128)}, u32[]{:S(2)}) copy-start(f32[32,16,128]{2,1,0:T(8,128)} %param.12) | copy-start | bytes 786436
  43.2 4.3 %copy-start.4 = (f32[32,16,128]{2,1,0:T(8,128)S(1)}, f32[32,16,128]{2,1,0:T(8,128)}, u32[]{:S(2)}) copy-start(f32[32,16,128]{2,1,0:T(8,128)} %param.14) | copy-start | bytes 786436
  47.5 3.6 copy-start.6
  47.5 3.6 copy-start.7
  47.5 3.6 copy-start.22
  47.6 3.6 copy-start.23
  55.3 3.6 copy-start.18
  59.5 3.8 copy-start.11
  59.5 3.8 copy-start.12
  59.5 3.8 copy-start.14
  59.5 3.8 copy-start.15
  238.0 4.8 %copy-start.5 = (f32[4,9,16,128]{3,2,1,0:T(8,128)S(1)}, f32[4,9,16,128]{3,2,1,0:T(8,128)}, u32[]{:S(2)}) copy-start(f32[4,9,16,128]{3,2,1,0:T(8,128)} %custom-call) | copy-start | bytes 884740
  (7 other events, 22.5 us)
Sparse Core Ops, SparseCore 0:
  366.5 22.7 all-gather.2
where the time goes:
time: 414 us; the launch traced here: 408 us
  other arithmetic  221 us (53%)
  local copies, waits for them, and re-layouts  127 us (31%)
  waiting for transfers between devices  29.2 us (7%)
  between operations  14 us (3%)
  starting transfers between devices  11.8 us (3%)
  loops' own time  4.99 us (1%)
    mul x65, local copies, waits for them, and re-layouts, block_mul(): return jnp.sum(left_block[:, :, None] * right_block[None, :, :], axis=1)  61 us
    dynamic_update_slice x32, other arithmetic, block_thomas(): lax.scan(forward, initial, (lower, diagonal, upper, right_side))  55.3 us
    dynamic_update_slice x64, local copies, waits for them, and re-layouts, block_thomas(): lax.scan(forward, initial, (lower, diagonal, upper, right_side))  45.3 us
    mul x41, other arithmetic, block_mul(): return jnp.sum(left_block[:, :, None] * right_block[None, :, :], axis=1)  32.3 us
    sub x32, other arithmetic, backward(): current = solved - block_mul(coupled, following)  32 us
    sub x32, other arithmetic, forward(): reduced = diag_row - block_mul(lower_row, coupled_prev)  30 us
    all_gather x1, waiting for transfers between devices, on_device(): every_tip = lax.all_gather(line_tips, 'wall', axis=0, tiled=True)  22.9 us
    another operation x4, other arithmetic, assemble(): residual_all = jnp.moveaxis(jnp.stack([e for e in residual], 0), 1, 0)  14.6 us
  transfers between devices with their start and end apart: 7, of which 3 were waited for; matrix products, arithmetic and copies ran while one was open for 3% of the time, Pallas kernels for 0%

commit v1 on v0

--- a/solution.py
+++ b/solution.py
@@ -1,11 +1,465 @@
+import functools
+
 import jax
 import jax.numpy as jnp
 from jax import lax
+from jax.experimental import pallas as pl
+from jax.experimental.pallas import tpu as pltpu
 from jax.sharding import PartitionSpec as P
 
 VALENCE = (1.0, -1.0, 2.0)
 MOBILITY = (1.0, 1.5, 0.7)
+HALF_ZD = tuple(0.5 * z * d for z, d in zip(VALENCE, MOBILITY))
 PLANE_WEIGHT = 0.01
+LANES = 128
+SUB = 8
+NQ = 11
+
+VMEM = pl.BlockSpec(memory_space=pltpu.VMEM)
+SMEM = pl.BlockSpec(memory_space=pltpu.SMEM)
+
+
+def sds(*shape):
+    return jax.ShapeDtypeStruct(shape, jnp.float32)
+
+
+def params(mib=8):
+    return pltpu.CompilerParams(vmem_limit_bytes=mib * 1024 * 1024)
+
+
+def face(phi, eps, conc, phi_m, eps_m, conc_m, weight):
+    x = phi_m - phi
+    y = 0.5 * x
+    y = jnp.where(y == 0.0, 1e-20, y)
+    t = jnp.tanh(y)
+    h = y * pl.reciprocal(t, approx=True)
+    e = (eps * eps_m) * pl.reciprocal(eps + eps_m, approx=True)
+    if weight is None:
+        e = e + e
+        h2 = h + y * t
+        xw, yw, hw = x, y, h
+    else:
+        e = e * (weight + weight)
+        hw = h * weight
+        yw = y * weight
+        xw = yw + yw
+        h2 = hw + yw * t
+    p1 = hw - yw
+    m1 = hw + yw
+    out = (p1, 1.5 * m1, 0.7 * (h2 - xw))
+    into = (m1, 1.5 * p1, 0.7 * (h2 + xw))
+    g = e * x
+    flux = tuple(out[k] * conc[k] - into[k] * conc_m[k] for k in range(3))
+    return e, g, out, into, flux
+
+
+def inv2(a, b, c, d):
+    r = pl.reciprocal(a * d - b * c, approx=True)
+    return d * r, b * r, c * r, a * r
+
+
+def inverse4(D):
+    a0, a1, a2, a3 = inv2(D[0][0], D[0][1], D[1][0], D[1][1])
+    A = ((a0, -a1), (-a2, a3))
+    E = [[D[2 + i][0] * A[0][j] + D[2 + i][1] * A[1][j] for j in range(2)] for i in range(2)]
+    S = [
+        [D[2 + i][2 + j] - (E[i][0] * D[0][2 + j] + E[i][1] * D[1][2 + j]) for j in range(2)]
+        for i in range(2)
+    ]
+    s0, s1, s2, s3 = inv2(S[0][0], S[0][1], S[1][0], S[1][1])
+    I = ((s0, -s1), (-s2, s3))
+    F = [[A[i][0] * D[0][2 + j] + A[i][1] * D[1][2 + j] for j in range(2)] for i in range(2)]
+    X = [[I[i][0] * E[0][j] + I[i][1] * E[1][j] for j in range(2)] for i in range(2)]
+    Y = [[F[i][0] * I[0][j] + F[i][1] * I[1][j] for j in range(2)] for i in range(2)]
+    Z = [[A[i][j] + (F[i][0] * X[0][j] + F[i][1] * X[1][j]) for j in range(2)] for i in range(2)]
+    return [
+        [Z[0][0], Z[0][1], -Y[0][0], -Y[0][1]],
+        [Z[1][0], Z[1][1], -Y[1][0], -Y[1][1]],
+        [-X[0][0], -X[0][1], I[0][0], I[0][1]],
+        [-X[1][0], -X[1][1], I[1][0], I[1][1]],
+    ]
+
+
+def mat_vec(G, v):
+    return [(G[i][0] * v[0] + G[i][1] * v[1]) + (G[i][2] * v[2] + G[i][3] * v[3]) for i in range(4)]
+
+
+def couple(D, r, e, m, f, T, s):
+    Dn = [[D[0][j] - e * T[0][j] for j in range(4)]]
+    rn = [r[0] + e * s[0]]
+    for k in range(3):
+        Dn.append([D[k + 1][j] - (m[k] * T[0][j] + f[k] * T[k + 1][j]) for j in range(4)])
+        rn.append(r[k + 1] + (m[k] * s[0] + f[k] * s[k + 1]))
+    return Dn, rn
+
+
+def solve_block(D, r, e, m, f):
+    G = inverse4(D)
+    first = mat_vec(G, [e] + list(m))
+    T = [[first[i]] + [G[i][k + 1] * f[k] for k in range(3)] for i in range(4)]
+    return T, mat_vec(G, r)
+
+
+def pack_kernel(
+    rows, planes, where_ref, phi_hbm, conc_hbm, eps_hbm, charge_hbm,
+    phi_ref, conc_ref, eps_ref, charge_ref, near_ref, far_ref, cols_ref, sems,
+):
+    copies = [
+        pltpu.make_async_copy(src, dst, sems.at[i])
+        for i, (src, dst) in enumerate(
+            (
+                (conc_hbm, conc_ref),
+                (phi_hbm, phi_ref),
+                (eps_hbm, eps_ref),
+                (charge_hbm, charge_ref),
+            )
+        )
+    ]
+    for copy in copies:
+        copy.start()
+    for copy in copies:
+        copy.wait()
+    odd = where_ref[1] > 0
+    views = [phi_ref, conc_ref.at[0], conc_ref.at[1], conc_ref.at[2], eps_ref]
+    even_lane = lax.broadcasted_iota(jnp.int32, (SUB, LANES), 1)
+    for f, ref in enumerate(views):
+        low = ref[pl.ds(0, rows, stride=planes), :]
+        high = ref[pl.ds(planes - 1, rows, stride=planes), :]
+        near_ref[f] = jnp.where(odd, low, high)
+        far_ref[f] = jnp.where(odd, high, low)
+    for f, ref in enumerate(views):
+        packed = jnp.zeros((SUB, LANES), jnp.float32)
+        for j in range(rows * planes // SUB):
+            moved = pltpu.roll(ref[SUB * j : SUB * (j + 1), :], 2 * j + 1, 1)
+            packed = jnp.where((even_lane // 2) == j, moved, packed)
+        cols_ref[f] = packed
+
+
+def assemble_kernel(
+    rows, planes, where_ref, phi_ref, conc_ref, eps_ref, charge_ref,
+    acc_ref, fe_ref, fu_ref, span_ref,
+):
+    wall = where_ref[0]
+    first_wall = (wall == 0).astype(jnp.float32)
+    last_wall = 1.0 - first_wall
+
+    def cell(p, row0):
+        at = pl.ds(row0 * planes + p, SUB, stride=planes)
+        return phi_ref[at, :], eps_ref[at, :], [conc_ref[k, at, :] for k in range(3)]
+
+    for row0 in range(0, rows, SUB):
+        zero = jnp.zeros((SUB, LANES), jnp.float32)
+        carry = [zero] * NQ
+        phi, eps, conc = cell(0, row0)
+        for p in range(planes):
+            total = list(carry)
+            if p + 1 < planes:
+                phi_m, eps_m, conc_m = cell(p + 1, row0)
+                e, g, out, into, flux = face(phi, eps, conc, phi_m, eps_m, conc_m, PLANE_WEIGHT)
+                mine = [e, g, *out, *flux, *conc_m]
+                total = [a + b for a, b in zip(total, mine)]
+                carry = [e, -g, *into, *[-v for v in flux], *conc]
+                phi, eps, conc = phi_m, eps_m, conc_m
+            for q in range(NQ):
+                span_ref[q, p * rows + row0 : p * rows + row0 + SUB, :] = total[q]
+
+    lane = lax.broadcasted_iota(jnp.int32, (planes, LANES), 1)
+    weight = jnp.where(lane < LANES - 1, PLANE_WEIGHT, 0.0).astype(jnp.float32)
+
+    def load(r):
+        at = pl.ds(pl.multiple_of(r * planes, planes), planes)
+        return phi_ref[at, :], eps_ref[at, :], [conc_ref[k, at, :] for k in range(3)]
+
+    def finish(r, phi, eps, conc, lower, upper):
+        at = pl.ds(pl.multiple_of(r * planes, planes), planes)
+
+        def fwd(v):
+            return pltpu.roll(v, LANES - 1, 1)
+
+        def back(v):
+            return pltpu.roll(v, 1, 1)
+
+        conc_m = [fwd(c) for c in conc]
+        e, g, out, into, flux = face(phi, eps, conc, fwd(phi), fwd(eps), conc_m, weight)
+        span = [span_ref[q, pl.ds(r, planes, stride=rows), :] for q in range(NQ)]
+        total_e = (e + back(e)) + (lower[0] + upper[0]) + span[0]
+        total_g = (g - back(g)) + (lower[1] + upper[1]) + span[1]
+        charge = charge_ref[at, :] + conc[0] - conc[1] + 2.0 * conc[2]
+        acc_ref[0, at, :] = total_e
+        acc_ref[1, at, :] = total_g + charge
+        for k in range(3):
+            acc_ref[2 + k, at, :] = (out[k] + back(into[k])) + (lower[2][k] + upper[2][k]) + span[2 + k]
+            acc_ref[5 + k, at, :] = -(
+                (flux[k] - back(flux[k])) + (lower[3][k] + upper[3][k]) + span[5 + k]
+            )
+            near = conc_m[k] + back(conc[k]) + span[8 + k] + 4.0 * conc[k]
+            acc_ref[8 + k, at, :] = (HALF_ZD[k] * PLANE_WEIGHT) * near + HALF_ZD[k] * (
+                lower[4][k] + upper[4][k]
+            )
+
+    zero = jnp.zeros((planes, LANES), jnp.float32)
+    zeros = [zero] * 3
+
+    phi, eps, conc = load(0)
+    e = first_wall * eps
+    lower = (e, -e * phi, zeros, zeros, zeros)
+
+    def step(r, carry):
+        phi, eps, conc, lower = carry
+        phi_m, eps_m, conc_m = load(r + 1)
+        e, g, out, into, flux = face(phi, eps, conc, phi_m, eps_m, conc_m, None)
+        at = pl.ds(pl.multiple_of(r * planes, planes), planes)
+        fe_ref[at, :] = e
+        for k in range(3):
+            fu_ref[wall, k, at, :] = into[k]
+            fu_ref[1 - wall, k, at, :] = out[k]
+        both = [conc[k] + conc_m[k] for k in range(3)]
+        upper = (e, g, out, flux, both)
+        finish(r, phi, eps, conc, lower, upper)
+        lower = (e, -g, list(into), [-v for v in flux], both)
+        return phi_m, eps_m, conc_m, lower
+
+    phi, eps, conc, lower = lax.fori_loop(0, rows - 1, step, (phi, eps, conc, lower))
+    e = last_wall * eps
+    upper = (e, -e * phi, zeros, zeros, zeros)
+    finish(rows - 1, phi, eps, conc, lower, upper)
+
+
+def halo_terms(own, near, wrapped):
+    e, g, out, _, flux = face(own[0], own[4], own[1:4], near[0], near[4], near[1:4], PLANE_WEIGHT)
+    c = [near[1 + k] if wrapped is None else near[1 + k] - wrapped[1 + k] for k in range(3)]
+    return [e, g, *out, *[-v for v in flux], *[(HALF_ZD[k] * PLANE_WEIGHT) * c[k] for k in range(3)]]
+
+
+def eliminate_kernel(
+    rows, planes, where_ref, phi_ref, conc_ref, eps_ref, acc_ref, fe_ref, fu_ref,
+    near_ref, far_ref, near_halo_ref, far_halo_ref, cols_ref, even_halo_ref, odd_halo_ref,
+    t_ref, s_ref, tip_ref, side_ref, rim_ref,
+):
+    wall = where_ref[0]
+    span_odd = where_ref[1]
+    stream_odd = where_ref[2] > 0
+
+    for own_ref, halo_ref, side in (
+        (near_ref, near_halo_ref, 1 - span_odd),
+        (far_ref, far_halo_ref, span_odd),
+    ):
+        own = [own_ref[f] for f in range(5)]
+        near = [halo_ref[f] for f in range(5)]
+        for q, v in enumerate(halo_terms(own, near, None)):
+            rim_ref[q, side] = v
+
+    odd = lax.broadcasted_iota(jnp.int32, (SUB, LANES), 1) % 2 == 1
+    own, near, wrapped = [], [], []
+    for f in range(5):
+        mine, a, b = cols_ref[f], even_halo_ref[f], odd_halo_ref[f]
+        right = jnp.where(stream_odd, b, a)
+        left = jnp.where(stream_odd, a, b)
+        own.append(mine)
+        near.append(jnp.where(odd, pltpu.roll(left, 1, 1), pltpu.roll(right, LANES - 1, 1)))
+        wrapped.append(jnp.where(odd, pltpu.roll(mine, 1, 1), pltpu.roll(mine, LANES - 1, 1)))
+    for q, v in enumerate(halo_terms(own, near, wrapped)):
+        side_ref[q] = v
+
+    lane = lax.broadcasted_iota(jnp.int32, (planes, LANES), 1)
+    edge = (lane == 0) | (lane == LANES - 1)
+    plane = lax.broadcasted_iota(jnp.int32, (planes, LANES), 0)
+    low_plane, high_plane = plane == 0, plane == planes - 1
+
+    def place(i):
+        return jnp.where(wall == 0, i, rows - 1 - i)
+
+    def own_block(i):
+        r = place(i)
+        at = pl.ds(pl.multiple_of(r * planes, planes), planes)
+        q_all = []
+        for q in range(NQ):
+            side = side_ref[q]
+            parts = [
+                pltpu.roll(side, LANES - 1 - 2 * ((planes // SUB) * r + part), 1)
+                for part in range(planes // SUB)
+            ]
+            moved = jnp.where(edge, jnp.concatenate(parts, 0), 0.0)
+            low = jnp.broadcast_to(rim_ref[q, 0, pl.ds(r, 1), :], (planes, LANES))
+            high = jnp.broadcast_to(rim_ref[q, 1, pl.ds(r, 1), :], (planes, LANES))
+            rim = jnp.where(low_plane, low, jnp.where(high_plane, high, 0.0))
+            q_all.append(acc_ref[q, at, :] + (moved + rim))
+        a, d, b = q_all[0], q_all[2:5], q_all[8:11]
+        one = jnp.ones_like(a)
+        zero = jnp.zeros_like(a)
+        D = [
+            [a, -one, one, -2.0 * one],
+            [b[0], d[0], zero, zero],
+            [b[1], zero, d[1], zero],
+            [b[2], zero, zero, d[2]],
+        ]
+        return at, D, [q_all[1], *q_all[5:8]]
+
+    def next_face(i):
+        r = place(i)
+        r_next = place(i + 1)
+        at = pl.ds(pl.multiple_of(r * planes, planes), planes)
+        at_next = pl.ds(pl.multiple_of(r_next * planes, planes), planes)
+        at_face = pl.ds(pl.multiple_of(jnp.minimum(r, r_next) * planes, planes), planes)
+        m = [HALF_ZD[k] * (conc_ref[k, at, :] + conc_ref[k, at_next, :]) for k in range(3)]
+        up = [fu_ref[0, k, at_face, :] for k in range(3)]
+        low = [fu_ref[1, k, at_face, :] for k in range(3)]
+        return fe_ref[at_face, :], m, up, low
+
+    def reduce_row(i, carry):
+        at, D, r = own_block(i)
+        if carry is not None:
+            T, s, e, m, low = carry
+            D, r = couple(D, r, e, m, low, T, s)
+        return at, D, r
+
+    def step(i, carry):
+        at, D, r = reduce_row(i, carry)
+        e, m, up, low = next_face(i)
+        T, s = solve_block(D, r, e, m, up)
+        for a in range(4):
+            for b in range(4):
+                t_ref[4 * a + b, at, :] = T[a][b]
+            s_ref[a, at, :] = s[a]
+        return T, s, e, m, low
+
+    carry = step(0, None)
+    carry = lax.fori_loop(1, rows - 1, step, carry)
+    at, D, r = reduce_row(rows - 1, carry)
+    for a in range(4):
+        for b in range(4):
+            tip_ref[4 * a + b] = D[a][b]
+        tip_ref[16 + a] = r[a]
+    tip_ref[20] = phi_ref[at, :]
+    for k in range(3):
+        tip_ref[21 + k] = conc_ref[k, at, :]
+    tip_ref[24] = eps_ref[at, :]
+
+
+def tip_block(ref):
+    D = [[ref[4 * a + b] for b in range(4)] for a in range(4)]
+    r = [ref[16 + a] for a in range(4)]
+    return D, r, ref[20], [ref[21 + k] for k in range(3)], ref[24]
+
+
+def with_face(D, r, e, g, m, out, flux):
+    D = [list(row) for row in D]
+    r = list(r)
+    D[0][0] = D[0][0] + e
+    r[0] = r[0] + g
+    for k in range(3):
+        D[k + 1][k + 1] = D[k + 1][k + 1] + out[k]
+        D[k + 1][0] = D[k + 1][0] + m[k]
+        r[k + 1] = r[k + 1] - flux[k]
+    return D, r
+
+
+def substitute_kernel(rows, planes, where_ref, own_ref, near_ref, t_ref, s_ref, out_ref):
+    wall = where_ref[0]
+    D, r, phi, conc, eps = tip_block(own_ref)
+    Dm, rm, phi_m, conc_m, eps_m = tip_block(near_ref)
+    e, g, out, into, flux = face(phi, eps, conc, phi_m, eps_m, conc_m, None)
+    m = [HALF_ZD[k] * (conc[k] + conc_m[k]) for k in range(3)]
+    Dm, rm = with_face(Dm, rm, e, -g, m, into, [-v for v in flux])
+    T, s = solve_block(Dm, rm, e, m, out)
+    D, r = with_face(D, r, e, g, m, out, flux)
+    D, r = couple(D, r, e, m, into, T, s)
+    x = mat_vec(inverse4(D), r)
+
+    def put(i, x):
+        row = jnp.where(wall == 0, i, rows - 1 - i)
+        at = pl.ds(pl.multiple_of(row * planes, planes), planes)
+        for a in range(4):
+            out_ref[a, at, :] = x[a]
+
+    put(rows - 1, x)
+
+    def step(j, x):
+        i = rows - 2 - j
+        row = jnp.where(wall == 0, i, rows - 1 - i)
+        at = pl.ds(pl.multiple_of(row * planes, planes), planes)
+        T = [[t_ref[4 * a + b, at, :] for b in range(4)] for a in range(4)]
+        x = [v + s_ref[a, at, :] for a, v in enumerate(mat_vec(T, x))]
+        put(i, x)
+        return x
+
+    lax.fori_loop(0, rows - 1, step, x)
+
+
+def swap_pairs(count, first):
+    pairs = []
+    for i in range(first, count + first, 2):
+        a, b = i % count, (i + 1) % count
+        pairs += [(a, b), (b, a)]
+    return pairs
+
+
+def on_device_pair(potential, concentration, permittivity, fixed_charge):
+    rows, planes, cols = potential.shape
+    cells = rows * planes
+    phi = potential.reshape(cells, cols)
+    conc = concentration.reshape(3, cells, cols)
+    eps = permittivity.reshape(cells, cols)
+    charge = fixed_charge.reshape(cells, cols)
+    n_span, n_stream = lax.axis_size("span"), lax.axis_size("stream")
+    where = jnp.stack(
+        [lax.axis_index("wall"), lax.axis_index("span") % 2, lax.axis_index("stream") % 2]
+    ).astype(jnp.int32)
+
+    phi, conc, eps, charge, near, far, edge_cols = pl.pallas_call(
+        functools.partial(pack_kernel, rows, planes),
+        out_shape=(
+            sds(cells, cols), sds(3, cells, cols), sds(cells, cols), sds(cells, cols),
+            sds(5, rows, cols), sds(5, rows, cols), sds(5, SUB, LANES),
+        ),
+        in_specs=[SMEM] + [pl.BlockSpec(memory_space=pltpu.HBM)] * 4,
+        out_specs=(VMEM,) * 7,
+        scratch_shapes=[pltpu.SemaphoreType.DMA((4,))],
+        compiler_params=params(),
+    )(where, *(pltpu.with_memory_space_constraint(v, pltpu.HBM) for v in (phi, conc, eps, charge)))
+
+    far_halo = lax.ppermute(far, "span", swap_pairs(n_span, 1))
+    near_halo = lax.ppermute(near, "span", swap_pairs(n_span, 0))
+    odd_halo = lax.ppermute(edge_cols, "stream", swap_pairs(n_stream, 1))
+    even_halo = lax.ppermute(edge_cols, "stream", swap_pairs(n_stream, 0))
+
+    acc, fe, fu = pl.pallas_call(
+        functools.partial(assemble_kernel, rows, planes),
+        out_shape=(sds(NQ, cells, cols), sds(cells, cols), sds(2, 3, cells, cols)),
+        in_specs=[SMEM] + [VMEM] * 4,
+        out_specs=(VMEM,) * 3,
+        scratch_shapes=[pltpu.VMEM((NQ, cells, cols), jnp.float32)],
+        compiler_params=params(),
+        cost_estimate=pl.CostEstimate(flops=12_000_000, bytes_accessed=6_000_000, transcendentals=0),
+    )(where, phi, conc, eps, charge)
+
+    T, s, tip = pl.pallas_call(
+        functools.partial(eliminate_kernel, rows, planes),
+        out_shape=(
+            sds(16, cells, cols), sds(4, cells, cols), sds(25, planes, cols)
+        ),
+        in_specs=[SMEM] + [VMEM] * 13,
+        out_specs=(VMEM,) * 3,
+        scratch_shapes=[
+            pltpu.VMEM((NQ, SUB, LANES), jnp.float32),
+            pltpu.VMEM((NQ, 2, rows, LANES), jnp.float32),
+        ],
+        compiler_params=params(),
+    )(
+        where, phi, conc, eps, acc, fe, fu, near, far, near_halo, far_halo, edge_cols,
+        even_halo, odd_halo,
+    )
+
+    tip_m = lax.ppermute(tip, "wall", [(0, 1), (1, 0)])
+
+    update = pl.pallas_call(
+        functools.partial(substitute_kernel, rows, planes),
+        out_shape=sds(4, cells, cols),
+        in_specs=[SMEM] + [VMEM] * 4,
+        out_specs=VMEM,
+        compiler_params=params(),
+    )(where, tip, tip_m, T, s)
+    return update.reshape(4, rows, planes, cols)
 
 
 def with_halo(block, sides, width, periodic):
@@ -221,9 +675,24 @@
     return jnp.moveaxis(update, 1, 0)
 
 
+def on_any(potential, concentration, permittivity, fixed_charge):
+    rows, planes, cols = potential.shape
+    pair = (
+        lax.axis_size("wall") == 2
+        and lax.axis_size("span") % 2 == 0
+        and lax.axis_size("stream") % 2 == 0
+        and cols == LANES
+        and rows % SUB == 0
+        and planes % SUB == 0
+        and rows * planes // SUB * 2 <= LANES
+    )
+    chosen = on_device_pair if pair else on_device
+    return chosen(potential, concentration, permittivity, fixed_charge)
+
+
 def solution(mesh):
     return jax.shard_map(
-        on_device,
+        on_any,
         mesh=mesh,
         in_specs=(
             P("wall", "span", "stream"),

time: 414 us -> 31.6 us (0.08); the launches traced: 408 us -> 31.5 us
  other arithmetic: 221 us -> 0.08 us
  local copies, waits for them, and re-layouts: 127 us -> 0 us
  waiting for transfers between devices: 29.2 us -> 5.51 us
  Pallas kernels: 0 us -> 17.1 us
  between operations: 14 us -> 0.06 us
  loops' own time: 4.99 us -> 0 us
    sub x237 -> x0, other arithmetic: 66.7 us -> none  [the longest x32 32 us: backward(): current = solved - block_mul(coupled, following)]
    mul x65 -> x0, local copies, waits for them, and re-layouts: 61 us -> none  [block_mul(): return jnp.sum(left_block[:, :, None] * right_block[None, :, :], axis=1)]
    dynamic_update_slice x38 -> x0, other arithmetic: 55.4 us -> none  [the longest x32 55.3 us: block_thomas(): lax.scan(forward, initial, (lower, diagonal, upper, right_side))]
    dynamic_update_slice x66 -> x0, local copies, waits for them, and re-layouts: 45.3 us -> none  [the longest x64 45.3 us: block_thomas(): lax.scan(forward, initial, (lower, diagonal, upper, right_side))]
    mul x88 -> x0, other arithmetic: 39 us -> none  [the longest x41 32.3 us: block_mul(): return jnp.sum(left_block[:, :, None] * right_block[None, :, :], axis=1)]
    all_gather x1 -> x0, waiting for transfers between devices: 22.9 us -> none  [on_device(): every_tip = lax.all_gather(line_tips, 'wall', axis=0, tiled=True)]
    another operation x183 -> x1, other arithmetic: 22 us -> 0.08 us  [on_device_pair(): jnp.stack([lax.axis_index('wall'), lax.axis_index('span') % 2, lax.axis_i...]
    reduce_sum x177 -> x0, other arithmetic: 17.2 us -> none  [the longest x176 12 us: block_mul(): return jnp.sum(left_block[:, :, None] * right_block[None, :, :], axis=1)]
  transfers between devices with their start and end apart: 7 -> 5, of which waited for: 3 -> 1; matrix products, arithmetic and copies ran while one was open for 3% -> 0% of each run, Pallas kernels for 0% -> 22%
where the time goes in v1:
time: 31.6 us; the launch traced here: 31.5 us
  Pallas kernels  17.1 us (54%)
  starting transfers between devices  8.75 us (28%)
  waiting for transfers between devices  5.51 us (17%)
    pallas_call x1, Pallas kernels, on_device_pair(): pl.pallas_call(functools.partial(assemble_kernel, rows, planes), out_shap...  7.04 us
    ppermute x1, waiting for transfers between devices, on_device_pair(): tip_m = lax.ppermute(tip, 'wall', [(0, 1), (1, 0)])  5.5 us
    pallas_call x1, Pallas kernels, on_device_pair(): pl.pallas_call(functools.partial(eliminate_kernel, rows, planes), out_sha...  5.49 us
    ppermute x1, starting transfers between devices, on_device_pair(): near_halo = lax.ppermute(near, 'span', swap_pairs(n_span, 0))  3.09 us
    ppermute x1, starting transfers between devices, on_device_pair(): far_halo = lax.ppermute(far, 'span', swap_pairs(n_span, 1))  2.47 us
    pallas_call x1, Pallas kernels, on_device_pair(): pl.pallas_call(functools.partial(pack_kernel, rows, planes), out_shape=(s...  2.36 us
    pallas_call x1, Pallas kernels, on_device_pair(): pl.pallas_call(functools.partial(substitute_kernel, rows, planes), out_sh...  2.19 us
    ppermute x1, starting transfers between devices, on_device_pair(): tip_m = lax.ppermute(tip, 'wall', [(0, 1), (1, 0)])  1.55 us
  transfers between devices with their start and end apart: 5, of which 1 were waited for; matrix products, arithmetic and copies ran while one was open for 0% of the time, Pallas kernels for 22%

profile of v1, /device:TPU:0, one launch (start us, length us, event | category | flops | bytes accessed | tf_op | source)
XLA Modules:
  0.0 31.5 jit_solution(15711740164795306865)
XLA Ops:
  0.0 0.1 pad_add_fusion.where_ref
  0.1 2.4 %shard_map.46 = (f32[512,128]{1,0:T(8,128)S(1)}, f32[3,512,128]{2,1,0:T(8,128)S(1)}, f32[512,128]{1,0:T(8,128)S(1)}, f32[512,128]{1,0:T(8,128)S(1)}, f32[5,32,12...) custom-call(s32[3]{0:T(128)S(1)} %pad_add_fusion.where_ref, f32[512,128]{1,0:T(8,128)} %bitcast.9, ...), custom_call_target="tpu_custom_call" | custom-call | tf_op jit(solution)/shard_map/pallas_call | solution.py:409
  2.4 3.1 %collective-permute-start = (f32[5,32,128]{2,1,0:T(8,128)S(1)}, f32[5,32,128]{2,1,0:T(8,128)S(1)}, u32[]{:S(2)}, u32[]{:S(2)}) collective-permute-start(f32[5,32,128]{2,1,0:T(8,128)S(1)} %get-tuple-element.25.near_ref), channel_id=1, source_target_pairs={{0,1},{1,0},{2,3},{3,2},{4,5},{5,4},{6,7},{7,6},{8,9},{9,8},{10,11... | collective-permute-start | bytes 245768 | tf_op jit(solution)/shard_map/ppermute | solution.py:422
  5.5 2.5 %collective-permute-start.1 = (f32[5,32,128]{2,1,0:T(8,128)S(1)}, f32[5,32,128]{2,1,0:T(8,128)S(1)}, u32[]{:S(2)}, u32[]{:S(2)}) collective-permute-start(f32[5,32,128]{2,1,0:T(8,128)S(1)} %get-tuple-element.26.far_ref), channel_id=1, source_target_pairs={{1,2},{2,1},{3,0},{0,3},{5,6},{6,5},{7,4},{4,7},{9,10},{10,9},{11,... | collective-permute-start | bytes 245768 | tf_op jit(solution)/shard_map/ppermute | solution.py:421
  8.0 0.4 %collective-permute-start.3 = (f32[5,8,128]{2,1,0:T(8,128)S(1)}, f32[5,8,128]{2,1,0:T(8,128)S(1)}, u32[]{:S(2)}, u32[]{:S(2)}) collective-permute-start(f32[5,8,128]{2,1,0:T(8,128)S(1)} %get-tuple-element.27.cols_ref), channel_id=1, source_target_pairs={{4,8},{8,4},{12,0},{0,12},{5,9},{9,5},{13,1},{1,13},{6,10},{10,6},... | collective-permute-start | bytes 61448 | tf_op jit(solution)/shard_map/ppermute | solution.py:423
  8.4 1.2 %collective-permute-start.2 = (f32[5,8,128]{2,1,0:T(8,128)S(1)}, f32[5,8,128]{2,1,0:T(8,128)S(1)}, u32[]{:S(2)}, u32[]{:S(2)}) collective-permute-start(f32[5,8,128]{2,1,0:T(8,128)S(1)} %get-tuple-element.27.cols_ref), channel_id=1, source_target_pairs={{0,4},{4,0},{8,12},{12,8},{1,5},{5,1},{9,13},{13,9},{2,6},{6,2},{1... | collective-permute-start | bytes 61448 | tf_op jit(solution)/shard_map/ppermute | solution.py:424
  9.6 7.0 %shard_map.47 = (f32[11,512,128]{2,1,0:T(8,128)S(1)}, f32[512,128]{1,0:T(8,128)S(1)}, f32[2,3,512,128]{3,2,1,0:T(8,128)S(1)}) custom-call(s32[3]{0:T(128)S(1)} %pad_add_fusion.where_ref, f32[512,128]{1,0:T(8,128)S(1)} %get-tuple-element.18.phi_ref, f32[3,512,128]{2,1,0:T(8,128)S(1)} %get-tuple-element.19.conc_ref, f32[512,128]{1,0:T(8,128)S(1)} %get-tuple-element.20.eps_ref, ...), custom_call_target="tpu_custom_call" | custom-call | flops 12000000 | bytes 6000000 | tf_op jit(solution)/shard_map/pallas_call | solution.py:426
  16.7 0.0 collective-permute-done.3.odd_halo_ref
  16.7 0.0 collective-permute-done.2.even_halo_ref
  16.7 0.0 collective-permute-done.near_halo_ref
  16.7 0.0 collective-permute-done.1.far_halo_ref
  16.7 5.5 %shard_map.48 = (f32[16,512,128]{2,1,0:T(8,128)S(1)}, f32[4,512,128]{2,1,0:T(8,128)S(1)}, f32[25,16,128]{2,1,0:T(8,128)S(1)}) custom-call(s32[3]{0:T(128)S(1)} %pad_add_fusion.where_ref, f32[512,128]{1,0:T(8,128)S(1)} %get-tuple-element.18.phi_ref, f32[3,512,128]{2,1,0:T(8,128)S(1)} %get-tuple-element.19.conc_ref, f32[512,128]{1,0:T(8,128)S(1)} %get-tuple-element.20.eps_ref, ...), custom_call_target="tpu_custom_call" | custom-call | tf_op jit(solution)/shard_map/pallas_call | solution.py:436
  22.2 1.6 %collective-permute-start.4 = (f32[25,16,128]{2,1,0:T(8,128)S(1)}, f32[25,16,128]{2,1,0:T(8,128)S(1)}, u32[]{:S(2)}, u32[]{:S(2)}) collective-permute-start(f32[25,16,128]{2,1,0:T(8,128)S(1)} %get-tuple-element.28.own_ref), channel_id=1, source_target_pairs={{0,16},{16,0},{1,17},{17,1},{2,18},{18,2},{3,19},{19,3},{4,20},{20... | collective-permute-start | bytes 614408 | tf_op jit(solution)/shard_map/ppermute | solution.py:453
  23.8 5.5 %collective-permute-done.4.near_ref = f32[25,16,128]{2,1,0:T(8,128)S(1)} collective-permute-done((f32[25,16,128]{2,1,0:T(8,128)S(1)}, f32[25,16,128]{2,1,0:T(8,128)S(1)}, u32[]{:S(2)}, u32[]{:S(2)}) %collective-permute-start.4) | collective-permute-done | bytes 204832 | tf_op jit(solution)/shard_map/ppermute | solution.py:453
  29.3 2.2 %shard_map.49 = f32[4,512,128]{2,1,0:T(8,128)} custom-call(s32[3]{0:T(128)S(1)} %pad_add_fusion.where_ref, f32[25,16,128]{2,1,0:T(8,128)S(1)} %get-tuple-element.28.own_ref, f32[25,16,128]{2,1,0:T(8,128)S(1)} %collective-permute-done.4.near_ref, f32[16,512,128]{2,1,0:T(8,128)S(1)} %get-tuple-element.29.t_ref, f32[4,512,128]{2,1,0:T(8,128)S(1)} %get-tuple-element.30.s_ref), custom_call_target="tpu_custom_call" | custom-call | tf_op jit(solution)/shard_map/pallas_call | solution.py:455
Async XLA Ops:
  2.4 14.3 %collective-permute-start = (f32[5,32,128]{2,1,0:T(8,128)S(1)}, f32[5,32,128]{2,1,0:T(8,128)S(1)}, u32[]{:S(2)}, u32[]{:S(2)}) collective-permute-start(f32[5,32,128]{2,1,0:T(8,128)S(1)} %get-tuple-element.25.near_ref), channel_id=1, source_target_pairs={{0,1},{1,0},{2,3},{3,2},{4,5},{5,4},{6,7},{7,6},{8,9},{9,8},{10,11... | collective-permute-start | bytes 245768 | tf_op jit(solution)/shard_map/ppermute | solution.py:422
  5.5 11.2 %collective-permute-start.1 = (f32[5,32,128]{2,1,0:T(8,128)S(1)}, f32[5,32,128]{2,1,0:T(8,128)S(1)}, u32[]{:S(2)}, u32[]{:S(2)}) collective-permute-start(f32[5,32,128]{2,1,0:T(8,128)S(1)} %get-tuple-element.26.far_ref), channel_id=1, source_target_pairs={{1,2},{2,1},{3,0},{0,3},{5,6},{6,5},{7,4},{4,7},{9,10},{10,9},{11,... | collective-permute-start | bytes 245768 | tf_op jit(solution)/shard_map/ppermute | solution.py:421
  8.0 8.7 %collective-permute-start.3 = (f32[5,8,128]{2,1,0:T(8,128)S(1)}, f32[5,8,128]{2,1,0:T(8,128)S(1)}, u32[]{:S(2)}, u32[]{:S(2)}) collective-permute-start(f32[5,8,128]{2,1,0:T(8,128)S(1)} %get-tuple-element.27.cols_ref), channel_id=1, source_target_pairs={{4,8},{8,4},{12,0},{0,12},{5,9},{9,5},{13,1},{1,13},{6,10},{10,6},... | collective-permute-start | bytes 61448 | tf_op jit(solution)/shard_map/ppermute | solution.py:423
  8.4 8.3 %collective-permute-start.2 = (f32[5,8,128]{2,1,0:T(8,128)S(1)}, f32[5,8,128]{2,1,0:T(8,128)S(1)}, u32[]{:S(2)}, u32[]{:S(2)}) collective-permute-start(f32[5,8,128]{2,1,0:T(8,128)S(1)} %get-tuple-element.27.cols_ref), channel_id=1, source_target_pairs={{0,4},{4,0},{8,12},{12,8},{1,5},{5,1},{9,13},{13,9},{2,6},{6,2},{1... | collective-permute-start | bytes 61448 | tf_op jit(solution)/shard_map/ppermute | solution.py:424
  22.2 7.1 %collective-permute-start.4 = (f32[25,16,128]{2,1,0:T(8,128)S(1)}, f32[25,16,128]{2,1,0:T(8,128)S(1)}, u32[]{:S(2)}, u32[]{:S(2)}) collective-permute-start(f32[25,16,128]{2,1,0:T(8,128)S(1)} %get-tuple-element.28.own_ref), channel_id=1, source_target_pairs={{0,16},{16,0},{1,17},{17,1},{2,18},{18,2},{3,19},{19,3},{4,20},{20... | collective-permute-start | bytes 614408 | tf_op jit(solution)/shard_map/ppermute | solution.py:453

commit v2 on v1

--- a/solution.py
+++ b/solution.py
@@ -14,6 +14,10 @@
 LANES = 128
 SUB = 8
 NQ = 11
+ASSEMBLE_GROUP = 4
+ELIMINATE_GROUP = 30
+SUBSTITUTE_GROUP = 31
+OUT_ROWS = 8
 
 VMEM = pl.BlockSpec(memory_space=pltpu.VMEM)
 SMEM = pl.BlockSpec(memory_space=pltpu.SMEM)
@@ -25,6 +29,21 @@
 
 def params(mib=8):
     return pltpu.CompilerParams(vmem_limit_bytes=mib * 1024 * 1024)
+
+
+def unrolled(start, stop, step, carry, group):
+    full = (stop - start) // group if stop - start > group else 0
+
+    def body(j, carry):
+        for u in range(group):
+            carry = step(start + group * j + u, carry)
+        return carry
+
+    if full:
+        carry = lax.fori_loop(0, full, body, carry)
+    for i in range(start + group * full, stop):
+        carry = step(i, carry)
+    return carry
 
 
 def face(phi, eps, conc, phi_m, eps_m, conc_m, weight):
@@ -104,35 +123,30 @@
     rows, planes, where_ref, phi_hbm, conc_hbm, eps_hbm, charge_hbm,
     phi_ref, conc_ref, eps_ref, charge_ref, near_ref, far_ref, cols_ref, sems,
 ):
-    copies = [
-        pltpu.make_async_copy(src, dst, sems.at[i])
-        for i, (src, dst) in enumerate(
-            (
-                (conc_hbm, conc_ref),
-                (phi_hbm, phi_ref),
-                (eps_hbm, eps_ref),
-                (charge_hbm, charge_ref),
-            )
-        )
+    fields = [
+        (phi_hbm, phi_ref),
+        *((conc_hbm.at[k], conc_ref.at[k]) for k in range(3)),
+        (eps_hbm, eps_ref),
+        (charge_hbm, charge_ref),
     ]
+    copies = [pltpu.make_async_copy(*pair, sems.at[i]) for i, pair in enumerate(fields)]
     for copy in copies:
         copy.start()
-    for copy in copies:
-        copy.wait()
     odd = where_ref[1] > 0
-    views = [phi_ref, conc_ref.at[0], conc_ref.at[1], conc_ref.at[2], eps_ref]
-    even_lane = lax.broadcasted_iota(jnp.int32, (SUB, LANES), 1)
-    for f, ref in enumerate(views):
+    pair_of_lane = lax.broadcasted_iota(jnp.int32, (SUB, LANES), 1) // 2
+    for f in range(5):
+        copies[f].wait()
+        ref = fields[f][1]
         low = ref[pl.ds(0, rows, stride=planes), :]
         high = ref[pl.ds(planes - 1, rows, stride=planes), :]
         near_ref[f] = jnp.where(odd, low, high)
         far_ref[f] = jnp.where(odd, high, low)
-    for f, ref in enumerate(views):
         packed = jnp.zeros((SUB, LANES), jnp.float32)
         for j in range(rows * planes // SUB):
             moved = pltpu.roll(ref[SUB * j : SUB * (j + 1), :], 2 * j + 1, 1)
-            packed = jnp.where((even_lane // 2) == j, moved, packed)
+            packed = jnp.where(pair_of_lane == j, moved, packed)
         cols_ref[f] = packed
+    copies[5].wait()
 
 
 def assemble_kernel(
@@ -161,7 +175,7 @@
                 carry = [e, -g, *into, *[-v for v in flux], *conc]
                 phi, eps, conc = phi_m, eps_m, conc_m
             for q in range(NQ):
-                span_ref[q, p * rows + row0 : p * rows + row0 + SUB, :] = total[q]
+                span_ref[q, p * (rows + 1) + row0 : p * (rows + 1) + row0 + SUB, :] = total[q]
 
     lane = lax.broadcasted_iota(jnp.int32, (planes, LANES), 1)
     weight = jnp.where(lane < LANES - 1, PLANE_WEIGHT, 0.0).astype(jnp.float32)
@@ -181,7 +195,7 @@
 
         conc_m = [fwd(c) for c in conc]
         e, g, out, into, flux = face(phi, eps, conc, fwd(phi), fwd(eps), conc_m, weight)
-        span = [span_ref[q, pl.ds(r, planes, stride=rows), :] for q in range(NQ)]
+        span = [span_ref[q, pl.ds(r, planes, stride=rows + 1), :] for q in range(NQ)]
         total_e = (e + back(e)) + (lower[0] + upper[0]) + span[0]
         total_g = (g - back(g)) + (lower[1] + upper[1]) + span[1]
         charge = charge_ref[at, :] + conc[0] - conc[1] + 2.0 * conc[2]
@@ -219,7 +233,7 @@
         lower = (e, -g, list(into), [-v for v in flux], both)
         return phi_m, eps_m, conc_m, lower
 
-    phi, eps, conc, lower = lax.fori_loop(0, rows - 1, step, (phi, eps, conc, lower))
+    phi, eps, conc, lower = unrolled(0, rows - 1, step, (phi, eps, conc, lower), ASSEMBLE_GROUP)
     e = last_wall * eps
     upper = (e, -e * phi, zeros, zeros, zeros)
     finish(rows - 1, phi, eps, conc, lower, upper)
@@ -231,12 +245,11 @@
     return [e, g, *out, *[-v for v in flux], *[(HALF_ZD[k] * PLANE_WEIGHT) * c[k] for k in range(3)]]
 
 
-def eliminate_kernel(
+def first_eliminate_kernel(
     rows, planes, where_ref, phi_ref, conc_ref, eps_ref, acc_ref, fe_ref, fu_ref,
     near_ref, far_ref, near_halo_ref, far_halo_ref, cols_ref, even_halo_ref, odd_halo_ref,
     t_ref, s_ref, tip_ref, side_ref, rim_ref,
 ):
-    wall = where_ref[0]
     span_odd = where_ref[1]
     stream_odd = where_ref[2] > 0
 
@@ -261,29 +274,48 @@
     for q, v in enumerate(halo_terms(own, near, wrapped)):
         side_ref[q] = v
 
-    lane = lax.broadcasted_iota(jnp.int32, (planes, LANES), 1)
+    last = pl.multiple_of(jnp.where(where_ref[0] == 0, rows - 1, 0) * planes, planes)
+    for part in range(planes // SUB):
+        at = pl.ds(last + SUB * part, SUB)
+        tip_ref[20 + 5 * part] = phi_ref[at, :]
+        for k in range(3):
+            tip_ref[21 + 5 * part + k] = conc_ref[k, at, :]
+        tip_ref[24 + 5 * part] = eps_ref[at, :]
+
+    eliminate_kernel(
+        rows, planes, 0, where_ref, conc_ref, acc_ref, fe_ref, fu_ref, side_ref, rim_ref,
+        t_ref, s_ref, tip_ref,
+    )
+
+
+def eliminate_kernel(
+    rows, planes, part, where_ref, conc_ref, acc_ref, fe_ref, fu_ref, side_ref, rim_ref,
+    t_ref, s_ref, tip_ref,
+):
+    wall = where_ref[0]
+    lane = lax.broadcasted_iota(jnp.int32, (SUB, LANES), 1)
     edge = (lane == 0) | (lane == LANES - 1)
-    plane = lax.broadcasted_iota(jnp.int32, (planes, LANES), 0)
-    low_plane, high_plane = plane == 0, plane == planes - 1
+    plane = lax.broadcasted_iota(jnp.int32, (SUB, LANES), 0) + SUB * part
+    rims = [side for side, p in enumerate((0, planes - 1)) if p // SUB == part]
+    on_rim = {side: plane == (planes - 1) * side for side in rims}
 
     def place(i):
         return jnp.where(wall == 0, i, rows - 1 - i)
 
+    def tile(r):
+        return pl.ds(pl.multiple_of(r * planes + SUB * part, SUB), SUB)
+
     def own_block(i):
         r = place(i)
-        at = pl.ds(pl.multiple_of(r * planes, planes), planes)
+        at = tile(r)
         q_all = []
         for q in range(NQ):
-            side = side_ref[q]
-            parts = [
-                pltpu.roll(side, LANES - 1 - 2 * ((planes // SUB) * r + part), 1)
-                for part in range(planes // SUB)
-            ]
-            moved = jnp.where(edge, jnp.concatenate(parts, 0), 0.0)
-            low = jnp.broadcast_to(rim_ref[q, 0, pl.ds(r, 1), :], (planes, LANES))
-            high = jnp.broadcast_to(rim_ref[q, 1, pl.ds(r, 1), :], (planes, LANES))
-            rim = jnp.where(low_plane, low, jnp.where(high_plane, high, 0.0))
-            q_all.append(acc_ref[q, at, :] + (moved + rim))
+            moved = pltpu.roll(side_ref[q], LANES - 1 - 2 * ((planes // SUB) * r + part), 1)
+            total = acc_ref[q, at, :] + jnp.where(edge, moved, 0.0)
+            for side in rims:
+                rim = jnp.broadcast_to(rim_ref[q, side, pl.ds(r, 1), :], (SUB, LANES))
+                total = total + jnp.where(on_rim[side], rim, 0.0)
+            q_all.append(total)
         a, d, b = q_all[0], q_all[2:5], q_all[8:11]
         one = jnp.ones_like(a)
         zero = jnp.zeros_like(a)
@@ -298,9 +330,7 @@
     def next_face(i):
         r = place(i)
         r_next = place(i + 1)
-        at = pl.ds(pl.multiple_of(r * planes, planes), planes)
-        at_next = pl.ds(pl.multiple_of(r_next * planes, planes), planes)
-        at_face = pl.ds(pl.multiple_of(jnp.minimum(r, r_next) * planes, planes), planes)
+        at, at_next, at_face = tile(r), tile(r_next), tile(jnp.minimum(r, r_next))
         m = [HALF_ZD[k] * (conc_ref[k, at, :] + conc_ref[k, at_next, :]) for k in range(3)]
         up = [fu_ref[0, k, at_face, :] for k in range(3)]
         low = [fu_ref[1, k, at_face, :] for k in range(3)]
@@ -317,29 +347,27 @@
         at, D, r = reduce_row(i, carry)
         e, m, up, low = next_face(i)
         T, s = solve_block(D, r, e, m, up)
+        keep = pl.ds(pl.multiple_of(place(i) * SUB, SUB), SUB)
         for a in range(4):
             for b in range(4):
-                t_ref[4 * a + b, at, :] = T[a][b]
-            s_ref[a, at, :] = s[a]
+                t_ref[4 * a + b, keep, :] = T[a][b]
+            s_ref[a, keep, :] = s[a]
         return T, s, e, m, low
 
     carry = step(0, None)
-    carry = lax.fori_loop(1, rows - 1, step, carry)
+    carry = unrolled(1, rows - 1, step, carry, ELIMINATE_GROUP)
     at, D, r = reduce_row(rows - 1, carry)
     for a in range(4):
         for b in range(4):
             tip_ref[4 * a + b] = D[a][b]
         tip_ref[16 + a] = r[a]
-    tip_ref[20] = phi_ref[at, :]
-    for k in range(3):
-        tip_ref[21 + k] = conc_ref[k, at, :]
-    tip_ref[24] = eps_ref[at, :]
-
-
-def tip_block(ref):
+
+
+def tip_block(ref, fields_ref, part):
     D = [[ref[4 * a + b] for b in range(4)] for a in range(4)]
     r = [ref[16 + a] for a in range(4)]
-    return D, r, ref[20], [ref[21 + k] for k in range(3)], ref[24]
+    f = [fields_ref[20 + 5 * part + q] for q in range(5)]
+    return D, r, f[0], f[1:4], f[4]
 
 
 def with_face(D, r, e, g, m, out, flux):
@@ -354,10 +382,13 @@
     return D, r
 
 
-def substitute_kernel(rows, planes, where_ref, own_ref, near_ref, t_ref, s_ref, out_ref):
+def substitute_kernel(
+    rows, part, where_ref, own_ref, near_ref, own_first_ref, near_first_ref, t_ref, s_ref, out_ref,
+    after=None,
+):
     wall = where_ref[0]
-    D, r, phi, conc, eps = tip_block(own_ref)
-    Dm, rm, phi_m, conc_m, eps_m = tip_block(near_ref)
+    D, r, phi, conc, eps = tip_block(own_ref, own_first_ref, part)
+    Dm, rm, phi_m, conc_m, eps_m = tip_block(near_ref, near_first_ref, part)
     e, g, out, into, flux = face(phi, eps, conc, phi_m, eps_m, conc_m, None)
     m = [HALF_ZD[k] * (conc[k] + conc_m[k]) for k in range(3)]
     Dm, rm = with_face(Dm, rm, e, -g, m, into, [-v for v in flux])
@@ -366,9 +397,11 @@
     D, r = couple(D, r, e, m, into, T, s)
     x = mat_vec(inverse4(D), r)
 
+    def tile(i):
+        return pl.ds(pl.multiple_of(jnp.where(wall == 0, i, rows - 1 - i) * SUB, SUB), SUB)
+
     def put(i, x):
-        row = jnp.where(wall == 0, i, rows - 1 - i)
-        at = pl.ds(pl.multiple_of(row * planes, planes), planes)
+        at = tile(i)
         for a in range(4):
             out_ref[a, at, :] = x[a]
 
@@ -376,14 +409,47 @@
 
     def step(j, x):
         i = rows - 2 - j
-        row = jnp.where(wall == 0, i, rows - 1 - i)
-        at = pl.ds(pl.multiple_of(row * planes, planes), planes)
+        at = tile(i)
         T = [[t_ref[4 * a + b, at, :] for b in range(4)] for a in range(4)]
         x = [v + s_ref[a, at, :] for a, v in enumerate(mat_vec(T, x))]
         put(i, x)
+        if after is not None and i % OUT_ROWS == 0:
+            after(i)
         return x
 
-    lax.fori_loop(0, rows - 1, step, x)
+    unrolled(0, rows - 1, step, x, rows - 1 if after is not None else SUBSTITUTE_GROUP)
+
+
+def last_substitute_kernel(
+    rows, planes, where_ref, own_ref, near_ref, own_first_ref, near_first_ref, t_ref, s_ref, *refs
+):
+    *done_refs, out_hbm, mine_ref, sems = refs
+    parts = planes // SUB
+    wall = where_ref[0]
+
+    def to_hbm(ref, part, chunk, n):
+        at = pl.ds(chunk, n)
+        return pltpu.make_async_copy(
+            ref.at[:, at], out_hbm.at[:, at, pl.ds(SUB * part, SUB), :], sems.at[len(copies)]
+        )
+
+    copies = []
+    for part, ref in enumerate(done_refs):
+        copies.append(to_hbm(ref, part, 0, rows))
+        copies[-1].start()
+    mine = mine_ref.reshape(4, rows, SUB, LANES)
+
+    def after(i):
+        first = jnp.where(wall == 0, i, rows - OUT_ROWS - i)
+        copies.append(to_hbm(mine, parts - 1, first, OUT_ROWS))
+        copies[-1].start()
+
+    substitute_kernel(
+        rows, parts - 1, where_ref, own_ref, near_ref, own_first_ref, near_first_ref, t_ref, s_ref,
+        mine_ref, after,
+    )
+    for copy in copies:
+        copy.wait()
 
 
 def swap_pairs(count, first):
@@ -408,13 +474,14 @@
 
     phi, conc, eps, charge, near, far, edge_cols = pl.pallas_call(
         functools.partial(pack_kernel, rows, planes),
+        name="pack",
         out_shape=(
             sds(cells, cols), sds(3, cells, cols), sds(cells, cols), sds(cells, cols),
             sds(5, rows, cols), sds(5, rows, cols), sds(5, SUB, LANES),
         ),
         in_specs=[SMEM] + [pl.BlockSpec(memory_space=pltpu.HBM)] * 4,
         out_specs=(VMEM,) * 7,
-        scratch_shapes=[pltpu.SemaphoreType.DMA((4,))],
+        scratch_shapes=[pltpu.SemaphoreType.DMA((6,))],
         compiler_params=params(),
     )(where, *(pltpu.with_memory_space_constraint(v, pltpu.HBM) for v in (phi, conc, eps, charge)))
 
@@ -425,41 +492,67 @@
 
     acc, fe, fu = pl.pallas_call(
         functools.partial(assemble_kernel, rows, planes),
+        name="assemble",
         out_shape=(sds(NQ, cells, cols), sds(cells, cols), sds(2, 3, cells, cols)),
         in_specs=[SMEM] + [VMEM] * 4,
         out_specs=(VMEM,) * 3,
-        scratch_shapes=[pltpu.VMEM((NQ, cells, cols), jnp.float32)],
+        scratch_shapes=[pltpu.VMEM((NQ, cells + planes, cols), jnp.float32)],
         compiler_params=params(),
         cost_estimate=pl.CostEstimate(flops=12_000_000, bytes_accessed=6_000_000, transcendentals=0),
     )(where, phi, conc, eps, charge)
 
-    T, s, tip = pl.pallas_call(
-        functools.partial(eliminate_kernel, rows, planes),
-        out_shape=(
-            sds(16, cells, cols), sds(4, cells, cols), sds(25, planes, cols)
-        ),
+    parts = planes // SUB
+    across = [(0, 1), (1, 0)]
+    kept = (sds(16, rows * SUB, cols), sds(4, rows * SUB, cols))
+    terms = (sds(NQ, SUB, LANES), sds(NQ, 2, rows, LANES))
+    T, s, tip, side, rim = pl.pallas_call(
+        functools.partial(first_eliminate_kernel, rows, planes),
+        name="eliminate",
+        out_shape=(*kept, sds(20 + 5 * parts, SUB, cols), *terms),
         in_specs=[SMEM] + [VMEM] * 13,
-        out_specs=(VMEM,) * 3,
-        scratch_shapes=[
-            pltpu.VMEM((NQ, SUB, LANES), jnp.float32),
-            pltpu.VMEM((NQ, 2, rows, LANES), jnp.float32),
-        ],
+        out_specs=(VMEM,) * 5,
         compiler_params=params(),
     )(
         where, phi, conc, eps, acc, fe, fu, near, far, near_halo, far_halo, edge_cols,
         even_halo, odd_halo,
     )
-
-    tip_m = lax.ppermute(tip, "wall", [(0, 1), (1, 0)])
-
-    update = pl.pallas_call(
-        functools.partial(substitute_kernel, rows, planes),
-        out_shape=sds(4, cells, cols),
-        in_specs=[SMEM] + [VMEM] * 4,
-        out_specs=VMEM,
+    solved = [(tip, lax.ppermute(tip, "wall", across), T, s)]
+    for part in range(1, parts):
+        T, s, tip = pl.pallas_call(
+            functools.partial(eliminate_kernel, rows, planes, part),
+            name="eliminate",
+            out_shape=(*kept, sds(20, SUB, cols)),
+            in_specs=[SMEM] + [VMEM] * 6,
+            out_specs=(VMEM,) * 3,
+            compiler_params=params(),
+        )(where, conc, acc, fe, fu, side, rim)
+        solved.append((tip, lax.ppermute(tip, "wall", across), T, s))
+
+    fields = solved[0][:2]
+    done = [
+        pl.pallas_call(
+            functools.partial(substitute_kernel, rows, part),
+            name="substitute",
+            out_shape=sds(4, rows * SUB, cols),
+            in_specs=[SMEM] + [VMEM] * 6,
+            out_specs=VMEM,
+            compiler_params=params(),
+        )(where, tip, tip_m, *fields, T, s)
+        for part, (tip, tip_m, T, s) in enumerate(solved[:-1])
+    ]
+    tip, tip_m, T, s = solved[-1]
+    return pl.pallas_call(
+        functools.partial(last_substitute_kernel, rows, planes),
+        name="substitute",
+        out_shape=sds(4, rows, planes, cols),
+        in_specs=[SMEM] + [VMEM] * (6 + len(done)),
+        out_specs=pl.BlockSpec(memory_space=pltpu.HBM),
+        scratch_shapes=[
+            pltpu.VMEM((4, rows * SUB, cols), jnp.float32),
+            pltpu.SemaphoreType.DMA((parts - 1 + rows // OUT_ROWS,)),
+        ],
         compiler_params=params(),
-    )(where, tip, tip_m, T, s)
-    return update.reshape(4, rows, planes, cols)
+    )(where, tip, tip_m, *fields, T, s, *(v.reshape(4, rows, SUB, cols) for v in done))
 
 
 def with_halo(block, sides, width, periodic):

time: 31.6 us -> 25.2 us (0.80)
  Pallas kernels: 17.1 us -> 12.6 us
  waiting for transfers between devices: 5.51 us -> 2.94 us
  starting transfers between devices: 8.75 us -> 9.36 us
    pallas_call x4 -> x6, Pallas kernels: 17.1 us -> 12.6 us  [the longest x1 3.42 us: on_device_pair(): pl.pallas_call(functools.partial(assemble_kernel, rows, planes), name='as...]
    ppermute x1 -> x2, waiting for transfers between devices: 5.5 us -> 2.93 us  [the longest x1 1.9 us: on_device_pair(): solved.append((tip, lax.ppermute(tip, 'wall', across), T, s))]
    ppermute x1, starting transfers between devices: 1.24 us -> 0.01 us  [on_device_pair(): even_halo = lax.ppermute(edge_cols, 'stream', swap_pairs(n_stream, 0))]
    ppermute x1, starting transfers between devices: 0.4 us -> 1.63 us  [on_device_pair(): odd_halo = lax.ppermute(edge_cols, 'stream', swap_pairs(n_stream, 1))]
    ppermute x1 -> x2, starting transfers between devices: 1.55 us -> 2.16 us  [the longest x1 1.55 us: on_device_pair(): solved = [(tip, lax.ppermute(tip, 'wall', across), T, s)]]
  transfers between devices with their start and end apart: 5 -> 6, of which waited for: 1 -> 2; matrix products, arithmetic and copies ran while one was open for 0% -> 0% of each run, Pallas kernels for 22% -> 26%
where the time goes in v2:
time: 25.2 us; the launch traced here: 25 us
  Pallas kernels  12.6 us (50%)
  starting transfers between devices  9.36 us (37%)
  waiting for transfers between devices  2.94 us (12%)
    pallas_call x1, Pallas kernels, on_device_pair(): pl.pallas_call(functools.partial(assemble_kernel, rows, planes), name='as...  3.42 us
    ppermute x1, starting transfers between devices, on_device_pair(): near_halo = lax.ppermute(near, 'span', swap_pairs(n_span, 0))  3.09 us
    ppermute x1, starting transfers between devices, on_device_pair(): far_halo = lax.ppermute(far, 'span', swap_pairs(n_span, 1))  2.47 us
    pallas_call x1, Pallas kernels, on_device_pair(): pl.pallas_call(functools.partial(pack_kernel, rows, planes), name='pack',...  2.27 us
    pallas_call x1, Pallas kernels, on_device_pair(): pl.pallas_call(functools.partial(first_eliminate_kernel, rows, planes), n...  2.2 us
    pallas_call x1, Pallas kernels, on_device_pair(): pl.pallas_call(functools.partial(eliminate_kernel, rows, planes, part), n...  2.09 us
    ppermute x1, waiting for transfers between devices, on_device_pair(): solved.append((tip, lax.ppermute(tip, 'wall', across), T, s))  1.9 us
    pallas_call x1, Pallas kernels, on_device_pair(): pl.pallas_call(functools.partial(last_substitute_kernel, rows, planes), n...  1.67 us
  transfers between devices with their start and end apart: 6, of which 2 were waited for; matrix products, arithmetic and copies ran while one was open for 0% of the time, Pallas kernels for 26%

profile of v2, /device:TPU:0, one launch (start us, length us, event | category | flops | bytes accessed | tf_op | source)
XLA Modules:
  0.0 25.0 jit_solution(4882662548879813662)
XLA Ops:
  0.0 0.1 pad_add_fusion.where_ref
  0.1 2.3 %pack.1 = (f32[512,128]{1,0:T(8,128)S(1)}, f32[3,512,128]{2,1,0:T(8,128)S(1)}, f32[512,128]{1,0:T(8,128)S(1)}, f32[512,128]{1,0:T(8,128)S(1)}, f32[5,32,128]{2,1...) custom-call(s32[3]{0:T(128)S(1)} %pad_add_fusion.where_ref, f32[512,128]{1,0:T(8,128)} %bitcast.10, ...), custom_call_target="tpu_custom_call" | custom-call | tf_op jit(solution)/shard_map/pack/pallas_call | solution.py:475
  2.3 3.1 %collective-permute-start = (f32[5,32,128]{2,1,0:T(8,128)S(1)}, f32[5,32,128]{2,1,0:T(8,128)S(1)}, u32[]{:S(2)}, u32[]{:S(2)}) collective-permute-start(f32[5,32,128]{2,1,0:T(8,128)S(1)} %get-tuple-element.30.near_ref), channel_id=1, source_target_pairs={{0,1},{1,0},{2,3},{3,2},{4,5},{5,4},{6,7},{7,6},{8,9},{9,8},{10,11... | collective-permute-start | bytes 245768 | tf_op jit(solution)/shard_map/ppermute | solution.py:489
  5.4 2.5 %collective-permute-start.1 = (f32[5,32,128]{2,1,0:T(8,128)S(1)}, f32[5,32,128]{2,1,0:T(8,128)S(1)}, u32[]{:S(2)}, u32[]{:S(2)}) collective-permute-start(f32[5,32,128]{2,1,0:T(8,128)S(1)} %get-tuple-element.31.far_ref), channel_id=1, source_target_pairs={{1,2},{2,1},{3,0},{0,3},{5,6},{6,5},{7,4},{4,7},{9,10},{10,9},{11,... | collective-permute-start | bytes 245768 | tf_op jit(solution)/shard_map/ppermute | solution.py:488
  7.9 0.0 collective-permute-start.2
  7.9 1.6 %collective-permute-start.3 = (f32[5,8,128]{2,1,0:T(8,128)S(1)}, f32[5,8,128]{2,1,0:T(8,128)S(1)}, u32[]{:S(2)}, u32[]{:S(2)}) collective-permute-start(f32[5,8,128]{2,1,0:T(8,128)S(1)} %get-tuple-element.32.cols_ref), channel_id=1, source_target_pairs={{4,8},{8,4},{12,0},{0,12},{5,9},{9,5},{13,1},{1,13},{6,10},{10,6},... | collective-permute-start | bytes 61448 | tf_op jit(solution)/shard_map/ppermute | solution.py:490
  9.5 3.4 %assemble.1 = (f32[11,512,128]{2,1,0:T(8,128)S(1)}, f32[512,128]{1,0:T(8,128)S(1)}, f32[2,3,512,128]{3,2,1,0:T(8,128)S(1)}) custom-call(s32[3]{0:T(128)S(1)} %pad_add_fusion.where_ref, f32[512,128]{1,0:T(8,128)S(1)} %get-tuple-element.24.phi_ref, f32[3,512,128]{2,1,0:T(8,128)S(1)} %get-tuple-element.23.conc_ref, f32[512,128]{1,0:T(8,128)S(1)} %get-tuple-element.25.eps_ref, ...), custom_call_target="tpu_custom_call" | custom-call | flops 12000000 | bytes 6000000 | tf_op jit(solution)/shard_map/assemble/pallas_call | solution.py:493
  13.0 0.0 collective-permute-done.2.even_halo_ref
  13.0 0.0 collective-permute-done.3.odd_halo_ref
  13.0 0.0 collective-permute-done.near_halo_ref
  13.0 0.0 collective-permute-done.1.far_halo_ref
  13.0 2.2 %eliminate.2 = (f32[16,256,128]{2,1,0:T(8,128)S(1)}, f32[4,256,128]{2,1,0:T(8,128)S(1)}, f32[30,8,128]{2,1,0:T(8,128)S(1)}, f32[11,8,128]{2,1,0:T(8,128)S(1)}, f32[11,2,32,128]{3,2,1,0:T(8,128)S(1)}) custom-call(s32[3]{0:T(128)S(1)} %pad_add_fusion.where_ref, f32[512,128]{1,0:T(8,128)S(1)} %get-tuple-element.24.phi_ref, ...), custom_call_target="tpu_custom_call" | custom-call | tf_op jit(solution)/shard_map/eliminate/pallas_call | solution.py:508
  15.2 1.6 %collective-permute-start.5 = (f32[30,8,128]{2,1,0:T(8,128)S(1)}, f32[30,8,128]{2,1,0:T(8,128)S(1)}, u32[]{:S(2)}, u32[]{:S(2)}) collective-permute-start(f32[30,8,128]{2,1,0:T(8,128)S(1)} %get-tuple-element.36.own_ref.own_first_ref), channel_id=1, source_target_pairs={{0,16},{16,0},{1,17},{17,1},{2,18},{18,2},{3,19},{19,3},{4,20},{20... | collective-permute-start | bytes 368648 | tf_op jit(solution)/shard_map/ppermute | solution.py:519
  16.8 2.1 %eliminate.3 = (f32[16,256,128]{2,1,0:T(8,128)S(1)}, f32[4,256,128]{2,1,0:T(8,128)S(1)}, f32[20,8,128]{2,1,0:T(8,128)S(1)}) custom-call(s32[3]{0:T(128)S(1)} %pad_add_fusion.where_ref, f32[3,512,128]{2,1,0:T(8,128)S(1)} %get-tuple-element.23.conc_ref, f32[11,512,128]{2,1,0:T(8,128)S(1)} %get-tuple-element.27.acc_ref, ...), custom_call_target="tpu_custom_call" | custom-call | tf_op jit(solution)/shard_map/eliminate/pallas_call | solution.py:521
  18.9 0.6 %collective-permute-start.4 = (f32[20,8,128]{2,1,0:T(8,128)S(1)}, f32[20,8,128]{2,1,0:T(8,128)S(1)}, u32[]{:S(2)}, u32[]{:S(2)}) collective-permute-start(f32[20,8,128]{2,1,0:T(8,128)S(1)} %get-tuple-element.35.own_ref), channel_id=1, source_target_pairs={{0,16},{16,0},{1,17},{17,1},{2,18},{18,2},{3,19},{19,3},{4,20},{20... | collective-permute-start | bytes 245768 | tf_op jit(solution)/shard_map/ppermute | solution.py:529
  19.5 1.0 %collective-permute-done.5.near_ref.near_first_ref = f32[30,8,128]{2,1,0:T(8,128)S(1)} collective-permute-done((f32[30,8,128]{2,1,0:T(8,128)S(1)}, f32[30,8,128]{2,1,0:T(8,128)S(1)}, u32[]{:S(2)}, u32[]{:S(2)}) %collective-permute-start.5) | collective-permute-done | bytes 122912 | tf_op jit(solution)/shard_map/ppermute | solution.py:519
  20.5 1.0 %substitute.2 = f32[4,256,128]{2,1,0:T(8,128)S(1)} custom-call(s32[3]{0:T(128)S(1)} %pad_add_fusion.where_ref, f32[30,8,128]{2,1,0:T(8,128)S(1)} %get-tuple-element.36.own_ref.own_first_ref, f32[30,8,128]{2,1,0:T(8,128)S(1)} %collective-permute-done.5.near_ref.near_first_ref, f32[30,8,128]{2,1,0:T(8,128)S(1)} %get-tuple-element.36.own_ref.own_first_ref, ...), custom_call_target="tpu_custom_call" | custom-call | tf_op jit(solution)/shard_map/substitute/pallas_call | solution.py:533
  21.5 1.9 %collective-permute-done.4.near_ref = f32[20,8,128]{2,1,0:T(8,128)S(1)} collective-permute-done((f32[20,8,128]{2,1,0:T(8,128)S(1)}, f32[20,8,128]{2,1,0:T(8,128)S(1)}, u32[]{:S(2)}, u32[]{:S(2)}) %collective-permute-start.4) | collective-permute-done | bytes 81952 | tf_op jit(solution)/shard_map/ppermute | solution.py:529
  23.4 1.7 %substitute.3 = f32[4,32,16,128]{3,2,1,0:T(8,128)} custom-call(s32[3]{0:T(128)S(1)} %pad_add_fusion.where_ref, f32[20,8,128]{2,1,0:T(8,128)S(1)} %get-tuple-element.35.own_ref, f32[20,8,128]{2,1,0:T(8,128)S(1)} %collective-permute-done.4.near_ref, f32[30,8,128]{2,1,0:T(8,128)S(1)} %get-tuple-element.36.own_ref.own_first_ref, ...), custom_call_target="tpu_custom_call" | custom-call | tf_op jit(solution)/shard_map/substitute/pallas_call | solution.py:544
Async XLA Ops:
  2.3 10.7 %collective-permute-start = (f32[5,32,128]{2,1,0:T(8,128)S(1)}, f32[5,32,128]{2,1,0:T(8,128)S(1)}, u32[]{:S(2)}, u32[]{:S(2)}) collective-permute-start(f32[5,32,128]{2,1,0:T(8,128)S(1)} %get-tuple-element.30.near_ref), channel_id=1, source_target_pairs={{0,1},{1,0},{2,3},{3,2},{4,5},{5,4},{6,7},{7,6},{8,9},{9,8},{10,11... | collective-permute-start | bytes 245768 | tf_op jit(solution)/shard_map/ppermute | solution.py:489
  5.4 7.6 %collective-permute-start.1 = (f32[5,32,128]{2,1,0:T(8,128)S(1)}, f32[5,32,128]{2,1,0:T(8,128)S(1)}, u32[]{:S(2)}, u32[]{:S(2)}) collective-permute-start(f32[5,32,128]{2,1,0:T(8,128)S(1)} %get-tuple-element.31.far_ref), channel_id=1, source_target_pairs={{1,2},{2,1},{3,0},{0,3},{5,6},{6,5},{7,4},{4,7},{9,10},{10,9},{11,... | collective-permute-start | bytes 245768 | tf_op jit(solution)/shard_map/ppermute | solution.py:488
  7.9 5.1 %collective-permute-start.2 = (f32[5,8,128]{2,1,0:T(8,128)S(1)}, f32[5,8,128]{2,1,0:T(8,128)S(1)}, u32[]{:S(2)}, u32[]{:S(2)}) collective-permute-start(f32[5,8,128]{2,1,0:T(8,128)S(1)} %get-tuple-element.32.cols_ref), channel_id=1, source_target_pairs={{0,4},{4,0},{8,12},{12,8},{1,5},{5,1},{9,13},{13,9},{2,6},{6,2},{1... | collective-permute-start | bytes 61448 | tf_op jit(solution)/shard_map/ppermute | solution.py:491
  7.9 5.1 %collective-permute-start.3 = (f32[5,8,128]{2,1,0:T(8,128)S(1)}, f32[5,8,128]{2,1,0:T(8,128)S(1)}, u32[]{:S(2)}, u32[]{:S(2)}) collective-permute-start(f32[5,8,128]{2,1,0:T(8,128)S(1)} %get-tuple-element.32.cols_ref), channel_id=1, source_target_pairs={{4,8},{8,4},{12,0},{0,12},{5,9},{9,5},{13,1},{1,13},{6,10},{10,6},... | collective-permute-start | bytes 61448 | tf_op jit(solution)/shard_map/ppermute | solution.py:490
  15.2 5.3 %collective-permute-start.5 = (f32[30,8,128]{2,1,0:T(8,128)S(1)}, f32[30,8,128]{2,1,0:T(8,128)S(1)}, u32[]{:S(2)}, u32[]{:S(2)}) collective-permute-start(f32[30,8,128]{2,1,0:T(8,128)S(1)} %get-tuple-element.36.own_ref.own_first_ref), channel_id=1, source_target_pairs={{0,16},{16,0},{1,17},{17,1},{2,18},{18,2},{3,19},{19,3},{4,20},{20... | collective-permute-start | bytes 368648 | tf_op jit(solution)/shard_map/ppermute | solution.py:519
  18.9 4.5 %collective-permute-start.4 = (f32[20,8,128]{2,1,0:T(8,128)S(1)}, f32[20,8,128]{2,1,0:T(8,128)S(1)}, u32[]{:S(2)}, u32[]{:S(2)}) collective-permute-start(f32[20,8,128]{2,1,0:T(8,128)S(1)} %get-tuple-element.35.own_ref), channel_id=1, source_target_pairs={{0,16},{16,0},{1,17},{17,1},{2,18},{18,2},{3,19},{19,3},{4,20},{20... | collective-permute-start | bytes 245768 | tf_op jit(solution)/shard_map/ppermute | solution.py:529

commit v3 on v2

--- a/solution.py
+++ b/solution.py
@@ -14,7 +14,7 @@
 LANES = 128
 SUB = 8
 NQ = 11
-ASSEMBLE_GROUP = 4
+ASSEMBLE_GROUP = 8
 ELIMINATE_GROUP = 30
 SUBSTITUTE_GROUP = 31
 OUT_ROWS = 8
@@ -139,8 +139,8 @@
         ref = fields[f][1]
         low = ref[pl.ds(0, rows, stride=planes), :]
         high = ref[pl.ds(planes - 1, rows, stride=planes), :]
-        near_ref[f] = jnp.where(odd, low, high)
-        far_ref[f] = jnp.where(odd, high, low)
+        near_ref[f] = jnp.where(odd, high, low)
+        far_ref[f] = jnp.where(odd, low, high)
         packed = jnp.zeros((SUB, LANES), jnp.float32)
         for j in range(rows * planes // SUB):
             moved = pltpu.roll(ref[SUB * j : SUB * (j + 1), :], 2 * j + 1, 1)
@@ -177,66 +177,73 @@
             for q in range(NQ):
                 span_ref[q, p * (rows + 1) + row0 : p * (rows + 1) + row0 + SUB, :] = total[q]
 
-    lane = lax.broadcasted_iota(jnp.int32, (planes, LANES), 1)
-    weight = jnp.where(lane < LANES - 1, PLANE_WEIGHT, 0.0).astype(jnp.float32)
-
-    def load(r):
-        at = pl.ds(pl.multiple_of(r * planes, planes), planes)
-        return phi_ref[at, :], eps_ref[at, :], [conc_ref[k, at, :] for k in range(3)]
-
-    def finish(r, phi, eps, conc, lower, upper):
-        at = pl.ds(pl.multiple_of(r * planes, planes), planes)
-
-        def fwd(v):
-            return pltpu.roll(v, LANES - 1, 1)
-
-        def back(v):
-            return pltpu.roll(v, 1, 1)
-
-        conc_m = [fwd(c) for c in conc]
-        e, g, out, into, flux = face(phi, eps, conc, fwd(phi), fwd(eps), conc_m, weight)
-        span = [span_ref[q, pl.ds(r, planes, stride=rows + 1), :] for q in range(NQ)]
-        total_e = (e + back(e)) + (lower[0] + upper[0]) + span[0]
-        total_g = (g - back(g)) + (lower[1] + upper[1]) + span[1]
-        charge = charge_ref[at, :] + conc[0] - conc[1] + 2.0 * conc[2]
-        acc_ref[0, at, :] = total_e
-        acc_ref[1, at, :] = total_g + charge
-        for k in range(3):
-            acc_ref[2 + k, at, :] = (out[k] + back(into[k])) + (lower[2][k] + upper[2][k]) + span[2 + k]
-            acc_ref[5 + k, at, :] = -(
-                (flux[k] - back(flux[k])) + (lower[3][k] + upper[3][k]) + span[5 + k]
-            )
-            near = conc_m[k] + back(conc[k]) + span[8 + k] + 4.0 * conc[k]
-            acc_ref[8 + k, at, :] = (HALF_ZD[k] * PLANE_WEIGHT) * near + HALF_ZD[k] * (
-                lower[4][k] + upper[4][k]
-            )
-
-    zero = jnp.zeros((planes, LANES), jnp.float32)
-    zeros = [zero] * 3
-
-    phi, eps, conc = load(0)
-    e = first_wall * eps
-    lower = (e, -e * phi, zeros, zeros, zeros)
-
-    def step(r, carry):
-        phi, eps, conc, lower = carry
-        phi_m, eps_m, conc_m = load(r + 1)
-        e, g, out, into, flux = face(phi, eps, conc, phi_m, eps_m, conc_m, None)
-        at = pl.ds(pl.multiple_of(r * planes, planes), planes)
-        fe_ref[at, :] = e
-        for k in range(3):
-            fu_ref[wall, k, at, :] = into[k]
-            fu_ref[1 - wall, k, at, :] = out[k]
-        both = [conc[k] + conc_m[k] for k in range(3)]
-        upper = (e, g, out, flux, both)
-        finish(r, phi, eps, conc, lower, upper)
-        lower = (e, -g, list(into), [-v for v in flux], both)
-        return phi_m, eps_m, conc_m, lower
-
-    phi, eps, conc, lower = unrolled(0, rows - 1, step, (phi, eps, conc, lower), ASSEMBLE_GROUP)
-    e = last_wall * eps
-    upper = (e, -e * phi, zeros, zeros, zeros)
-    finish(rows - 1, phi, eps, conc, lower, upper)
+    def row_pass(part):
+        lane = lax.broadcasted_iota(jnp.int32, (SUB, LANES), 1)
+        weight = jnp.where(lane < LANES - 1, PLANE_WEIGHT, 0.0).astype(jnp.float32)
+
+        def tile(r):
+            return pl.ds(pl.multiple_of(r * planes + SUB * part, SUB), SUB)
+
+        def load(r):
+            at = tile(r)
+            return phi_ref[at, :], eps_ref[at, :], [conc_ref[k, at, :] for k in range(3)]
+
+        def finish(r, phi, eps, conc, lower, upper):
+            at = tile(r)
+
+            def fwd(v):
+                return pltpu.roll(v, LANES - 1, 1)
+
+            def back(v):
+                return pltpu.roll(v, 1, 1)
+
+            conc_m = [fwd(c) for c in conc]
+            e, g, out, into, flux = face(phi, eps, conc, fwd(phi), fwd(eps), conc_m, weight)
+            span = [span_ref[q, pl.ds(r + (rows + 1) * SUB * part, SUB, stride=rows + 1), :] for q in range(NQ)]
+            total_e = (e + back(e)) + (lower[0] + upper[0]) + span[0]
+            total_g = (g - back(g)) + (lower[1] + upper[1]) + span[1]
+            charge = charge_ref[at, :] + conc[0] - conc[1] + 2.0 * conc[2]
+            acc_ref[0, at, :] = total_e
+            acc_ref[1, at, :] = total_g + charge
+            for k in range(3):
+                acc_ref[2 + k, at, :] = (out[k] + back(into[k])) + (lower[2][k] + upper[2][k]) + span[2 + k]
+                acc_ref[5 + k, at, :] = -(
+                    (flux[k] - back(flux[k])) + (lower[3][k] + upper[3][k]) + span[5 + k]
+                )
+                near = conc_m[k] + back(conc[k]) + span[8 + k] + 4.0 * conc[k]
+                acc_ref[8 + k, at, :] = (HALF_ZD[k] * PLANE_WEIGHT) * near + HALF_ZD[k] * (
+                    lower[4][k] + upper[4][k]
+                )
+
+        zero = jnp.zeros((SUB, LANES), jnp.float32)
+        zeros = [zero] * 3
+
+        phi, eps, conc = load(0)
+        e = first_wall * eps
+        lower = (e, -e * phi, zeros, zeros, zeros)
+
+        def step(r, carry):
+            phi, eps, conc, lower = carry
+            phi_m, eps_m, conc_m = load(r + 1)
+            e, g, out, into, flux = face(phi, eps, conc, phi_m, eps_m, conc_m, None)
+            at = tile(r)
+            fe_ref[at, :] = e
+            for k in range(3):
+                fu_ref[wall, k, at, :] = into[k]
+                fu_ref[1 - wall, k, at, :] = out[k]
+            both = [conc[k] + conc_m[k] for k in range(3)]
+            upper = (e, g, out, flux, both)
+            finish(r, phi, eps, conc, lower, upper)
+            lower = (e, -g, list(into), [-v for v in flux], both)
+            return phi_m, eps_m, conc_m, lower
+
+        phi, eps, conc, lower = unrolled(0, rows - 1, step, (phi, eps, conc, lower), ASSEMBLE_GROUP)
+        e = last_wall * eps
+        upper = (e, -e * phi, zeros, zeros, zeros)
+        finish(rows - 1, phi, eps, conc, lower, upper)
+
+    for part in range(planes // SUB):
+        row_pass(part)
 
 
 def halo_terms(own, near, wrapped):
@@ -254,8 +261,8 @@
     stream_odd = where_ref[2] > 0
 
     for own_ref, halo_ref, side in (
-        (near_ref, near_halo_ref, 1 - span_odd),
-        (far_ref, far_halo_ref, span_odd),
+        (near_ref, near_halo_ref, span_odd),
+        (far_ref, far_halo_ref, 1 - span_odd),
     ):
         own = [own_ref[f] for f in range(5)]
         near = [halo_ref[f] for f in range(5)]
@@ -485,8 +492,8 @@
         compiler_params=params(),
     )(where, *(pltpu.with_memory_space_constraint(v, pltpu.HBM) for v in (phi, conc, eps, charge)))
 
-    far_halo = lax.ppermute(far, "span", swap_pairs(n_span, 1))
-    near_halo = lax.ppermute(near, "span", swap_pairs(n_span, 0))
+    near_halo = lax.ppermute(near, "span", swap_pairs(n_span, 1))
+    far_halo = lax.ppermute(far, "span", swap_pairs(n_span, 0))
     odd_halo = lax.ppermute(edge_cols, "stream", swap_pairs(n_stream, 1))
     even_halo = lax.ppermute(edge_cols, "stream", swap_pairs(n_stream, 0))
 

time: 25.2 us -> 24.7 us (0.980)
  starting transfers between devices: 9.36 us -> 8.91 us
    ppermute x2, starting transfers between devices: 5.56 us -> 5.12 us  [the longest x1 5.11 us: on_device_pair(): near_halo = lax.ppermute(near, 'span', swap_pairs(n_span, 1))]
where the time goes in v3:
time: 24.7 us; the launch traced here: 24.5 us
  Pallas kernels  12.5 us (51%)
  starting transfers between devices  8.91 us (36%)
  waiting for transfers between devices  2.94 us (12%)
    ppermute x1, starting transfers between devices, on_device_pair(): near_halo = lax.ppermute(near, 'span', swap_pairs(n_span, 1))  5.11 us
    pallas_call x1, Pallas kernels, on_device_pair(): pl.pallas_call(functools.partial(assemble_kernel, rows, planes), name='as...  3.34 us
    pallas_call x1, Pallas kernels, on_device_pair(): pl.pallas_call(functools.partial(pack_kernel, rows, planes), name='pack',...  2.27 us
    pallas_call x1, Pallas kernels, on_device_pair(): pl.pallas_call(functools.partial(first_eliminate_kernel, rows, planes), n...  2.19 us
    pallas_call x1, Pallas kernels, on_device_pair(): pl.pallas_call(functools.partial(eliminate_kernel, rows, planes, part), n...  2.09 us
    ppermute x1, waiting for transfers between devices, on_device_pair(): solved.append((tip, lax.ppermute(tip, 'wall', across), T, s))  1.9 us
    pallas_call x1, Pallas kernels, on_device_pair(): pl.pallas_call(functools.partial(last_substitute_kernel, rows, planes), n...  1.67 us
    ppermute x1, starting transfers between devices, on_device_pair(): odd_halo = lax.ppermute(edge_cols, 'stream', swap_pairs(n_stream, 1))  1.63 us
  transfers between devices with their start and end apart: 6, of which 2 were waited for; matrix products, arithmetic and copies ran while one was open for 0% of the time, Pallas kernels for 26%

profile of v3, /device:TPU:0, one launch (start us, length us, event | category | flops | bytes accessed | tf_op | source)
XLA Modules:
  0.0 24.5 jit_solution(6858913362785026747)
XLA Ops:
  0.0 0.1 pad_add_fusion.where_ref
  0.1 2.3 %pack.1 = (f32[512,128]{1,0:T(8,128)S(1)}, f32[3,512,128]{2,1,0:T(8,128)S(1)}, f32[512,128]{1,0:T(8,128)S(1)}, f32[512,128]{1,0:T(8,128)S(1)}, f32[5,32,128]{2,1...) custom-call(s32[3]{0:T(128)S(1)} %pad_add_fusion.where_ref, f32[512,128]{1,0:T(8,128)} %bitcast.10, ...), custom_call_target="tpu_custom_call" | custom-call | tf_op jit(solution)/shard_map/pack/pallas_call | solution.py:482
  2.3 5.1 %collective-permute-start = (f32[5,32,128]{2,1,0:T(8,128)S(1)}, f32[5,32,128]{2,1,0:T(8,128)S(1)}, u32[]{:S(2)}, u32[]{:S(2)}) collective-permute-start(f32[5,32,128]{2,1,0:T(8,128)S(1)} %get-tuple-element.30.near_ref), channel_id=1, source_target_pairs={{1,2},{2,1},{3,0},{0,3},{5,6},{6,5},{7,4},{4,7},{9,10},{10,9},{11,... | collective-permute-start | bytes 245768 | tf_op jit(solution)/shard_map/ppermute | solution.py:495
  7.5 0.0 collective-permute-start.1
  7.5 0.0 collective-permute-start.2
  7.5 1.6 %collective-permute-start.3 = (f32[5,8,128]{2,1,0:T(8,128)S(1)}, f32[5,8,128]{2,1,0:T(8,128)S(1)}, u32[]{:S(2)}, u32[]{:S(2)}) collective-permute-start(f32[5,8,128]{2,1,0:T(8,128)S(1)} %get-tuple-element.32.cols_ref), channel_id=1, source_target_pairs={{4,8},{8,4},{12,0},{0,12},{5,9},{9,5},{13,1},{1,13},{6,10},{10,6},... | collective-permute-start | bytes 61448 | tf_op jit(solution)/shard_map/ppermute | solution.py:497
  9.1 3.3 %assemble.1 = (f32[11,512,128]{2,1,0:T(8,128)S(1)}, f32[512,128]{1,0:T(8,128)S(1)}, f32[2,3,512,128]{3,2,1,0:T(8,128)S(1)}) custom-call(s32[3]{0:T(128)S(1)} %pad_add_fusion.where_ref, f32[512,128]{1,0:T(8,128)S(1)} %get-tuple-element.24.phi_ref, f32[3,512,128]{2,1,0:T(8,128)S(1)} %get-tuple-element.23.conc_ref, f32[512,128]{1,0:T(8,128)S(1)} %get-tuple-element.25.eps_ref, ...), custom_call_target="tpu_custom_call" | custom-call | flops 12000000 | bytes 6000000 | tf_op jit(solution)/shard_map/assemble/pallas_call | solution.py:500
  12.4 0.0 collective-permute-done.2.even_halo_ref
  12.5 0.0 collective-permute-done.3.odd_halo_ref
  12.5 0.0 collective-permute-done.near_halo_ref
  12.5 0.0 collective-permute-done.1.far_halo_ref
  12.5 2.2 %eliminate.2 = (f32[16,256,128]{2,1,0:T(8,128)S(1)}, f32[4,256,128]{2,1,0:T(8,128)S(1)}, f32[30,8,128]{2,1,0:T(8,128)S(1)}, f32[11,8,128]{2,1,0:T(8,128)S(1)}, f32[11,2,32,128]{3,2,1,0:T(8,128)S(1)}) custom-call(s32[3]{0:T(128)S(1)} %pad_add_fusion.where_ref, f32[512,128]{1,0:T(8,128)S(1)} %get-tuple-element.24.phi_ref, ...), custom_call_target="tpu_custom_call" | custom-call | tf_op jit(solution)/shard_map/eliminate/pallas_call | solution.py:515
  14.7 1.6 %collective-permute-start.5 = (f32[30,8,128]{2,1,0:T(8,128)S(1)}, f32[30,8,128]{2,1,0:T(8,128)S(1)}, u32[]{:S(2)}, u32[]{:S(2)}) collective-permute-start(f32[30,8,128]{2,1,0:T(8,128)S(1)} %get-tuple-element.36.own_ref.own_first_ref), channel_id=1, source_target_pairs={{0,16},{16,0},{1,17},{17,1},{2,18},{18,2},{3,19},{19,3},{4,20},{20... | collective-permute-start | bytes 368648 | tf_op jit(solution)/shard_map/ppermute | solution.py:526
  16.2 2.1 %eliminate.3 = (f32[16,256,128]{2,1,0:T(8,128)S(1)}, f32[4,256,128]{2,1,0:T(8,128)S(1)}, f32[20,8,128]{2,1,0:T(8,128)S(1)}) custom-call(s32[3]{0:T(128)S(1)} %pad_add_fusion.where_ref, f32[3,512,128]{2,1,0:T(8,128)S(1)} %get-tuple-element.23.conc_ref, f32[11,512,128]{2,1,0:T(8,128)S(1)} %get-tuple-element.27.acc_ref, ...), custom_call_target="tpu_custom_call" | custom-call | tf_op jit(solution)/shard_map/eliminate/pallas_call | solution.py:528
  18.3 0.6 %collective-permute-start.4 = (f32[20,8,128]{2,1,0:T(8,128)S(1)}, f32[20,8,128]{2,1,0:T(8,128)S(1)}, u32[]{:S(2)}, u32[]{:S(2)}) collective-permute-start(f32[20,8,128]{2,1,0:T(8,128)S(1)} %get-tuple-element.35.own_ref), channel_id=1, source_target_pairs={{0,16},{16,0},{1,17},{17,1},{2,18},{18,2},{3,19},{19,3},{4,20},{20... | collective-permute-start | bytes 245768 | tf_op jit(solution)/shard_map/ppermute | solution.py:536
  18.9 1.0 %collective-permute-done.5.near_ref.near_first_ref = f32[30,8,128]{2,1,0:T(8,128)S(1)} collective-permute-done((f32[30,8,128]{2,1,0:T(8,128)S(1)}, f32[30,8,128]{2,1,0:T(8,128)S(1)}, u32[]{:S(2)}, u32[]{:S(2)}) %collective-permute-start.5) | collective-permute-done | bytes 122912 | tf_op jit(solution)/shard_map/ppermute | solution.py:526
  20.0 1.0 %substitute.2 = f32[4,256,128]{2,1,0:T(8,128)S(1)} custom-call(s32[3]{0:T(128)S(1)} %pad_add_fusion.where_ref, f32[30,8,128]{2,1,0:T(8,128)S(1)} %get-tuple-element.36.own_ref.own_first_ref, f32[30,8,128]{2,1,0:T(8,128)S(1)} %collective-permute-done.5.near_ref.near_first_ref, f32[30,8,128]{2,1,0:T(8,128)S(1)} %get-tuple-element.36.own_ref.own_first_ref, ...), custom_call_target="tpu_custom_call" | custom-call | tf_op jit(solution)/shard_map/substitute/pallas_call | solution.py:540
  20.9 1.9 %collective-permute-done.4.near_ref = f32[20,8,128]{2,1,0:T(8,128)S(1)} collective-permute-done((f32[20,8,128]{2,1,0:T(8,128)S(1)}, f32[20,8,128]{2,1,0:T(8,128)S(1)}, u32[]{:S(2)}, u32[]{:S(2)}) %collective-permute-start.4) | collective-permute-done | bytes 81952 | tf_op jit(solution)/shard_map/ppermute | solution.py:536
  22.8 1.7 %substitute.3 = f32[4,32,16,128]{3,2,1,0:T(8,128)} custom-call(s32[3]{0:T(128)S(1)} %pad_add_fusion.where_ref, f32[20,8,128]{2,1,0:T(8,128)S(1)} %get-tuple-element.35.own_ref, f32[20,8,128]{2,1,0:T(8,128)S(1)} %collective-permute-done.4.near_ref, f32[30,8,128]{2,1,0:T(8,128)S(1)} %get-tuple-element.36.own_ref.own_first_ref, ...), custom_call_target="tpu_custom_call" | custom-call | tf_op jit(solution)/shard_map/substitute/pallas_call | solution.py:551
Async XLA Ops:
  2.3 10.1 %collective-permute-start = (f32[5,32,128]{2,1,0:T(8,128)S(1)}, f32[5,32,128]{2,1,0:T(8,128)S(1)}, u32[]{:S(2)}, u32[]{:S(2)}) collective-permute-start(f32[5,32,128]{2,1,0:T(8,128)S(1)} %get-tuple-element.30.near_ref), channel_id=1, source_target_pairs={{1,2},{2,1},{3,0},{0,3},{5,6},{6,5},{7,4},{4,7},{9,10},{10,9},{11,... | collective-permute-start | bytes 245768 | tf_op jit(solution)/shard_map/ppermute | solution.py:495
  7.5 5.0 %collective-permute-start.1 = (f32[5,32,128]{2,1,0:T(8,128)S(1)}, f32[5,32,128]{2,1,0:T(8,128)S(1)}, u32[]{:S(2)}, u32[]{:S(2)}) collective-permute-start(f32[5,32,128]{2,1,0:T(8,128)S(1)} %get-tuple-element.31.far_ref), channel_id=1, source_target_pairs={{0,1},{1,0},{2,3},{3,2},{4,5},{5,4},{6,7},{7,6},{8,9},{9,8},{10,11... | collective-permute-start | bytes 245768 | tf_op jit(solution)/shard_map/ppermute | solution.py:496
  7.5 5.0 %collective-permute-start.2 = (f32[5,8,128]{2,1,0:T(8,128)S(1)}, f32[5,8,128]{2,1,0:T(8,128)S(1)}, u32[]{:S(2)}, u32[]{:S(2)}) collective-permute-start(f32[5,8,128]{2,1,0:T(8,128)S(1)} %get-tuple-element.32.cols_ref), channel_id=1, source_target_pairs={{0,4},{4,0},{8,12},{12,8},{1,5},{5,1},{9,13},{13,9},{2,6},{6,2},{1... | collective-permute-start | bytes 61448 | tf_op jit(solution)/shard_map/ppermute | solution.py:498
  7.5 5.0 %collective-permute-start.3 = (f32[5,8,128]{2,1,0:T(8,128)S(1)}, f32[5,8,128]{2,1,0:T(8,128)S(1)}, u32[]{:S(2)}, u32[]{:S(2)}) collective-permute-start(f32[5,8,128]{2,1,0:T(8,128)S(1)} %get-tuple-element.32.cols_ref), channel_id=1, source_target_pairs={{4,8},{8,4},{12,0},{0,12},{5,9},{9,5},{13,1},{1,13},{6,10},{10,6},... | collective-permute-start | bytes 61448 | tf_op jit(solution)/shard_map/ppermute | solution.py:497
  14.7 5.3 %collective-permute-start.5 = (f32[30,8,128]{2,1,0:T(8,128)S(1)}, f32[30,8,128]{2,1,0:T(8,128)S(1)}, u32[]{:S(2)}, u32[]{:S(2)}) collective-permute-start(f32[30,8,128]{2,1,0:T(8,128)S(1)} %get-tuple-element.36.own_ref.own_first_ref), channel_id=1, source_target_pairs={{0,16},{16,0},{1,17},{17,1},{2,18},{18,2},{3,19},{19,3},{4,20},{20... | collective-permute-start | bytes 368648 | tf_op jit(solution)/shard_map/ppermute | solution.py:526
  18.3 4.5 %collective-permute-start.4 = (f32[20,8,128]{2,1,0:T(8,128)S(1)}, f32[20,8,128]{2,1,0:T(8,128)S(1)}, u32[]{:S(2)}, u32[]{:S(2)}) collective-permute-start(f32[20,8,128]{2,1,0:T(8,128)S(1)} %get-tuple-element.35.own_ref), channel_id=1, source_target_pairs={{0,16},{16,0},{1,17},{17,1},{2,18},{18,2},{3,19},{19,3},{4,20},{20... | collective-permute-start | bytes 245768 | tf_op jit(solution)/shard_map/ppermute | solution.py:536

commit v4 on v3

--- a/solution.py
+++ b/solution.py
@@ -15,12 +15,10 @@
 SUB = 8
 NQ = 11
 ASSEMBLE_GROUP = 8
-ELIMINATE_GROUP = 30
-SUBSTITUTE_GROUP = 31
 OUT_ROWS = 8
+COMPOSE_LAST = False
 
 VMEM = pl.BlockSpec(memory_space=pltpu.VMEM)
-SMEM = pl.BlockSpec(memory_space=pltpu.SMEM)
 
 
 def sds(*shape):
@@ -72,31 +70,71 @@
     return e, g, out, into, flux
 
 
+class Signed:
+    def __init__(self, value, sign=1):
+        self.value, self.sign = value, sign
+
+    def __neg__(self):
+        return Signed(self.value, -self.sign)
+
+    def __add__(self, other):
+        if self.value is None:
+            return other
+        if other.value is None:
+            return self
+        if self.sign == other.sign:
+            return Signed(self.value + other.value, self.sign)
+        if self.sign > 0:
+            return Signed(self.value - other.value)
+        return Signed(other.value - self.value)
+
+    def __sub__(self, other):
+        return self + (-other)
+
+    def __mul__(self, other):
+        if self.value is None or other.value is None:
+            return Signed(None)
+        return Signed(self.value * other.value, self.sign * other.sign)
+
+    def inverse(self):
+        return Signed(pl.reciprocal(self.value, approx=True), self.sign)
+
+    def array(self, like, sign=1):
+        if self.value is None:
+            return jnp.zeros_like(like)
+        return self.value if self.sign == sign else -self.value
+
+
+def signed(values):
+    return [Signed(v) for v in values]
+
+
+T_SIGN = ((1, 1, -1, -1), (1, 1, -1, -1), (1, -1, 1, -1), (1, -1, -1, 1))
+
+
 def inv2(a, b, c, d):
-    r = pl.reciprocal(a * d - b * c, approx=True)
-    return d * r, b * r, c * r, a * r
+    r = (a * d - b * c).inverse()
+    return ((d * r, -(b * r)), (-(c * r), a * r))
+
+
+def mul2(P, Q):
+    return [[P[i][0] * Q[0][j] + P[i][1] * Q[1][j] for j in range(2)] for i in range(2)]
 
 
 def inverse4(D):
-    a0, a1, a2, a3 = inv2(D[0][0], D[0][1], D[1][0], D[1][1])
-    A = ((a0, -a1), (-a2, a3))
-    E = [[D[2 + i][0] * A[0][j] + D[2 + i][1] * A[1][j] for j in range(2)] for i in range(2)]
-    S = [
-        [D[2 + i][2 + j] - (E[i][0] * D[0][2 + j] + E[i][1] * D[1][2 + j]) for j in range(2)]
-        for i in range(2)
-    ]
-    s0, s1, s2, s3 = inv2(S[0][0], S[0][1], S[1][0], S[1][1])
-    I = ((s0, -s1), (-s2, s3))
-    F = [[A[i][0] * D[0][2 + j] + A[i][1] * D[1][2 + j] for j in range(2)] for i in range(2)]
-    X = [[I[i][0] * E[0][j] + I[i][1] * E[1][j] for j in range(2)] for i in range(2)]
-    Y = [[F[i][0] * I[0][j] + F[i][1] * I[1][j] for j in range(2)] for i in range(2)]
-    Z = [[A[i][j] + (F[i][0] * X[0][j] + F[i][1] * X[1][j]) for j in range(2)] for i in range(2)]
-    return [
-        [Z[0][0], Z[0][1], -Y[0][0], -Y[0][1]],
-        [Z[1][0], Z[1][1], -Y[1][0], -Y[1][1]],
-        [-X[0][0], -X[0][1], I[0][0], I[0][1]],
-        [-X[1][0], -X[1][1], I[1][0], I[1][1]],
-    ]
+    two = range(2)
+    A = inv2(D[0][0], D[0][1], D[1][0], D[1][1])
+    B = [[D[i][2 + j] for j in two] for i in two]
+    E = mul2([[D[2 + i][j] for j in two] for i in two], A)
+    EB = mul2(E, B)
+    S = [[D[2 + i][2 + j] - EB[i][j] for j in two] for i in two]
+    I = inv2(S[0][0], S[0][1], S[1][0], S[1][1])
+    F = mul2(A, B)
+    X = mul2(I, E)
+    Y = mul2(F, I)
+    FX = mul2(F, X)
+    Z = [[A[i][j] + FX[i][j] for j in two] for i in two]
+    return [[*Z[i], *(-y for y in Y[i])] for i in two] + [[*(-x for x in X[i]), *I[i]] for i in two]
 
 
 def mat_vec(G, v):
@@ -120,7 +158,7 @@
 
 
 def pack_kernel(
-    rows, planes, where_ref, phi_hbm, conc_hbm, eps_hbm, charge_hbm,
+    rows, planes, phi_hbm, conc_hbm, eps_hbm, charge_hbm,
     phi_ref, conc_ref, eps_ref, charge_ref, near_ref, far_ref, cols_ref, sems,
 ):
     fields = [
@@ -132,7 +170,7 @@
     copies = [pltpu.make_async_copy(*pair, sems.at[i]) for i, pair in enumerate(fields)]
     for copy in copies:
         copy.start()
-    odd = where_ref[1] > 0
+    odd = lax.axis_index("span") % 2 > 0
     pair_of_lane = lax.broadcasted_iota(jnp.int32, (SUB, LANES), 1) // 2
     for f in range(5):
         copies[f].wait()
@@ -150,10 +188,10 @@
 
 
 def assemble_kernel(
-    rows, planes, where_ref, phi_ref, conc_ref, eps_ref, charge_ref,
+    rows, planes, phi_ref, conc_ref, eps_ref, charge_ref,
     acc_ref, fe_ref, fu_ref, span_ref,
 ):
-    wall = where_ref[0]
+    wall = lax.axis_index("wall")
     first_wall = (wall == 0).astype(jnp.float32)
     last_wall = 1.0 - first_wall
 
@@ -253,12 +291,12 @@
 
 
 def first_eliminate_kernel(
-    rows, planes, where_ref, phi_ref, conc_ref, eps_ref, acc_ref, fe_ref, fu_ref,
+    rows, planes, phi_ref, conc_ref, eps_ref, acc_ref, fe_ref, fu_ref,
     near_ref, far_ref, near_halo_ref, far_halo_ref, cols_ref, even_halo_ref, odd_halo_ref,
     t_ref, s_ref, tip_ref, side_ref, rim_ref,
 ):
-    span_odd = where_ref[1]
-    stream_odd = where_ref[2] > 0
+    span_odd = lax.axis_index("span") % 2
+    stream_odd = lax.axis_index("stream") % 2 > 0
 
     for own_ref, halo_ref, side in (
         (near_ref, near_halo_ref, span_odd),
@@ -281,7 +319,7 @@
     for q, v in enumerate(halo_terms(own, near, wrapped)):
         side_ref[q] = v
 
-    last = pl.multiple_of(jnp.where(where_ref[0] == 0, rows - 1, 0) * planes, planes)
+    last = pl.multiple_of(jnp.where(lax.axis_index("wall") == 0, rows - 1, 0) * planes, planes)
     for part in range(planes // SUB):
         at = pl.ds(last + SUB * part, SUB)
         tip_ref[20 + 5 * part] = phi_ref[at, :]
@@ -290,16 +328,16 @@
         tip_ref[24 + 5 * part] = eps_ref[at, :]
 
     eliminate_kernel(
-        rows, planes, 0, where_ref, conc_ref, acc_ref, fe_ref, fu_ref, side_ref, rim_ref,
+        rows, planes, 0, conc_ref, acc_ref, fe_ref, fu_ref, side_ref, rim_ref,
         t_ref, s_ref, tip_ref,
     )
 
 
 def eliminate_kernel(
-    rows, planes, part, where_ref, conc_ref, acc_ref, fe_ref, fu_ref, side_ref, rim_ref,
+    rows, planes, part, conc_ref, acc_ref, fe_ref, fu_ref, side_ref, rim_ref,
     t_ref, s_ref, tip_ref,
 ):
-    wall = where_ref[0]
+    wall = lax.axis_index("wall")
     lane = lax.broadcasted_iota(jnp.int32, (SUB, LANES), 1)
     edge = (lane == 0) | (lane == LANES - 1)
     plane = lax.broadcasted_iota(jnp.int32, (SUB, LANES), 0) + SUB * part
@@ -325,14 +363,15 @@
             q_all.append(total)
         a, d, b = q_all[0], q_all[2:5], q_all[8:11]
         one = jnp.ones_like(a)
-        zero = jnp.zeros_like(a)
+        zero = Signed(None)
+        b, d = signed(b), signed(d)
         D = [
-            [a, -one, one, -2.0 * one],
+            [Signed(a), Signed(one, -1), Signed(one), Signed(2.0 * one, -1)],
             [b[0], d[0], zero, zero],
             [b[1], zero, d[1], zero],
             [b[2], zero, zero, d[2]],
         ]
-        return at, D, [q_all[1], *q_all[5:8]]
+        return at, D, signed([q_all[1], *q_all[5:8]])
 
     def next_face(i):
         r = place(i)
@@ -341,7 +380,7 @@
         m = [HALF_ZD[k] * (conc_ref[k, at, :] + conc_ref[k, at_next, :]) for k in range(3)]
         up = [fu_ref[0, k, at_face, :] for k in range(3)]
         low = [fu_ref[1, k, at_face, :] for k in range(3)]
-        return fe_ref[at_face, :], m, up, low
+        return Signed(fe_ref[at_face, :]), signed(m), signed(up), signed(low)
 
     def reduce_row(i, carry):
         at, D, r = own_block(i)
@@ -354,25 +393,27 @@
         at, D, r = reduce_row(i, carry)
         e, m, up, low = next_face(i)
         T, s = solve_block(D, r, e, m, up)
+        like = e.value
         keep = pl.ds(pl.multiple_of(place(i) * SUB, SUB), SUB)
         for a in range(4):
             for b in range(4):
-                t_ref[4 * a + b, keep, :] = T[a][b]
-            s_ref[a, keep, :] = s[a]
+                t_ref[4 * a + b, keep, :] = T[a][b].array(like, T_SIGN[a][b])
+            s_ref[a, keep, :] = s[a].array(like)
         return T, s, e, m, low
 
     carry = step(0, None)
-    carry = unrolled(1, rows - 1, step, carry, ELIMINATE_GROUP)
+    for i in range(1, rows - 1):
+        carry = step(i, carry)
     at, D, r = reduce_row(rows - 1, carry)
     for a in range(4):
         for b in range(4):
-            tip_ref[4 * a + b] = D[a][b]
-        tip_ref[16 + a] = r[a]
+            tip_ref[4 * a + b] = D[a][b].array(fe_ref[at, :])
+        tip_ref[16 + a] = r[a].array(fe_ref[at, :])
 
 
 def tip_block(ref, fields_ref, part):
-    D = [[ref[4 * a + b] for b in range(4)] for a in range(4)]
-    r = [ref[16 + a] for a in range(4)]
+    D = [signed(ref[4 * a + b] for b in range(4)) for a in range(4)]
+    r = signed(ref[16 + a] for a in range(4))
     f = [fields_ref[20 + 5 * part + q] for q in range(5)]
     return D, r, f[0], f[1:4], f[4]
 
@@ -390,49 +431,78 @@
 
 
 def substitute_kernel(
-    rows, part, where_ref, own_ref, near_ref, own_first_ref, near_first_ref, t_ref, s_ref, out_ref,
-    after=None,
+    rows, part, own_ref, near_ref, own_first_ref, near_first_ref, t_ref, s_ref, out_ref,
+    after=None, composed=False,
 ):
-    wall = where_ref[0]
+    wall = lax.axis_index("wall")
     D, r, phi, conc, eps = tip_block(own_ref, own_first_ref, part)
     Dm, rm, phi_m, conc_m, eps_m = tip_block(near_ref, near_first_ref, part)
     e, g, out, into, flux = face(phi, eps, conc, phi_m, eps_m, conc_m, None)
-    m = [HALF_ZD[k] * (conc[k] + conc_m[k]) for k in range(3)]
+    e, g = Signed(e), Signed(g)
+    out, into, flux = signed(out), signed(into), signed(flux)
+    m = [Signed(HALF_ZD[k] * (conc[k] + conc_m[k])) for k in range(3)]
     Dm, rm = with_face(Dm, rm, e, -g, m, into, [-v for v in flux])
     T, s = solve_block(Dm, rm, e, m, out)
     D, r = with_face(D, r, e, g, m, out, flux)
     D, r = couple(D, r, e, m, into, T, s)
     x = mat_vec(inverse4(D), r)
 
-    def tile(i):
-        return pl.ds(pl.multiple_of(jnp.where(wall == 0, i, rows - 1 - i) * SUB, SUB), SUB)
-
     def put(i, x):
-        at = tile(i)
+        at = kept_tile(rows, wall, i)
         for a in range(4):
-            out_ref[a, at, :] = x[a]
+            out_ref[a, at, :] = x[a].array(phi)
 
     put(rows - 1, x)
-
-    def step(j, x):
-        i = rows - 2 - j
-        at = tile(i)
-        T = [[t_ref[4 * a + b, at, :] for b in range(4)] for a in range(4)]
-        x = [v + s_ref[a, at, :] for a, v in enumerate(mat_vec(T, x))]
+    if composed:
+        for i in range(rows - 2, -1, -1):
+            T, s = kept_block(t_ref, s_ref, kept_tile(rows, wall, i))
+            put(i, [v + w for v, w in zip(mat_vec(T, x), s)])
+            if after is not None and i % OUT_ROWS == 0:
+                after(i)
+        return
+
+    for i in range(rows - 2, -1, -1):
+        T, s = kept_block(t_ref, s_ref, kept_tile(rows, wall, i))
+        x = [v + w for v, w in zip(mat_vec(T, x), s)]
         put(i, x)
         if after is not None and i % OUT_ROWS == 0:
             after(i)
-        return x
-
-    unrolled(0, rows - 1, step, x, rows - 1 if after is not None else SUBSTITUTE_GROUP)
+
+
+def kept_tile(rows, wall, i):
+    return pl.ds(pl.multiple_of(jnp.where(wall == 0, i, rows - 1 - i) * SUB, SUB), SUB)
+
+
+def kept_block(t_ref, s_ref, at):
+    T = [[Signed(t_ref[4 * a + b, at, :], T_SIGN[a][b]) for b in range(4)] for a in range(4)]
+    return T, signed(s_ref[a, at, :] for a in range(4))
+
+
+def compose_kernel(rows, t_ref, s_ref, t_out_ref, s_out_ref):
+    wall = lax.axis_index("wall")
+    T, s = None, None
+    for i in range(rows - 2, -1, -1):
+        at = kept_tile(rows, wall, i)
+        T_row, s_row = kept_block(t_ref, s_ref, at)
+        if T is None:
+            T, s = T_row, s_row
+        else:
+            s = [v + w for v, w in zip(mat_vec(T_row, s), s_row)]
+            columns = [mat_vec(T_row, [T[a][b] for a in range(4)]) for b in range(4)]
+            T = [[columns[b][a] for b in range(4)] for a in range(4)]
+        for a in range(4):
+            like = t_ref[0, at, :]
+            for b in range(4):
+                t_out_ref[4 * a + b, at, :] = T[a][b].array(like, T_SIGN[a][b])
+            s_out_ref[a, at, :] = s[a].array(like)
 
 
 def last_substitute_kernel(
-    rows, planes, where_ref, own_ref, near_ref, own_first_ref, near_first_ref, t_ref, s_ref, *refs
+    rows, planes, own_ref, near_ref, own_first_ref, near_first_ref, t_ref, s_ref, *refs
 ):
     *done_refs, out_hbm, mine_ref, sems = refs
     parts = planes // SUB
-    wall = where_ref[0]
+    wall = lax.axis_index("wall")
 
     def to_hbm(ref, part, chunk, n):
         at = pl.ds(chunk, n)
@@ -452,8 +522,8 @@
         copies[-1].start()
 
     substitute_kernel(
-        rows, parts - 1, where_ref, own_ref, near_ref, own_first_ref, near_first_ref, t_ref, s_ref,
-        mine_ref, after,
+        rows, parts - 1, own_ref, near_ref, own_first_ref, near_first_ref, t_ref, s_ref,
+        mine_ref, after, COMPOSE_LAST,
     )
     for copy in copies:
         copy.wait()
@@ -475,9 +545,6 @@
     eps = permittivity.reshape(cells, cols)
     charge = fixed_charge.reshape(cells, cols)
     n_span, n_stream = lax.axis_size("span"), lax.axis_size("stream")
-    where = jnp.stack(
-        [lax.axis_index("wall"), lax.axis_index("span") % 2, lax.axis_index("stream") % 2]
-    ).astype(jnp.int32)
 
     phi, conc, eps, charge, near, far, edge_cols = pl.pallas_call(
         functools.partial(pack_kernel, rows, planes),
@@ -486,11 +553,11 @@
             sds(cells, cols), sds(3, cells, cols), sds(cells, cols), sds(cells, cols),
             sds(5, rows, cols), sds(5, rows, cols), sds(5, SUB, LANES),
         ),
-        in_specs=[SMEM] + [pl.BlockSpec(memory_space=pltpu.HBM)] * 4,
+        in_specs=[pl.BlockSpec(memory_space=pltpu.HBM)] * 4,
         out_specs=(VMEM,) * 7,
         scratch_shapes=[pltpu.SemaphoreType.DMA((6,))],
         compiler_params=params(),
-    )(where, *(pltpu.with_memory_space_constraint(v, pltpu.HBM) for v in (phi, conc, eps, charge)))
+    )(*(pltpu.with_memory_space_constraint(v, pltpu.HBM) for v in (phi, conc, eps, charge)))
 
     near_halo = lax.ppermute(near, "span", swap_pairs(n_span, 1))
     far_halo = lax.ppermute(far, "span", swap_pairs(n_span, 0))
@@ -501,12 +568,12 @@
         functools.partial(assemble_kernel, rows, planes),
         name="assemble",
         out_shape=(sds(NQ, cells, cols), sds(cells, cols), sds(2, 3, cells, cols)),
-        in_specs=[SMEM] + [VMEM] * 4,
+        in_specs=[VMEM] * 4,
         out_specs=(VMEM,) * 3,
         scratch_shapes=[pltpu.VMEM((NQ, cells + planes, cols), jnp.float32)],
         compiler_params=params(),
         cost_estimate=pl.CostEstimate(flops=12_000_000, bytes_accessed=6_000_000, transcendentals=0),
-    )(where, phi, conc, eps, charge)
+    )(phi, conc, eps, charge)
 
     parts = planes // SUB
     across = [(0, 1), (1, 0)]
@@ -516,11 +583,11 @@
         functools.partial(first_eliminate_kernel, rows, planes),
         name="eliminate",
         out_shape=(*kept, sds(20 + 5 * parts, SUB, cols), *terms),
-        in_specs=[SMEM] + [VMEM] * 13,
+        in_specs=[VMEM] * 13,
         out_specs=(VMEM,) * 5,
         compiler_params=params(),
     )(
-        where, phi, conc, eps, acc, fe, fu, near, far, near_halo, far_halo, edge_cols,
+        phi, conc, eps, acc, fe, fu, near, far, near_halo, far_halo, edge_cols,
         even_halo, odd_halo,
     )
     solved = [(tip, lax.ppermute(tip, "wall", across), T, s)]
@@ -529,10 +596,10 @@
             functools.partial(eliminate_kernel, rows, planes, part),
             name="eliminate",
             out_shape=(*kept, sds(20, SUB, cols)),
-            in_specs=[SMEM] + [VMEM] * 6,
+            in_specs=[VMEM] * 6,
             out_specs=(VMEM,) * 3,
             compiler_params=params(),
-        )(where, conc, acc, fe, fu, side, rim)
+        )(conc, acc, fe, fu, side, rim)
         solved.append((tip, lax.ppermute(tip, "wall", across), T, s))
 
     fields = solved[0][:2]
@@ -541,25 +608,34 @@
             functools.partial(substitute_kernel, rows, part),
             name="substitute",
             out_shape=sds(4, rows * SUB, cols),
-            in_specs=[SMEM] + [VMEM] * 6,
+            in_specs=[VMEM] * 6,
             out_specs=VMEM,
             compiler_params=params(),
-        )(where, tip, tip_m, *fields, T, s)
+        )(tip, tip_m, *fields, T, s)
         for part, (tip, tip_m, T, s) in enumerate(solved[:-1])
     ]
     tip, tip_m, T, s = solved[-1]
+    if COMPOSE_LAST:
+        T, s = pl.pallas_call(
+            functools.partial(compose_kernel, rows),
+            name="compose",
+            out_shape=kept,
+            in_specs=[VMEM] * 2,
+            out_specs=(VMEM,) * 2,
+            compiler_params=params(),
+        )(T, s)
     return pl.pallas_call(
         functools.partial(last_substitute_kernel, rows, planes),
         name="substitute",
         out_shape=sds(4, rows, planes, cols),
-        in_specs=[SMEM] + [VMEM] * (6 + len(done)),
+        in_specs=[VMEM] * (6 + len(done)),
         out_specs=pl.BlockSpec(memory_space=pltpu.HBM),
         scratch_shapes=[
             pltpu.VMEM((4, rows * SUB, cols), jnp.float32),
             pltpu.SemaphoreType.DMA((parts - 1 + rows // OUT_ROWS,)),
         ],
         compiler_params=params(),
-    )(where, tip, tip_m, *fields, T, s, *(v.reshape(4, rows, SUB, cols) for v in done))
+    )(tip, tip_m, *fields, T, s, *(v.reshape(4, rows, SUB, cols) for v in done))
 
 
 def with_halo(block, sides, width, periodic):

time: 24.7 us -> 21.9 us (0.89)
  Pallas kernels: 12.5 us -> 9.21 us
  waiting for transfers between devices: 2.94 us -> 3.62 us
    pallas_call x1, Pallas kernels: 2.19 us -> 1.62 us  [on_device_pair(): pl.pallas_call(functools.partial(first_eliminate_kernel, rows, planes), n...]
    ppermute x1, waiting for transfers between devices: 1.03 us -> 1.6 us  [on_device_pair(): solved = [(tip, lax.ppermute(tip, 'wall', across), T, s)]]
    pallas_call x1, Pallas kernels: 2.09 us -> 1.53 us  [on_device_pair(): pl.pallas_call(functools.partial(eliminate_kernel, rows, planes, part), n...]
    pallas_call x1, Pallas kernels: 3.34 us -> 2.79 us  [on_device_pair(): pl.pallas_call(functools.partial(assemble_kernel, rows, planes), name='as...]
    pallas_call x1, Pallas kernels: 0.96 us -> 0.41 us  [on_device_pair(): pl.pallas_call(functools.partial(substitute_kernel, rows, part), name='su...]
    pallas_call x1, Pallas kernels: 1.67 us -> 1.12 us  [on_device_pair(): pl.pallas_call(functools.partial(last_substitute_kernel, rows, planes), n...]
    pallas_call x1, Pallas kernels: 2.27 us -> 1.73 us  [on_device_pair(): pl.pallas_call(functools.partial(pack_kernel, rows, planes), name='pack',...]
  transfers between devices with their start and end apart: 6 -> 6, of which waited for: 2 -> 2; matrix products, arithmetic and copies ran while one was open for 0% -> 0% of each run, Pallas kernels for 26% -> 22%
where the time goes in v4:
time: 21.9 us; the launch traced here: 21.8 us
  Pallas kernels  9.21 us (42%)
  starting transfers between devices  8.9 us (41%)
  waiting for transfers between devices  3.62 us (17%)
    ppermute x1, starting transfers between devices, on_device_pair(): near_halo = lax.ppermute(near, 'span', swap_pairs(n_span, 1))  5.11 us
    pallas_call x1, Pallas kernels, on_device_pair(): pl.pallas_call(functools.partial(assemble_kernel, rows, planes), name='as...  2.79 us
    ppermute x1, waiting for transfers between devices, on_device_pair(): solved.append((tip, lax.ppermute(tip, 'wall', across), T, s))  2.01 us
    pallas_call x1, Pallas kernels, on_device_pair(): pl.pallas_call(functools.partial(pack_kernel, rows, planes), name='pack',...  1.73 us
    ppermute x1, starting transfers between devices, on_device_pair(): solved = [(tip, lax.ppermute(tip, 'wall', across), T, s)]  1.67 us
    ppermute x1, starting transfers between devices, on_device_pair(): odd_halo = lax.ppermute(edge_cols, 'stream', swap_pairs(n_stream, 1))  1.63 us
    pallas_call x1, Pallas kernels, on_device_pair(): pl.pallas_call(functools.partial(first_eliminate_kernel, rows, planes), n...  1.62 us
    ppermute x1, waiting for transfers between devices, on_device_pair(): solved = [(tip, lax.ppermute(tip, 'wall', across), T, s)]  1.6 us
  transfers between devices with their start and end apart: 6, of which 2 were waited for; matrix products, arithmetic and copies ran while one was open for 0% of the time, Pallas kernels for 22%

profile of v4, /device:TPU:0, one launch (start us, length us, event | category | flops | bytes accessed | tf_op | source)
XLA Modules:
  0.0 21.8 jit_solution(3413658698297121869)
XLA Ops:
  0.0 1.7 %pack.1 = (f32[512,128]{1,0:T(8,128)S(1)}, f32[3,512,128]{2,1,0:T(8,128)S(1)}, f32[512,128]{1,0:T(8,128)S(1)}, f32[512,128]{1,0:T(8,128)S(1)}, f32[5,32,128]{2,1...) custom-call(f32[512,128]{1,0:T(8,128)} %bitcast.7, f32[3,512,128]{2,1,0:T(8,128)} %bitcast.6, ...), custom_call_target="tpu_custom_call" | custom-call | tf_op jit(solution)/shard_map/pack/pallas_call | solution.py:549
  1.7 5.1 %collective-permute-start = (f32[5,32,128]{2,1,0:T(8,128)S(1)}, f32[5,32,128]{2,1,0:T(8,128)S(1)}, u32[]{:S(2)}, u32[]{:S(2)}) collective-permute-start(f32[5,32,128]{2,1,0:T(8,128)S(1)} %get-tuple-element.30.near_ref), channel_id=1, source_target_pairs={{1,2},{2,1},{3,0},{0,3},{5,6},{6,5},{7,4},{4,7},{9,10},{10,9},{11,... | collective-permute-start | bytes 245768 | tf_op jit(solution)/shard_map/ppermute | solution.py:562
  6.8 0.0 collective-permute-start.1
  6.9 0.0 collective-permute-start.2
  6.9 1.6 %collective-permute-start.3 = (f32[5,8,128]{2,1,0:T(8,128)S(1)}, f32[5,8,128]{2,1,0:T(8,128)S(1)}, u32[]{:S(2)}, u32[]{:S(2)}) collective-permute-start(f32[5,8,128]{2,1,0:T(8,128)S(1)} %get-tuple-element.32.cols_ref), channel_id=1, source_target_pairs={{4,8},{8,4},{12,0},{0,12},{5,9},{9,5},{13,1},{1,13},{6,10},{10,6},... | collective-permute-start | bytes 61448 | tf_op jit(solution)/shard_map/ppermute | solution.py:564
  8.5 2.8 %assemble.1 = (f32[11,512,128]{2,1,0:T(8,128)S(1)}, f32[512,128]{1,0:T(8,128)S(1)}, f32[2,3,512,128]{3,2,1,0:T(8,128)S(1)}) custom-call(f32[512,128]{1,0:T(8,128)S(1)} %get-tuple-element.24.phi_ref, f32[3,512,128]{2,1,0:T(8,128)S(1)} %get-tuple-element.23.conc_ref, f32[512,128]{1,0:T(8,128)S(1)} %get-tuple-element.25.eps_ref, ...), custom_call_target="tpu_custom_call" | custom-call | flops 12000000 | bytes 6000000 | tf_op jit(solution)/shard_map/assemble/pallas_call | solution.py:567
  11.3 0.0 collective-permute-done.2.even_halo_ref
  11.3 0.0 collective-permute-done.3.odd_halo_ref
  11.3 0.0 collective-permute-done.near_halo_ref
  11.3 0.0 collective-permute-done.1.far_halo_ref
  11.3 1.6 %eliminate.2 = (f32[16,256,128]{2,1,0:T(8,128)S(1)}, f32[4,256,128]{2,1,0:T(8,128)S(1)}, f32[30,8,128]{2,1,0:T(8,128)S(1)}, f32[11,8,128]{2,1,0:T(8,128)S(1)}, f32[11,2,32,128]{3,2,1,0:T(8,128)S(1)}) custom-call(f32[512,128]{1,0:T(8,128)S(1)} %get-tuple-element.24.phi_ref, f32[3,512,128]{2,1,0:T(8,128)S(1)} %get-tuple-element.23.conc_ref, ...), custom_call_target="tpu_custom_call" | custom-call | tf_op jit(solution)/shard_map/eliminate/pallas_call | solution.py:582
  13.0 1.7 %collective-permute-start.5 = (f32[30,8,128]{2,1,0:T(8,128)S(1)}, f32[30,8,128]{2,1,0:T(8,128)S(1)}, u32[]{:S(2)}, u32[]{:S(2)}) collective-permute-start(f32[30,8,128]{2,1,0:T(8,128)S(1)} %get-tuple-element.36.own_ref.own_first_ref), channel_id=1, source_target_pairs={{0,16},{16,0},{1,17},{17,1},{2,18},{18,2},{3,19},{19,3},{4,20},{20... | collective-permute-start | bytes 368648 | tf_op jit(solution)/shard_map/ppermute | solution.py:593
  14.6 1.5 %eliminate.3 = (f32[16,256,128]{2,1,0:T(8,128)S(1)}, f32[4,256,128]{2,1,0:T(8,128)S(1)}, f32[20,8,128]{2,1,0:T(8,128)S(1)}) custom-call(f32[3,512,128]{2,1,0:T(8,128)S(1)} %get-tuple-element.23.conc_ref, f32[11,512,128]{2,1,0:T(8,128)S(1)} %get-tuple-element.27.acc_ref, f32[512,128]{1,0:T(8,128)S(1)} %get-tuple-element.28.fe_ref, ...), custom_call_target="tpu_custom_call" | custom-call | tf_op jit(solution)/shard_map/eliminate/pallas_call | solution.py:595
  16.2 0.5 %collective-permute-start.4 = (f32[20,8,128]{2,1,0:T(8,128)S(1)}, f32[20,8,128]{2,1,0:T(8,128)S(1)}, u32[]{:S(2)}, u32[]{:S(2)}) collective-permute-start(f32[20,8,128]{2,1,0:T(8,128)S(1)} %get-tuple-element.35.own_ref), channel_id=1, source_target_pairs={{0,16},{16,0},{1,17},{17,1},{2,18},{18,2},{3,19},{19,3},{4,20},{20... | collective-permute-start | bytes 245768 | tf_op jit(solution)/shard_map/ppermute | solution.py:603
  16.6 1.6 %collective-permute-done.5.near_ref.near_first_ref = f32[30,8,128]{2,1,0:T(8,128)S(1)} collective-permute-done((f32[30,8,128]{2,1,0:T(8,128)S(1)}, f32[30,8,128]{2,1,0:T(8,128)S(1)}, u32[]{:S(2)}, u32[]{:S(2)}) %collective-permute-start.5) | collective-permute-done | bytes 122912 | tf_op jit(solution)/shard_map/ppermute | solution.py:593
  18.2 0.4 %substitute.2 = f32[4,256,128]{2,1,0:T(8,128)S(1)} custom-call(f32[30,8,128]{2,1,0:T(8,128)S(1)} %get-tuple-element.36.own_ref.own_first_ref, f32[30,8,128]{2,1,0:T(8,128)S(1)} %collective-permute-done.5.near_ref.near_first_ref, f32[30,8,128]{2,1,0:T(8,128)S(1)} %get-tuple-element.36.own_ref.own_first_ref, ...), custom_call_target="tpu_custom_call" | custom-call | tf_op jit(solution)/shard_map/substitute/pallas_call | solution.py:607
  18.7 2.0 %collective-permute-done.4.near_ref = f32[20,8,128]{2,1,0:T(8,128)S(1)} collective-permute-done((f32[20,8,128]{2,1,0:T(8,128)S(1)}, f32[20,8,128]{2,1,0:T(8,128)S(1)}, u32[]{:S(2)}, u32[]{:S(2)}) %collective-permute-start.4) | collective-permute-done | bytes 81952 | tf_op jit(solution)/shard_map/ppermute | solution.py:603
  20.7 1.1 %substitute.3 = f32[4,32,16,128]{3,2,1,0:T(8,128)} custom-call(f32[20,8,128]{2,1,0:T(8,128)S(1)} %get-tuple-element.35.own_ref, f32[20,8,128]{2,1,0:T(8,128)S(1)} %collective-permute-done.4.near_ref, f32[30,8,128]{2,1,0:T(8,128)S(1)} %get-tuple-element.36.own_ref.own_first_ref, f32[30,8,128]{2,1,0:T(8,128)S(1)} %collective-permute-done.5.near_ref.near_first_ref, ...), custom_call_target="tpu_custom_call" | custom-call | tf_op jit(solution)/shard_map/substitute/pallas_call | solution.py:627
Async XLA Ops:
  1.7 9.6 %collective-permute-start = (f32[5,32,128]{2,1,0:T(8,128)S(1)}, f32[5,32,128]{2,1,0:T(8,128)S(1)}, u32[]{:S(2)}, u32[]{:S(2)}) collective-permute-start(f32[5,32,128]{2,1,0:T(8,128)S(1)} %get-tuple-element.30.near_ref), channel_id=1, source_target_pairs={{1,2},{2,1},{3,0},{0,3},{5,6},{6,5},{7,4},{4,7},{9,10},{10,9},{11,... | collective-permute-start | bytes 245768 | tf_op jit(solution)/shard_map/ppermute | solution.py:562
  6.8 4.5 %collective-permute-start.1 = (f32[5,32,128]{2,1,0:T(8,128)S(1)}, f32[5,32,128]{2,1,0:T(8,128)S(1)}, u32[]{:S(2)}, u32[]{:S(2)}) collective-permute-start(f32[5,32,128]{2,1,0:T(8,128)S(1)} %get-tuple-element.31.far_ref), channel_id=1, source_target_pairs={{0,1},{1,0},{2,3},{3,2},{4,5},{5,4},{6,7},{7,6},{8,9},{9,8},{10,11... | collective-permute-start | bytes 245768 | tf_op jit(solution)/shard_map/ppermute | solution.py:563
  6.9 4.4 %collective-permute-start.2 = (f32[5,8,128]{2,1,0:T(8,128)S(1)}, f32[5,8,128]{2,1,0:T(8,128)S(1)}, u32[]{:S(2)}, u32[]{:S(2)}) collective-permute-start(f32[5,8,128]{2,1,0:T(8,128)S(1)} %get-tuple-element.32.cols_ref), channel_id=1, source_target_pairs={{0,4},{4,0},{8,12},{12,8},{1,5},{5,1},{9,13},{13,9},{2,6},{6,2},{1... | collective-permute-start | bytes 61448 | tf_op jit(solution)/shard_map/ppermute | solution.py:565
  6.9 4.4 %collective-permute-start.3 = (f32[5,8,128]{2,1,0:T(8,128)S(1)}, f32[5,8,128]{2,1,0:T(8,128)S(1)}, u32[]{:S(2)}, u32[]{:S(2)}) collective-permute-start(f32[5,8,128]{2,1,0:T(8,128)S(1)} %get-tuple-element.32.cols_ref), channel_id=1, source_target_pairs={{4,8},{8,4},{12,0},{0,12},{5,9},{9,5},{13,1},{1,13},{6,10},{10,6},... | collective-permute-start | bytes 61448 | tf_op jit(solution)/shard_map/ppermute | solution.py:564
  13.0 5.3 %collective-permute-start.5 = (f32[30,8,128]{2,1,0:T(8,128)S(1)}, f32[30,8,128]{2,1,0:T(8,128)S(1)}, u32[]{:S(2)}, u32[]{:S(2)}) collective-permute-start(f32[30,8,128]{2,1,0:T(8,128)S(1)} %get-tuple-element.36.own_ref.own_first_ref), channel_id=1, source_target_pairs={{0,16},{16,0},{1,17},{17,1},{2,18},{18,2},{3,19},{19,3},{4,20},{20... | collective-permute-start | bytes 368648 | tf_op jit(solution)/shard_map/ppermute | solution.py:593
  16.2 4.5 %collective-permute-start.4 = (f32[20,8,128]{2,1,0:T(8,128)S(1)}, f32[20,8,128]{2,1,0:T(8,128)S(1)}, u32[]{:S(2)}, u32[]{:S(2)}) collective-permute-start(f32[20,8,128]{2,1,0:T(8,128)S(1)} %get-tuple-element.35.own_ref), channel_id=1, source_target_pairs={{0,16},{16,0},{1,17},{17,1},{2,18},{18,2},{3,19},{19,3},{4,20},{20... | collective-permute-start | bytes 245768 | tf_op jit(solution)/shard_map/ppermute | solution.py:603

commit v5 on v4

--- a/solution.py
+++ b/solution.py
@@ -16,7 +16,6 @@
 NQ = 11
 ASSEMBLE_GROUP = 8
 OUT_ROWS = 8
-COMPOSE_LAST = False
 
 VMEM = pl.BlockSpec(memory_space=pltpu.VMEM)
 
@@ -121,7 +120,7 @@
     return [[P[i][0] * Q[0][j] + P[i][1] * Q[1][j] for j in range(2)] for i in range(2)]
 
 
-def inverse4(D):
+def factor4(D):
     two = range(2)
     A = inv2(D[0][0], D[0][1], D[1][0], D[1][1])
     B = [[D[i][2 + j] for j in two] for i in two]
@@ -129,12 +128,18 @@
     EB = mul2(E, B)
     S = [[D[2 + i][2 + j] - EB[i][j] for j in two] for i in two]
     I = inv2(S[0][0], S[0][1], S[1][0], S[1][1])
-    F = mul2(A, B)
-    X = mul2(I, E)
-    Y = mul2(F, I)
-    FX = mul2(F, X)
-    Z = [[A[i][j] + FX[i][j] for j in two] for i in two]
-    return [[*Z[i], *(-y for y in Y[i])] for i in two] + [[*(-x for x in X[i]), *I[i]] for i in two]
+    return A, E, I, mul2(A, B)
+
+
+def apply4(factors, w):
+    A, E, I, F = factors
+    two = range(2)
+    t = [w[2 + i] - (E[i][0] * w[0] + E[i][1] * w[1]) for i in two]
+    low = [I[i][0] * t[0] + I[i][1] * t[1] for i in two]
+    high = [
+        (A[i][0] * w[0] + A[i][1] * w[1]) - (F[i][0] * low[0] + F[i][1] * low[1]) for i in two
+    ]
+    return high + low
 
 
 def mat_vec(G, v):
@@ -151,15 +156,18 @@
 
 
 def solve_block(D, r, e, m, f):
-    G = inverse4(D)
-    first = mat_vec(G, [e] + list(m))
-    T = [[first[i]] + [G[i][k + 1] * f[k] for k in range(3)] for i in range(4)]
-    return T, mat_vec(G, r)
+    factors = factor4(D)
+    columns = [apply4(factors, [e] + list(m))]
+    for k in range(3):
+        w = [Signed(None)] * 4
+        w[k + 1] = f[k]
+        columns.append(apply4(factors, w))
+    return [[columns[b][a] for b in range(4)] for a in range(4)], apply4(factors, r)
 
 
 def pack_kernel(
     rows, planes, phi_hbm, conc_hbm, eps_hbm, charge_hbm,
-    phi_ref, conc_ref, eps_ref, charge_ref, near_ref, far_ref, cols_ref, sems,
+    phi_ref, conc_ref, eps_ref, charge_ref, near_ref, far_ref, sems,
 ):
     fields = [
         (phi_hbm, phi_ref),
@@ -171,7 +179,6 @@
     for copy in copies:
         copy.start()
     odd = lax.axis_index("span") % 2 > 0
-    pair_of_lane = lax.broadcasted_iota(jnp.int32, (SUB, LANES), 1) // 2
     for f in range(5):
         copies[f].wait()
         ref = fields[f][1]
@@ -179,12 +186,17 @@
         high = ref[pl.ds(planes - 1, rows, stride=planes), :]
         near_ref[f] = jnp.where(odd, high, low)
         far_ref[f] = jnp.where(odd, low, high)
+    copies[5].wait()
+
+
+def columns_kernel(rows, planes, phi_ref, conc_ref, eps_ref, cols_ref):
+    pair_of_lane = lax.broadcasted_iota(jnp.int32, (SUB, LANES), 1) // 2
+    for f, ref in enumerate([phi_ref, *(conc_ref.at[k] for k in range(3)), eps_ref]):
         packed = jnp.zeros((SUB, LANES), jnp.float32)
         for j in range(rows * planes // SUB):
             moved = pltpu.roll(ref[SUB * j : SUB * (j + 1), :], 2 * j + 1, 1)
             packed = jnp.where(pair_of_lane == j, moved, packed)
         cols_ref[f] = packed
-    copies[5].wait()
 
 
 def assemble_kernel(
@@ -432,7 +444,7 @@
 
 def substitute_kernel(
     rows, part, own_ref, near_ref, own_first_ref, near_first_ref, t_ref, s_ref, out_ref,
-    after=None, composed=False,
+    after=None,
 ):
     wall = lax.axis_index("wall")
     D, r, phi, conc, eps = tip_block(own_ref, own_first_ref, part)
@@ -445,7 +457,7 @@
     T, s = solve_block(Dm, rm, e, m, out)
     D, r = with_face(D, r, e, g, m, out, flux)
     D, r = couple(D, r, e, m, into, T, s)
-    x = mat_vec(inverse4(D), r)
+    x = apply4(factor4(D), r)
 
     def put(i, x):
         at = kept_tile(rows, wall, i)
@@ -453,14 +465,6 @@
             out_ref[a, at, :] = x[a].array(phi)
 
     put(rows - 1, x)
-    if composed:
-        for i in range(rows - 2, -1, -1):
-            T, s = kept_block(t_ref, s_ref, kept_tile(rows, wall, i))
-            put(i, [v + w for v, w in zip(mat_vec(T, x), s)])
-            if after is not None and i % OUT_ROWS == 0:
-                after(i)
-        return
-
     for i in range(rows - 2, -1, -1):
         T, s = kept_block(t_ref, s_ref, kept_tile(rows, wall, i))
         x = [v + w for v, w in zip(mat_vec(T, x), s)]
@@ -478,25 +482,6 @@
     return T, signed(s_ref[a, at, :] for a in range(4))
 
 
-def compose_kernel(rows, t_ref, s_ref, t_out_ref, s_out_ref):
-    wall = lax.axis_index("wall")
-    T, s = None, None
-    for i in range(rows - 2, -1, -1):
-        at = kept_tile(rows, wall, i)
-        T_row, s_row = kept_block(t_ref, s_ref, at)
-        if T is None:
-            T, s = T_row, s_row
-        else:
-            s = [v + w for v, w in zip(mat_vec(T_row, s), s_row)]
-            columns = [mat_vec(T_row, [T[a][b] for a in range(4)]) for b in range(4)]
-            T = [[columns[b][a] for b in range(4)] for a in range(4)]
-        for a in range(4):
-            like = t_ref[0, at, :]
-            for b in range(4):
-                t_out_ref[4 * a + b, at, :] = T[a][b].array(like, T_SIGN[a][b])
-            s_out_ref[a, at, :] = s[a].array(like)
-
-
 def last_substitute_kernel(
     rows, planes, own_ref, near_ref, own_first_ref, near_first_ref, t_ref, s_ref, *refs
 ):
@@ -523,7 +508,7 @@
 
     substitute_kernel(
         rows, parts - 1, own_ref, near_ref, own_first_ref, near_first_ref, t_ref, s_ref,
-        mine_ref, after, COMPOSE_LAST,
+        mine_ref, after,
     )
     for copy in copies:
         copy.wait()
@@ -546,21 +531,29 @@
     charge = fixed_charge.reshape(cells, cols)
     n_span, n_stream = lax.axis_size("span"), lax.axis_size("stream")
 
-    phi, conc, eps, charge, near, far, edge_cols = pl.pallas_call(
+    phi, conc, eps, charge, near, far = pl.pallas_call(
         functools.partial(pack_kernel, rows, planes),
         name="pack",
         out_shape=(
             sds(cells, cols), sds(3, cells, cols), sds(cells, cols), sds(cells, cols),
-            sds(5, rows, cols), sds(5, rows, cols), sds(5, SUB, LANES),
+            sds(5, rows, cols), sds(5, rows, cols),
         ),
         in_specs=[pl.BlockSpec(memory_space=pltpu.HBM)] * 4,
-        out_specs=(VMEM,) * 7,
+        out_specs=(VMEM,) * 6,
         scratch_shapes=[pltpu.SemaphoreType.DMA((6,))],
         compiler_params=params(),
     )(*(pltpu.with_memory_space_constraint(v, pltpu.HBM) for v in (phi, conc, eps, charge)))
 
     near_halo = lax.ppermute(near, "span", swap_pairs(n_span, 1))
     far_halo = lax.ppermute(far, "span", swap_pairs(n_span, 0))
+    edge_cols = pl.pallas_call(
+        functools.partial(columns_kernel, rows, planes),
+        name="columns",
+        out_shape=sds(5, SUB, LANES),
+        in_specs=[VMEM] * 3,
+        out_specs=VMEM,
+        compiler_params=params(),
+    )(phi, conc, eps)
     odd_halo = lax.ppermute(edge_cols, "stream", swap_pairs(n_stream, 1))
     even_halo = lax.ppermute(edge_cols, "stream", swap_pairs(n_stream, 0))
 
@@ -615,15 +608,6 @@
         for part, (tip, tip_m, T, s) in enumerate(solved[:-1])
     ]
     tip, tip_m, T, s = solved[-1]
-    if COMPOSE_LAST:
-        T, s = pl.pallas_call(
-            functools.partial(compose_kernel, rows),
-            name="compose",
-            out_shape=kept,
-            in_specs=[VMEM] * 2,
-            out_specs=(VMEM,) * 2,
-            compiler_params=params(),
-        )(T, s)
     return pl.pallas_call(
         functools.partial(last_substitute_kernel, rows, planes),
         name="substitute",

time: 21.9 us -> 21.7 us (level)
    pallas_call x0 -> x1, Pallas kernels: none -> 0.4 us  [on_device_pair(): pl.pallas_call(functools.partial(columns_kernel, rows, planes), name='col...]
    pallas_call x1, Pallas kernels: 1.73 us -> 1.39 us  [on_device_pair(): pl.pallas_call(functools.partial(pack_kernel, rows, planes), name='pack',...]
    ppermute x1, waiting for transfers between devices: 2.01 us -> 1.73 us  [on_device_pair(): solved.append((tip, lax.ppermute(tip, 'wall', across), T, s))]
  transfers between devices with their start and end apart: 6 -> 6, of which waited for: 2 -> 2; matrix products, arithmetic and copies ran while one was open for 0% -> 0% of each run, Pallas kernels for 22% -> 23%
where the time goes in v5:
time: 21.7 us; the launch traced here: 21.6 us
  Pallas kernels  9 us (41%)
  starting transfers between devices  8.97 us (41%)
  waiting for transfers between devices  3.53 us (16%)
    ppermute x1, starting transfers between devices, on_device_pair(): near_halo = lax.ppermute(near, 'span', swap_pairs(n_span, 1))  5.11 us
    pallas_call x1, Pallas kernels, on_device_pair(): pl.pallas_call(functools.partial(assemble_kernel, rows, planes), name='as...  2.76 us
    ppermute x1, waiting for transfers between devices, on_device_pair(): solved = [(tip, lax.ppermute(tip, 'wall', across), T, s)]  1.79 us
    ppermute x1, waiting for transfers between devices, on_device_pair(): solved.append((tip, lax.ppermute(tip, 'wall', across), T, s))  1.73 us
    ppermute x1, starting transfers between devices, on_device_pair(): odd_halo = lax.ppermute(edge_cols, 'stream', swap_pairs(n_stream, 1))  1.64 us
    ppermute x1, starting transfers between devices, on_device_pair(): solved = [(tip, lax.ppermute(tip, 'wall', across), T, s)]  1.56 us
    pallas_call x1, Pallas kernels, on_device_pair(): pl.pallas_call(functools.partial(first_eliminate_kernel, rows, planes), n...  1.53 us
    pallas_call x1, Pallas kernels, on_device_pair(): pl.pallas_call(functools.partial(eliminate_kernel, rows, planes, part), n...  1.42 us
  transfers between devices with their start and end apart: 6, of which 2 were waited for; matrix products, arithmetic and copies ran while one was open for 0% of the time, Pallas kernels for 23%

profile of v5, /device:TPU:0, one launch (start us, length us, event | category | flops | bytes accessed | tf_op | source)
XLA Modules:
  0.0 21.6 jit_solution(10801773301541853525)
XLA Ops:
  0.0 1.4 %pack.1 = (f32[512,128]{1,0:T(8,128)S(1)}, f32[3,512,128]{2,1,0:T(8,128)S(1)}, f32[512,128]{1,0:T(8,128)S(1)}, f32[512,128]{1,0:T(8,128)S(1)}, f32[5,32,128]{2,1,0:T(8,128)S(1)}, /*index=5*/f32[5,32,128]{2,1,0:T(8,128)S(1)}) custom-call(f32[512,128]{1,0:T(8,128)} %bitcast.7, f32[3,512,128]{2,1,0:T(8,128)} %bitcast.6, f32[512,128]{1,0:T(8,128)} %bitcast.8, ...), custom_call_target="tpu_custom_call" | custom-call | tf_op jit(solution)/shard_map/pack/pallas_call | solution.py:534
  1.4 5.1 %collective-permute-start = (f32[5,32,128]{2,1,0:T(8,128)S(1)}, f32[5,32,128]{2,1,0:T(8,128)S(1)}, u32[]{:S(2)}, u32[]{:S(2)}) collective-permute-start(f32[5,32,128]{2,1,0:T(8,128)S(1)} %get-tuple-element.29.near_ref), channel_id=1, source_target_pairs={{1,2},{2,1},{3,0},{0,3},{5,6},{6,5},{7,4},{4,7},{9,10},{10,9},{11,... | collective-permute-start | bytes 245768 | tf_op jit(solution)/shard_map/ppermute | solution.py:547
  6.5 0.0 collective-permute-start.1
  6.5 0.4 %columns.1.cols_ref = f32[5,8,128]{2,1,0:T(8,128)S(1)} custom-call(f32[512,128]{1,0:T(8,128)S(1)} %get-tuple-element.23.phi_ref, f32[3,512,128]{2,1,0:T(8,128)S(1)} %get-tuple-element.22.conc_ref, f32[512,128]{1,0:T(8,128)S(1)} %get-tuple-element.24.eps_ref), custom_call_target="tpu_custom_call" | custom-call | tf_op jit(solution)/shard_map/columns/pallas_call | solution.py:549
  6.9 0.1 collective-permute-start.2
  7.0 1.6 %collective-permute-start.3 = (f32[5,8,128]{2,1,0:T(8,128)S(1)}, f32[5,8,128]{2,1,0:T(8,128)S(1)}, u32[]{:S(2)}, u32[]{:S(2)}) collective-permute-start(f32[5,8,128]{2,1,0:T(8,128)S(1)} %columns.1.cols_ref), channel_id=1, source_target_pairs={{4,8},{8,4},{12,0},{0,12},{5,9},{9,5},{13,1},{1,13},{6,10},{10,6},... | collective-permute-start | bytes 61448 | tf_op jit(solution)/shard_map/ppermute | solution.py:557
  8.6 2.8 %assemble.1 = (f32[11,512,128]{2,1,0:T(8,128)S(1)}, f32[512,128]{1,0:T(8,128)S(1)}, f32[2,3,512,128]{3,2,1,0:T(8,128)S(1)}) custom-call(f32[512,128]{1,0:T(8,128)S(1)} %get-tuple-element.23.phi_ref, f32[3,512,128]{2,1,0:T(8,128)S(1)} %get-tuple-element.22.conc_ref, f32[512,128]{1,0:T(8,128)S(1)} %get-tuple-element.24.eps_ref, ...), custom_call_target="tpu_custom_call" | custom-call | flops 12000000 | bytes 6000000 | tf_op jit(solution)/shard_map/assemble/pallas_call | solution.py:560
  11.4 0.0 collective-permute-done.2.even_halo_ref
  11.4 0.0 collective-permute-done.3.odd_halo_ref
  11.4 0.0 collective-permute-done.near_halo_ref
  11.4 0.0 collective-permute-done.1.far_halo_ref
  11.4 1.5 %eliminate.2 = (f32[16,256,128]{2,1,0:T(8,128)S(1)}, f32[4,256,128]{2,1,0:T(8,128)S(1)}, f32[30,8,128]{2,1,0:T(8,128)S(1)}, f32[11,8,128]{2,1,0:T(8,128)S(1)}, f32[11,2,32,128]{3,2,1,0:T(8,128)S(1)}) custom-call(f32[512,128]{1,0:T(8,128)S(1)} %get-tuple-element.23.phi_ref, f32[3,512,128]{2,1,0:T(8,128)S(1)} %get-tuple-element.22.conc_ref, ...), custom_call_target="tpu_custom_call" | custom-call | tf_op jit(solution)/shard_map/eliminate/pallas_call | solution.py:575
  13.0 1.6 %collective-permute-start.5 = (f32[30,8,128]{2,1,0:T(8,128)S(1)}, f32[30,8,128]{2,1,0:T(8,128)S(1)}, u32[]{:S(2)}, u32[]{:S(2)}) collective-permute-start(f32[30,8,128]{2,1,0:T(8,128)S(1)} %get-tuple-element.34.own_ref.own_first_ref), channel_id=1, source_target_pairs={{0,16},{16,0},{1,17},{17,1},{2,18},{18,2},{3,19},{19,3},{4,20},{20... | collective-permute-start | bytes 368648 | tf_op jit(solution)/shard_map/ppermute | solution.py:586
  14.6 1.4 %eliminate.3 = (f32[16,256,128]{2,1,0:T(8,128)S(1)}, f32[4,256,128]{2,1,0:T(8,128)S(1)}, f32[20,8,128]{2,1,0:T(8,128)S(1)}) custom-call(f32[3,512,128]{2,1,0:T(8,128)S(1)} %get-tuple-element.22.conc_ref, f32[11,512,128]{2,1,0:T(8,128)S(1)} %get-tuple-element.26.acc_ref, f32[512,128]{1,0:T(8,128)S(1)} %get-tuple-element.27.fe_ref, ...), custom_call_target="tpu_custom_call" | custom-call | tf_op jit(solution)/shard_map/eliminate/pallas_call | solution.py:588
  16.0 0.6 %collective-permute-start.4 = (f32[20,8,128]{2,1,0:T(8,128)S(1)}, f32[20,8,128]{2,1,0:T(8,128)S(1)}, u32[]{:S(2)}, u32[]{:S(2)}) collective-permute-start(f32[20,8,128]{2,1,0:T(8,128)S(1)} %get-tuple-element.33.own_ref), channel_id=1, source_target_pairs={{0,16},{16,0},{1,17},{17,1},{2,18},{18,2},{3,19},{19,3},{4,20},{20... | collective-permute-start | bytes 245768 | tf_op jit(solution)/shard_map/ppermute | solution.py:596
  16.6 1.8 %collective-permute-done.5.near_ref.near_first_ref = f32[30,8,128]{2,1,0:T(8,128)S(1)} collective-permute-done((f32[30,8,128]{2,1,0:T(8,128)S(1)}, f32[30,8,128]{2,1,0:T(8,128)S(1)}, u32[]{:S(2)}, u32[]{:S(2)}) %collective-permute-start.5) | collective-permute-done | bytes 122912 | tf_op jit(solution)/shard_map/ppermute | solution.py:586
  18.3 0.4 %substitute.2 = f32[4,256,128]{2,1,0:T(8,128)S(1)} custom-call(f32[30,8,128]{2,1,0:T(8,128)S(1)} %get-tuple-element.34.own_ref.own_first_ref, f32[30,8,128]{2,1,0:T(8,128)S(1)} %collective-permute-done.5.near_ref.near_first_ref, f32[30,8,128]{2,1,0:T(8,128)S(1)} %get-tuple-element.34.own_ref.own_first_ref, ...), custom_call_target="tpu_custom_call" | custom-call | tf_op jit(solution)/shard_map/substitute/pallas_call | solution.py:600
  18.8 1.7 %collective-permute-done.4.near_ref = f32[20,8,128]{2,1,0:T(8,128)S(1)} collective-permute-done((f32[20,8,128]{2,1,0:T(8,128)S(1)}, f32[20,8,128]{2,1,0:T(8,128)S(1)}, u32[]{:S(2)}, u32[]{:S(2)}) %collective-permute-start.4) | collective-permute-done | bytes 81952 | tf_op jit(solution)/shard_map/ppermute | solution.py:596
  20.5 1.1 %substitute.3 = f32[4,32,16,128]{3,2,1,0:T(8,128)} custom-call(f32[20,8,128]{2,1,0:T(8,128)S(1)} %get-tuple-element.33.own_ref, f32[20,8,128]{2,1,0:T(8,128)S(1)} %collective-permute-done.4.near_ref, f32[30,8,128]{2,1,0:T(8,128)S(1)} %get-tuple-element.34.own_ref.own_first_ref, f32[30,8,128]{2,1,0:T(8,128)S(1)} %collective-permute-done.5.near_ref.near_first_ref, ...), custom_call_target="tpu_custom_call" | custom-call | tf_op jit(solution)/shard_map/substitute/pallas_call | solution.py:611
Async XLA Ops:
  1.4 10.0 %collective-permute-start = (f32[5,32,128]{2,1,0:T(8,128)S(1)}, f32[5,32,128]{2,1,0:T(8,128)S(1)}, u32[]{:S(2)}, u32[]{:S(2)}) collective-permute-start(f32[5,32,128]{2,1,0:T(8,128)S(1)} %get-tuple-element.29.near_ref), channel_id=1, source_target_pairs={{1,2},{2,1},{3,0},{0,3},{5,6},{6,5},{7,4},{4,7},{9,10},{10,9},{11,... | collective-permute-start | bytes 245768 | tf_op jit(solution)/shard_map/ppermute | solution.py:547
  6.5 4.9 %collective-permute-start.1 = (f32[5,32,128]{2,1,0:T(8,128)S(1)}, f32[5,32,128]{2,1,0:T(8,128)S(1)}, u32[]{:S(2)}, u32[]{:S(2)}) collective-permute-start(f32[5,32,128]{2,1,0:T(8,128)S(1)} %get-tuple-element.30.far_ref), channel_id=1, source_target_pairs={{0,1},{1,0},{2,3},{3,2},{4,5},{5,4},{6,7},{7,6},{8,9},{9,8},{10,11... | collective-permute-start | bytes 245768 | tf_op jit(solution)/shard_map/ppermute | solution.py:548
  6.9 4.5 %collective-permute-start.2 = (f32[5,8,128]{2,1,0:T(8,128)S(1)}, f32[5,8,128]{2,1,0:T(8,128)S(1)}, u32[]{:S(2)}, u32[]{:S(2)}) collective-permute-start(f32[5,8,128]{2,1,0:T(8,128)S(1)} %columns.1.cols_ref), channel_id=1, source_target_pairs={{0,4},{4,0},{8,12},{12,8},{1,5},{5,1},{9,13},{13,9},{2,6},{6,2},{1... | collective-permute-start | bytes 61448 | tf_op jit(solution)/shard_map/ppermute | solution.py:558
  7.0 4.4 %collective-permute-start.3 = (f32[5,8,128]{2,1,0:T(8,128)S(1)}, f32[5,8,128]{2,1,0:T(8,128)S(1)}, u32[]{:S(2)}, u32[]{:S(2)}) collective-permute-start(f32[5,8,128]{2,1,0:T(8,128)S(1)} %columns.1.cols_ref), channel_id=1, source_target_pairs={{4,8},{8,4},{12,0},{0,12},{5,9},{9,5},{13,1},{1,13},{6,10},{10,6},... | collective-permute-start | bytes 61448 | tf_op jit(solution)/shard_map/ppermute | solution.py:557
  13.0 5.4 %collective-permute-start.5 = (f32[30,8,128]{2,1,0:T(8,128)S(1)}, f32[30,8,128]{2,1,0:T(8,128)S(1)}, u32[]{:S(2)}, u32[]{:S(2)}) collective-permute-start(f32[30,8,128]{2,1,0:T(8,128)S(1)} %get-tuple-element.34.own_ref.own_first_ref), channel_id=1, source_target_pairs={{0,16},{16,0},{1,17},{17,1},{2,18},{18,2},{3,19},{19,3},{4,20},{20... | collective-permute-start | bytes 368648 | tf_op jit(solution)/shard_map/ppermute | solution.py:586
  16.0 4.5 %collective-permute-start.4 = (f32[20,8,128]{2,1,0:T(8,128)S(1)}, f32[20,8,128]{2,1,0:T(8,128)S(1)}, u32[]{:S(2)}, u32[]{:S(2)}) collective-permute-start(f32[20,8,128]{2,1,0:T(8,128)S(1)} %get-tuple-element.33.own_ref), channel_id=1, source_target_pairs={{0,16},{16,0},{1,17},{17,1},{2,18},{18,2},{3,19},{19,3},{4,20},{20... | collective-permute-start | bytes 245768 | tf_op jit(solution)/shard_map/ppermute | solution.py:596

commit v6 on v5

--- a/solution.py
+++ b/solution.py
@@ -189,18 +189,21 @@
     copies[5].wait()
 
 
-def columns_kernel(rows, planes, phi_ref, conc_ref, eps_ref, cols_ref):
+def columns_kernel(rows, planes, phi_ref, conc_ref, eps_ref, cols_ref, wide_ref):
+    parts = planes // SUB
     pair_of_lane = lax.broadcasted_iota(jnp.int32, (SUB, LANES), 1) // 2
     for f, ref in enumerate([phi_ref, *(conc_ref.at[k] for k in range(3)), eps_ref]):
         packed = jnp.zeros((SUB, LANES), jnp.float32)
         for j in range(rows * planes // SUB):
-            moved = pltpu.roll(ref[SUB * j : SUB * (j + 1), :], 2 * j + 1, 1)
+            tile = ref[SUB * j : SUB * (j + 1), :]
+            wide_ref[f, pl.ds(j // parts * (planes + 1) + SUB * (j % parts), SUB), :] = tile
+            moved = pltpu.roll(tile, 2 * j + 1, 1)
             packed = jnp.where(pair_of_lane == j, moved, packed)
         cols_ref[f] = packed
 
 
 def assemble_kernel(
-    rows, planes, phi_ref, conc_ref, eps_ref, charge_ref,
+    rows, planes, phi_ref, conc_ref, eps_ref, charge_ref, wide_ref,
     acc_ref, fe_ref, fu_ref, span_ref,
 ):
     wall = lax.axis_index("wall")
@@ -208,8 +211,8 @@
     last_wall = 1.0 - first_wall
 
     def cell(p, row0):
-        at = pl.ds(row0 * planes + p, SUB, stride=planes)
-        return phi_ref[at, :], eps_ref[at, :], [conc_ref[k, at, :] for k in range(3)]
+        at = pl.ds(row0 * (planes + 1) + p, SUB, stride=planes + 1)
+        return wide_ref[0, at, :], wide_ref[4, at, :], [wide_ref[1 + k, at, :] for k in range(3)]
 
     for row0 in range(0, rows, SUB):
         zero = jnp.zeros((SUB, LANES), jnp.float32)
@@ -482,33 +485,26 @@
     return T, signed(s_ref[a, at, :] for a in range(4))
 
 
-def last_substitute_kernel(
-    rows, planes, own_ref, near_ref, own_first_ref, near_first_ref, t_ref, s_ref, *refs
+def write_kernel(
+    rows, planes, part, own_ref, near_ref, own_first_ref, near_first_ref, t_ref, s_ref, *refs
 ):
-    *done_refs, out_hbm, mine_ref, sems = refs
-    parts = planes // SUB
+    out_hbm, mine_ref, sems = refs[-3:]
     wall = lax.axis_index("wall")
-
-    def to_hbm(ref, part, chunk, n):
-        at = pl.ds(chunk, n)
-        return pltpu.make_async_copy(
-            ref.at[:, at], out_hbm.at[:, at, pl.ds(SUB * part, SUB), :], sems.at[len(copies)]
-        )
-
+    mine = mine_ref.reshape(4, rows, SUB, LANES)
     copies = []
-    for part, ref in enumerate(done_refs):
-        copies.append(to_hbm(ref, part, 0, rows))
-        copies[-1].start()
-    mine = mine_ref.reshape(4, rows, SUB, LANES)
 
     def after(i):
         first = jnp.where(wall == 0, i, rows - OUT_ROWS - i)
-        copies.append(to_hbm(mine, parts - 1, first, OUT_ROWS))
+        at = pl.ds(first, OUT_ROWS)
+        copies.append(
+            pltpu.make_async_copy(
+                mine.at[:, at], out_hbm.at[:, at, pl.ds(SUB * part, SUB), :], sems.at[len(copies)]
+            )
+        )
         copies[-1].start()
 
     substitute_kernel(
-        rows, parts - 1, own_ref, near_ref, own_first_ref, near_first_ref, t_ref, s_ref,
-        mine_ref, after,
+        rows, part, own_ref, near_ref, own_first_ref, near_first_ref, t_ref, s_ref, mine_ref, after
     )
     for copy in copies:
         copy.wait()
@@ -546,12 +542,12 @@
 
     near_halo = lax.ppermute(near, "span", swap_pairs(n_span, 1))
     far_halo = lax.ppermute(far, "span", swap_pairs(n_span, 0))
-    edge_cols = pl.pallas_call(
+    edge_cols, wide = pl.pallas_call(
         functools.partial(columns_kernel, rows, planes),
         name="columns",
-        out_shape=sds(5, SUB, LANES),
+        out_shape=(sds(5, SUB, LANES), sds(5, rows * (planes + 1), cols)),
         in_specs=[VMEM] * 3,
-        out_specs=VMEM,
+        out_specs=(VMEM,) * 2,
         compiler_params=params(),
     )(phi, conc, eps)
     odd_halo = lax.ppermute(edge_cols, "stream", swap_pairs(n_stream, 1))
@@ -561,12 +557,12 @@
         functools.partial(assemble_kernel, rows, planes),
         name="assemble",
         out_shape=(sds(NQ, cells, cols), sds(cells, cols), sds(2, 3, cells, cols)),
-        in_specs=[VMEM] * 4,
+        in_specs=[VMEM] * 5,
         out_specs=(VMEM,) * 3,
         scratch_shapes=[pltpu.VMEM((NQ, cells + planes, cols), jnp.float32)],
         compiler_params=params(),
         cost_estimate=pl.CostEstimate(flops=12_000_000, bytes_accessed=6_000_000, transcendentals=0),
-    )(phi, conc, eps, charge)
+    )(phi, conc, eps, charge, wide)
 
     parts = planes // SUB
     across = [(0, 1), (1, 0)]
@@ -596,30 +592,23 @@
         solved.append((tip, lax.ppermute(tip, "wall", across), T, s))
 
     fields = solved[0][:2]
-    done = [
-        pl.pallas_call(
-            functools.partial(substitute_kernel, rows, part),
+    update = ()
+    hbm = pl.BlockSpec(memory_space=pltpu.HBM)
+    for part, (tip, tip_m, T, s) in enumerate(solved):
+        update = pl.pallas_call(
+            functools.partial(write_kernel, rows, planes, part),
             name="substitute",
-            out_shape=sds(4, rows * SUB, cols),
-            in_specs=[VMEM] * 6,
-            out_specs=VMEM,
+            out_shape=(sds(4, rows, planes, cols),),
+            in_specs=[VMEM] * 6 + [hbm] * len(update),
+            out_specs=(hbm,),
+            scratch_shapes=[
+                pltpu.VMEM((4, rows * SUB, cols), jnp.float32),
+                pltpu.SemaphoreType.DMA((rows // OUT_ROWS,)),
+            ],
+            input_output_aliases={6: 0} if update else {},
             compiler_params=params(),
-        )(tip, tip_m, *fields, T, s)
-        for part, (tip, tip_m, T, s) in enumerate(solved[:-1])
-    ]
-    tip, tip_m, T, s = solved[-1]
-    return pl.pallas_call(
-        functools.partial(last_substitute_kernel, rows, planes),
-        name="substitute",
-        out_shape=sds(4, rows, planes, cols),
-        in_specs=[VMEM] * (6 + len(done)),
-        out_specs=pl.BlockSpec(memory_space=pltpu.HBM),
-        scratch_shapes=[
-            pltpu.VMEM((4, rows * SUB, cols), jnp.float32),
-            pltpu.SemaphoreType.DMA((parts - 1 + rows // OUT_ROWS,)),
-        ],
-        compiler_params=params(),
-    )(tip, tip_m, *fields, T, s, *(v.reshape(4, rows, SUB, cols) for v in done))
+        )(tip, tip_m, *fields, T, s, *update)
+    return update[0]
 
 
 def with_halo(block, sides, width, periodic):

time: 21.7 us -> 21.5 us (level)
  waiting for transfers between devices: 3.53 us -> 2.83 us
  Pallas kernels: 9 us -> 9.52 us
    pallas_call x2, Pallas kernels: 1.5 us -> 2.19 us  [on_device_pair(): pl.pallas_call(functools.partial(write_kernel, rows, planes, part), name=...]
    ppermute x1, waiting for transfers between devices: 1.73 us -> 1.04 us  [on_device_pair(): solved.append((tip, lax.ppermute(tip, 'wall', across), T, s))]
  transfers between devices with their start and end apart: 6 -> 6, of which waited for: 2 -> 2; matrix products, arithmetic and copies ran while one was open for 0% -> 0% of each run, Pallas kernels for 23% -> 26%
where the time goes in v6:
time: 21.5 us; the launch traced here: 21.4 us
  Pallas kernels  9.52 us (44%)
  starting transfers between devices  8.97 us (42%)
  waiting for transfers between devices  2.83 us (13%)
    ppermute x1, starting transfers between devices, on_device_pair(): near_halo = lax.ppermute(near, 'span', swap_pairs(n_span, 1))  5.11 us
    pallas_call x1, Pallas kernels, on_device_pair(): pl.pallas_call(functools.partial(assemble_kernel, rows, planes), name='as...  2.56 us
    pallas_call x2, Pallas kernels, on_device_pair(): pl.pallas_call(functools.partial(write_kernel, rows, planes, part), name=...  2.19 us
    ppermute x1, waiting for transfers between devices, on_device_pair(): solved = [(tip, lax.ppermute(tip, 'wall', across), T, s)]  1.78 us
    ppermute x1, starting transfers between devices, on_device_pair(): odd_halo = lax.ppermute(edge_cols, 'stream', swap_pairs(n_stream, 1))  1.64 us
    ppermute x1, starting transfers between devices, on_device_pair(): solved = [(tip, lax.ppermute(tip, 'wall', across), T, s)]  1.56 us
    pallas_call x1, Pallas kernels, on_device_pair(): pl.pallas_call(functools.partial(first_eliminate_kernel, rows, planes), n...  1.54 us
    pallas_call x1, Pallas kernels, on_device_pair(): pl.pallas_call(functools.partial(eliminate_kernel, rows, planes, part), n...  1.43 us
  transfers between devices with their start and end apart: 6, of which 2 were waited for; matrix products, arithmetic and copies ran while one was open for 0% of the time, Pallas kernels for 26%

profile of v6, /device:TPU:0, one launch (start us, length us, event | category | flops | bytes accessed | tf_op | source)
XLA Modules:
  0.0 21.4 jit_solution(5990493857283740895)
XLA Ops:
  0.0 1.4 %pack.1 = (f32[512,128]{1,0:T(8,128)S(1)}, f32[3,512,128]{2,1,0:T(8,128)S(1)}, f32[512,128]{1,0:T(8,128)S(1)}, f32[512,128]{1,0:T(8,128)S(1)}, f32[5,32,128]{2,1,0:T(8,128)S(1)}, /*index=5*/f32[5,32,128]{2,1,0:T(8,128)S(1)}) custom-call(f32[512,128]{1,0:T(8,128)} %bitcast.5, f32[3,512,128]{2,1,0:T(8,128)} %bitcast.4, f32[512,128]{1,0:T(8,128)} %bitcast.6, ...), custom_call_target="tpu_custom_call" | custom-call | tf_op jit(solution)/shard_map/pack/pallas_call | solution.py:530
  1.4 5.1 %collective-permute-start = (f32[5,32,128]{2,1,0:T(8,128)S(1)}, f32[5,32,128]{2,1,0:T(8,128)S(1)}, u32[]{:S(2)}, u32[]{:S(2)}) collective-permute-start(f32[5,32,128]{2,1,0:T(8,128)S(1)} %get-tuple-element.32.near_ref), channel_id=1, source_target_pairs={{1,2},{2,1},{3,0},{0,3},{5,6},{6,5},{7,4},{4,7},{9,10},{10,9},{11,... | collective-permute-start | bytes 245768 | tf_op jit(solution)/shard_map/ppermute | solution.py:543
  6.5 0.0 collective-permute-start.1
  6.5 0.4 %columns.1 = (f32[5,8,128]{2,1,0:T(8,128)S(1)}, f32[5,544,128]{2,1,0:T(8,128)S(1)}) custom-call(f32[512,128]{1,0:T(8,128)S(1)} %get-tuple-element.25.phi_ref, f32[3,512,128]{2,1,0:T(8,128)S(1)} %get-tuple-element.24.conc_ref, f32[512,128]{1,0:T(8,128)S(1)} %get-tuple-element.26.eps_ref), custom_call_target="tpu_custom_call" | custom-call | tf_op jit(solution)/shard_map/columns/pallas_call | solution.py:545
  6.9 0.1 collective-permute-start.2
  7.0 1.6 %collective-permute-start.3 = (f32[5,8,128]{2,1,0:T(8,128)S(1)}, f32[5,8,128]{2,1,0:T(8,128)S(1)}, u32[]{:S(2)}, u32[]{:S(2)}) collective-permute-start(f32[5,8,128]{2,1,0:T(8,128)S(1)} %get-tuple-element.34.cols_ref), channel_id=1, source_target_pairs={{4,8},{8,4},{12,0},{0,12},{5,9},{9,5},{13,1},{1,13},{6,10},{10,6},... | collective-permute-start | bytes 61448 | tf_op jit(solution)/shard_map/ppermute | solution.py:553
  8.6 2.6 %assemble.1 = (f32[11,512,128]{2,1,0:T(8,128)S(1)}, f32[512,128]{1,0:T(8,128)S(1)}, f32[2,3,512,128]{3,2,1,0:T(8,128)S(1)}) custom-call(f32[512,128]{1,0:T(8,128)S(1)} %get-tuple-element.25.phi_ref, f32[3,512,128]{2,1,0:T(8,128)S(1)} %get-tuple-element.24.conc_ref, f32[512,128]{1,0:T(8,128)S(1)} %get-tuple-element.26.eps_ref, ...), custom_call_target="tpu_custom_call" | custom-call | flops 12000000 | bytes 6000000 | tf_op jit(solution)/shard_map/assemble/pallas_call | solution.py:556
  11.2 0.0 collective-permute-done.2.even_halo_ref
  11.2 0.0 collective-permute-done.3.odd_halo_ref
  11.2 0.0 collective-permute-done.near_halo_ref
  11.2 0.0 collective-permute-done.1.far_halo_ref
  11.3 1.5 %eliminate.2 = (f32[16,256,128]{2,1,0:T(8,128)S(1)}, f32[4,256,128]{2,1,0:T(8,128)S(1)}, f32[30,8,128]{2,1,0:T(8,128)S(1)}, f32[11,8,128]{2,1,0:T(8,128)S(1)}, f32[11,2,32,128]{3,2,1,0:T(8,128)S(1)}) custom-call(f32[512,128]{1,0:T(8,128)S(1)} %get-tuple-element.25.phi_ref, f32[3,512,128]{2,1,0:T(8,128)S(1)} %get-tuple-element.24.conc_ref, ...), custom_call_target="tpu_custom_call" | custom-call | tf_op jit(solution)/shard_map/eliminate/pallas_call | solution.py:571
  12.8 1.6 %collective-permute-start.5 = (f32[30,8,128]{2,1,0:T(8,128)S(1)}, f32[30,8,128]{2,1,0:T(8,128)S(1)}, u32[]{:S(2)}, u32[]{:S(2)}) collective-permute-start(f32[30,8,128]{2,1,0:T(8,128)S(1)} %get-tuple-element.38.own_ref.own_first_ref), channel_id=1, source_target_pairs={{0,16},{16,0},{1,17},{17,1},{2,18},{18,2},{3,19},{19,3},{4,20},{20... | collective-permute-start | bytes 368648 | tf_op jit(solution)/shard_map/ppermute | solution.py:582
  14.4 1.4 %eliminate.3 = (f32[16,256,128]{2,1,0:T(8,128)S(1)}, f32[4,256,128]{2,1,0:T(8,128)S(1)}, f32[20,8,128]{2,1,0:T(8,128)S(1)}) custom-call(f32[3,512,128]{2,1,0:T(8,128)S(1)} %get-tuple-element.24.conc_ref, f32[11,512,128]{2,1,0:T(8,128)S(1)} %get-tuple-element.29.acc_ref, f32[512,128]{1,0:T(8,128)S(1)} %get-tuple-element.30.fe_ref, ...), custom_call_target="tpu_custom_call" | custom-call | tf_op jit(solution)/shard_map/eliminate/pallas_call | solution.py:584
  15.8 0.6 %collective-permute-start.4 = (f32[20,8,128]{2,1,0:T(8,128)S(1)}, f32[20,8,128]{2,1,0:T(8,128)S(1)}, u32[]{:S(2)}, u32[]{:S(2)}) collective-permute-start(f32[20,8,128]{2,1,0:T(8,128)S(1)} %get-tuple-element.37.own_ref), channel_id=1, source_target_pairs={{0,16},{16,0},{1,17},{17,1},{2,18},{18,2},{3,19},{19,3},{4,20},{20... | collective-permute-start | bytes 245768 | tf_op jit(solution)/shard_map/ppermute | solution.py:592
  16.4 1.8 %collective-permute-done.5.near_ref.near_first_ref = f32[30,8,128]{2,1,0:T(8,128)S(1)} collective-permute-done((f32[30,8,128]{2,1,0:T(8,128)S(1)}, f32[30,8,128]{2,1,0:T(8,128)S(1)}, u32[]{:S(2)}, u32[]{:S(2)}) %collective-permute-start.5) | collective-permute-done | bytes 122912 | tf_op jit(solution)/shard_map/ppermute | solution.py:582
  18.2 1.1 %substitute.2.refs_0_ = f32[4,32,16,128]{3,2,1,0:T(8,128)} custom-call(f32[30,8,128]{2,1,0:T(8,128)S(1)} %get-tuple-element.38.own_ref.own_first_ref, f32[30,8,128]{2,1,0:T(8,128)S(1)} %collective-permute-done.5.near_ref.near_first_ref, f32[30,8,128]{2,1,0:T(8,128)S(1)} %get-tuple-element.38.own_ref.own_first_ref, ...), custom_call_target="tpu_custom_call" | custom-call | tf_op jit(solution)/shard_map/substitute/pallas_call | solution.py:598
  19.3 1.0 %collective-permute-done.4.near_ref = f32[20,8,128]{2,1,0:T(8,128)S(1)} collective-permute-done((f32[20,8,128]{2,1,0:T(8,128)S(1)}, f32[20,8,128]{2,1,0:T(8,128)S(1)}, u32[]{:S(2)}, u32[]{:S(2)}) %collective-permute-start.4) | collective-permute-done | bytes 81952 | tf_op jit(solution)/shard_map/ppermute | solution.py:592
  20.3 1.1 %substitute.3 = f32[4,32,16,128]{3,2,1,0:T(8,128)} custom-call(f32[20,8,128]{2,1,0:T(8,128)S(1)} %get-tuple-element.37.own_ref, f32[20,8,128]{2,1,0:T(8,128)S(1)} %collective-permute-done.4.near_ref, f32[30,8,128]{2,1,0:T(8,128)S(1)} %get-tuple-element.38.own_ref.own_first_ref, ...), custom_call_target="tpu_custom_call", output_to_operand_aliasing={{}: (6, {})} | custom-call | tf_op jit(solution)/shard_map/substitute/pallas_call | solution.py:598
Async XLA Ops:
  1.4 9.8 %collective-permute-start = (f32[5,32,128]{2,1,0:T(8,128)S(1)}, f32[5,32,128]{2,1,0:T(8,128)S(1)}, u32[]{:S(2)}, u32[]{:S(2)}) collective-permute-start(f32[5,32,128]{2,1,0:T(8,128)S(1)} %get-tuple-element.32.near_ref), channel_id=1, source_target_pairs={{1,2},{2,1},{3,0},{0,3},{5,6},{6,5},{7,4},{4,7},{9,10},{10,9},{11,... | collective-permute-start | bytes 245768 | tf_op jit(solution)/shard_map/ppermute | solution.py:543
  6.5 4.7 %collective-permute-start.1 = (f32[5,32,128]{2,1,0:T(8,128)S(1)}, f32[5,32,128]{2,1,0:T(8,128)S(1)}, u32[]{:S(2)}, u32[]{:S(2)}) collective-permute-start(f32[5,32,128]{2,1,0:T(8,128)S(1)} %get-tuple-element.33.far_ref), channel_id=1, source_target_pairs={{0,1},{1,0},{2,3},{3,2},{4,5},{5,4},{6,7},{7,6},{8,9},{9,8},{10,11... | collective-permute-start | bytes 245768 | tf_op jit(solution)/shard_map/ppermute | solution.py:544
  6.9 4.3 %collective-permute-start.2 = (f32[5,8,128]{2,1,0:T(8,128)S(1)}, f32[5,8,128]{2,1,0:T(8,128)S(1)}, u32[]{:S(2)}, u32[]{:S(2)}) collective-permute-start(f32[5,8,128]{2,1,0:T(8,128)S(1)} %get-tuple-element.34.cols_ref), channel_id=1, source_target_pairs={{0,4},{4,0},{8,12},{12,8},{1,5},{5,1},{9,13},{13,9},{2,6},{6,2},{1... | collective-permute-start | bytes 61448 | tf_op jit(solution)/shard_map/ppermute | solution.py:554
  7.0 4.2 %collective-permute-start.3 = (f32[5,8,128]{2,1,0:T(8,128)S(1)}, f32[5,8,128]{2,1,0:T(8,128)S(1)}, u32[]{:S(2)}, u32[]{:S(2)}) collective-permute-start(f32[5,8,128]{2,1,0:T(8,128)S(1)} %get-tuple-element.34.cols_ref), channel_id=1, source_target_pairs={{4,8},{8,4},{12,0},{0,12},{5,9},{9,5},{13,1},{1,13},{6,10},{10,6},... | collective-permute-start | bytes 61448 | tf_op jit(solution)/shard_map/ppermute | solution.py:553
  12.8 5.4 %collective-permute-start.5 = (f32[30,8,128]{2,1,0:T(8,128)S(1)}, f32[30,8,128]{2,1,0:T(8,128)S(1)}, u32[]{:S(2)}, u32[]{:S(2)}) collective-permute-start(f32[30,8,128]{2,1,0:T(8,128)S(1)} %get-tuple-element.38.own_ref.own_first_ref), channel_id=1, source_target_pairs={{0,16},{16,0},{1,17},{17,1},{2,18},{18,2},{3,19},{19,3},{4,20},{20... | collective-permute-start | bytes 368648 | tf_op jit(solution)/shard_map/ppermute | solution.py:582
  15.8 4.5 %collective-permute-start.4 = (f32[20,8,128]{2,1,0:T(8,128)S(1)}, f32[20,8,128]{2,1,0:T(8,128)S(1)}, u32[]{:S(2)}, u32[]{:S(2)}) collective-permute-start(f32[20,8,128]{2,1,0:T(8,128)S(1)} %get-tuple-element.37.own_ref), channel_id=1, source_target_pairs={{0,16},{16,0},{1,17},{17,1},{2,18},{18,2},{3,19},{19,3},{4,20},{20... | collective-permute-start | bytes 245768 | tf_op jit(solution)/shard_map/ppermute | solution.py:592

commit v7 on v6

--- a/solution.py
+++ b/solution.py
@@ -14,7 +14,7 @@
 LANES = 128
 SUB = 8
 NQ = 11
-ASSEMBLE_GROUP = 8
+ASSEMBLE_GROUP = 9
 OUT_ROWS = 8
 
 VMEM = pl.BlockSpec(memory_space=pltpu.VMEM)

time: 21.5 us -> 21.5 us (level)
  no operation moved by 1% of the time
where the time goes in v7:
time: 21.5 us; the launch traced here: 21.3 us
  Pallas kernels  9.46 us (44%)
  starting transfers between devices  8.97 us (42%)
  waiting for transfers between devices  2.83 us (13%)
    ppermute x1, starting transfers between devices, on_device_pair(): near_halo = lax.ppermute(near, 'span', swap_pairs(n_span, 1))  5.11 us
    pallas_call x1, Pallas kernels, on_device_pair(): pl.pallas_call(functools.partial(assemble_kernel, rows, planes), name='as...  2.5 us
    pallas_call x2, Pallas kernels, on_device_pair(): pl.pallas_call(functools.partial(write_kernel, rows, planes, part), name=...  2.19 us
    ppermute x1, waiting for transfers between devices, on_device_pair(): solved = [(tip, lax.ppermute(tip, 'wall', across), T, s)]  1.78 us
    ppermute x1, starting transfers between devices, on_device_pair(): odd_halo = lax.ppermute(edge_cols, 'stream', swap_pairs(n_stream, 1))  1.64 us
    ppermute x1, starting transfers between devices, on_device_pair(): solved = [(tip, lax.ppermute(tip, 'wall', across), T, s)]  1.56 us
    pallas_call x1, Pallas kernels, on_device_pair(): pl.pallas_call(functools.partial(first_eliminate_kernel, rows, planes), n...  1.54 us
    pallas_call x1, Pallas kernels, on_device_pair(): pl.pallas_call(functools.partial(eliminate_kernel, rows, planes, part), n...  1.43 us
  transfers between devices with their start and end apart: 6, of which 2 were waited for; matrix products, arithmetic and copies ran while one was open for 0% of the time, Pallas kernels for 26%

profile of v7, /device:TPU:0, one launch (start us, length us, event | category | flops | bytes accessed | tf_op | source)
XLA Modules:
  0.0 21.3 jit_solution(16447197385601019635)
XLA Ops:
  0.0 1.4 %pack.1 = (f32[512,128]{1,0:T(8,128)S(1)}, f32[3,512,128]{2,1,0:T(8,128)S(1)}, f32[512,128]{1,0:T(8,128)S(1)}, f32[512,128]{1,0:T(8,128)S(1)}, f32[5,32,128]{2,1,0:T(8,128)S(1)}, /*index=5*/f32[5,32,128]{2,1,0:T(8,128)S(1)}) custom-call(f32[512,128]{1,0:T(8,128)} %bitcast.5, f32[3,512,128]{2,1,0:T(8,128)} %bitcast.4, f32[512,128]{1,0:T(8,128)} %bitcast.6, ...), custom_call_target="tpu_custom_call" | custom-call | tf_op jit(solution)/shard_map/pack/pallas_call | solution.py:530
  1.4 5.1 %collective-permute-start = (f32[5,32,128]{2,1,0:T(8,128)S(1)}, f32[5,32,128]{2,1,0:T(8,128)S(1)}, u32[]{:S(2)}, u32[]{:S(2)}) collective-permute-start(f32[5,32,128]{2,1,0:T(8,128)S(1)} %get-tuple-element.32.near_ref), channel_id=1, source_target_pairs={{1,2},{2,1},{3,0},{0,3},{5,6},{6,5},{7,4},{4,7},{9,10},{10,9},{11,... | collective-permute-start | bytes 245768 | tf_op jit(solution)/shard_map/ppermute | solution.py:543
  6.5 0.0 collective-permute-start.1
  6.5 0.4 %columns.1 = (f32[5,8,128]{2,1,0:T(8,128)S(1)}, f32[5,544,128]{2,1,0:T(8,128)S(1)}) custom-call(f32[512,128]{1,0:T(8,128)S(1)} %get-tuple-element.25.phi_ref, f32[3,512,128]{2,1,0:T(8,128)S(1)} %get-tuple-element.24.conc_ref, f32[512,128]{1,0:T(8,128)S(1)} %get-tuple-element.26.eps_ref), custom_call_target="tpu_custom_call" | custom-call | tf_op jit(solution)/shard_map/columns/pallas_call | solution.py:545
  6.9 0.1 collective-permute-start.2
  7.0 1.6 %collective-permute-start.3 = (f32[5,8,128]{2,1,0:T(8,128)S(1)}, f32[5,8,128]{2,1,0:T(8,128)S(1)}, u32[]{:S(2)}, u32[]{:S(2)}) collective-permute-start(f32[5,8,128]{2,1,0:T(8,128)S(1)} %get-tuple-element.34.cols_ref), channel_id=1, source_target_pairs={{4,8},{8,4},{12,0},{0,12},{5,9},{9,5},{13,1},{1,13},{6,10},{10,6},... | collective-permute-start | bytes 61448 | tf_op jit(solution)/shard_map/ppermute | solution.py:553
  8.6 2.5 %assemble.1 = (f32[11,512,128]{2,1,0:T(8,128)S(1)}, f32[512,128]{1,0:T(8,128)S(1)}, f32[2,3,512,128]{3,2,1,0:T(8,128)S(1)}) custom-call(f32[512,128]{1,0:T(8,128)S(1)} %get-tuple-element.25.phi_ref, f32[3,512,128]{2,1,0:T(8,128)S(1)} %get-tuple-element.24.conc_ref, f32[512,128]{1,0:T(8,128)S(1)} %get-tuple-element.26.eps_ref, ...), custom_call_target="tpu_custom_call" | custom-call | flops 12000000 | bytes 6000000 | tf_op jit(solution)/shard_map/assemble/pallas_call | solution.py:556
  11.2 0.0 collective-permute-done.2.even_halo_ref
  11.2 0.0 collective-permute-done.3.odd_halo_ref
  11.2 0.0 collective-permute-done.near_halo_ref
  11.2 0.0 collective-permute-done.1.far_halo_ref
  11.2 1.5 %eliminate.2 = (f32[16,256,128]{2,1,0:T(8,128)S(1)}, f32[4,256,128]{2,1,0:T(8,128)S(1)}, f32[30,8,128]{2,1,0:T(8,128)S(1)}, f32[11,8,128]{2,1,0:T(8,128)S(1)}, f32[11,2,32,128]{3,2,1,0:T(8,128)S(1)}) custom-call(f32[512,128]{1,0:T(8,128)S(1)} %get-tuple-element.25.phi_ref, f32[3,512,128]{2,1,0:T(8,128)S(1)} %get-tuple-element.24.conc_ref, ...), custom_call_target="tpu_custom_call" | custom-call | tf_op jit(solution)/shard_map/eliminate/pallas_call | solution.py:571
  12.7 1.6 %collective-permute-start.5 = (f32[30,8,128]{2,1,0:T(8,128)S(1)}, f32[30,8,128]{2,1,0:T(8,128)S(1)}, u32[]{:S(2)}, u32[]{:S(2)}) collective-permute-start(f32[30,8,128]{2,1,0:T(8,128)S(1)} %get-tuple-element.38.own_ref.own_first_ref), channel_id=1, source_target_pairs={{0,16},{16,0},{1,17},{17,1},{2,18},{18,2},{3,19},{19,3},{4,20},{20... | collective-permute-start | bytes 368648 | tf_op jit(solution)/shard_map/ppermute | solution.py:582
  14.3 1.4 %eliminate.3 = (f32[16,256,128]{2,1,0:T(8,128)S(1)}, f32[4,256,128]{2,1,0:T(8,128)S(1)}, f32[20,8,128]{2,1,0:T(8,128)S(1)}) custom-call(f32[3,512,128]{2,1,0:T(8,128)S(1)} %get-tuple-element.24.conc_ref, f32[11,512,128]{2,1,0:T(8,128)S(1)} %get-tuple-element.29.acc_ref, f32[512,128]{1,0:T(8,128)S(1)} %get-tuple-element.30.fe_ref, ...), custom_call_target="tpu_custom_call" | custom-call | tf_op jit(solution)/shard_map/eliminate/pallas_call | solution.py:584
  15.7 0.6 %collective-permute-start.4 = (f32[20,8,128]{2,1,0:T(8,128)S(1)}, f32[20,8,128]{2,1,0:T(8,128)S(1)}, u32[]{:S(2)}, u32[]{:S(2)}) collective-permute-start(f32[20,8,128]{2,1,0:T(8,128)S(1)} %get-tuple-element.37.own_ref), channel_id=1, source_target_pairs={{0,16},{16,0},{1,17},{17,1},{2,18},{18,2},{3,19},{19,3},{4,20},{20... | collective-permute-start | bytes 245768 | tf_op jit(solution)/shard_map/ppermute | solution.py:592
  16.3 1.8 %collective-permute-done.5.near_ref.near_first_ref = f32[30,8,128]{2,1,0:T(8,128)S(1)} collective-permute-done((f32[30,8,128]{2,1,0:T(8,128)S(1)}, f32[30,8,128]{2,1,0:T(8,128)S(1)}, u32[]{:S(2)}, u32[]{:S(2)}) %collective-permute-start.5) | collective-permute-done | bytes 122912 | tf_op jit(solution)/shard_map/ppermute | solution.py:582
  18.1 1.1 %substitute.2.refs_0_ = f32[4,32,16,128]{3,2,1,0:T(8,128)} custom-call(f32[30,8,128]{2,1,0:T(8,128)S(1)} %get-tuple-element.38.own_ref.own_first_ref, f32[30,8,128]{2,1,0:T(8,128)S(1)} %collective-permute-done.5.near_ref.near_first_ref, f32[30,8,128]{2,1,0:T(8,128)S(1)} %get-tuple-element.38.own_ref.own_first_ref, ...), custom_call_target="tpu_custom_call" | custom-call | tf_op jit(solution)/shard_map/substitute/pallas_call | solution.py:598
  19.2 1.0 %collective-permute-done.4.near_ref = f32[20,8,128]{2,1,0:T(8,128)S(1)} collective-permute-done((f32[20,8,128]{2,1,0:T(8,128)S(1)}, f32[20,8,128]{2,1,0:T(8,128)S(1)}, u32[]{:S(2)}, u32[]{:S(2)}) %collective-permute-start.4) | collective-permute-done | bytes 81952 | tf_op jit(solution)/shard_map/ppermute | solution.py:592
  20.2 1.1 %substitute.3 = f32[4,32,16,128]{3,2,1,0:T(8,128)} custom-call(f32[20,8,128]{2,1,0:T(8,128)S(1)} %get-tuple-element.37.own_ref, f32[20,8,128]{2,1,0:T(8,128)S(1)} %collective-permute-done.4.near_ref, f32[30,8,128]{2,1,0:T(8,128)S(1)} %get-tuple-element.38.own_ref.own_first_ref, ...), custom_call_target="tpu_custom_call", output_to_operand_aliasing={{}: (6, {})} | custom-call | tf_op jit(solution)/shard_map/substitute/pallas_call | solution.py:598
Async XLA Ops:
  1.4 9.8 %collective-permute-start = (f32[5,32,128]{2,1,0:T(8,128)S(1)}, f32[5,32,128]{2,1,0:T(8,128)S(1)}, u32[]{:S(2)}, u32[]{:S(2)}) collective-permute-start(f32[5,32,128]{2,1,0:T(8,128)S(1)} %get-tuple-element.32.near_ref), channel_id=1, source_target_pairs={{1,2},{2,1},{3,0},{0,3},{5,6},{6,5},{7,4},{4,7},{9,10},{10,9},{11,... | collective-permute-start | bytes 245768 | tf_op jit(solution)/shard_map/ppermute | solution.py:543
  6.5 4.7 %collective-permute-start.1 = (f32[5,32,128]{2,1,0:T(8,128)S(1)}, f32[5,32,128]{2,1,0:T(8,128)S(1)}, u32[]{:S(2)}, u32[]{:S(2)}) collective-permute-start(f32[5,32,128]{2,1,0:T(8,128)S(1)} %get-tuple-element.33.far_ref), channel_id=1, source_target_pairs={{0,1},{1,0},{2,3},{3,2},{4,5},{5,4},{6,7},{7,6},{8,9},{9,8},{10,11... | collective-permute-start | bytes 245768 | tf_op jit(solution)/shard_map/ppermute | solution.py:544
  6.9 4.2 %collective-permute-start.2 = (f32[5,8,128]{2,1,0:T(8,128)S(1)}, f32[5,8,128]{2,1,0:T(8,128)S(1)}, u32[]{:S(2)}, u32[]{:S(2)}) collective-permute-start(f32[5,8,128]{2,1,0:T(8,128)S(1)} %get-tuple-element.34.cols_ref), channel_id=1, source_target_pairs={{0,4},{4,0},{8,12},{12,8},{1,5},{5,1},{9,13},{13,9},{2,6},{6,2},{1... | collective-permute-start | bytes 61448 | tf_op jit(solution)/shard_map/ppermute | solution.py:554
  7.0 4.2 %collective-permute-start.3 = (f32[5,8,128]{2,1,0:T(8,128)S(1)}, f32[5,8,128]{2,1,0:T(8,128)S(1)}, u32[]{:S(2)}, u32[]{:S(2)}) collective-permute-start(f32[5,8,128]{2,1,0:T(8,128)S(1)} %get-tuple-element.34.cols_ref), channel_id=1, source_target_pairs={{4,8},{8,4},{12,0},{0,12},{5,9},{9,5},{13,1},{1,13},{6,10},{10,6},... | collective-permute-start | bytes 61448 | tf_op jit(solution)/shard_map/ppermute | solution.py:553
  12.7 5.4 %collective-permute-start.5 = (f32[30,8,128]{2,1,0:T(8,128)S(1)}, f32[30,8,128]{2,1,0:T(8,128)S(1)}, u32[]{:S(2)}, u32[]{:S(2)}) collective-permute-start(f32[30,8,128]{2,1,0:T(8,128)S(1)} %get-tuple-element.38.own_ref.own_first_ref), channel_id=1, source_target_pairs={{0,16},{16,0},{1,17},{17,1},{2,18},{18,2},{3,19},{19,3},{4,20},{20... | collective-permute-start | bytes 368648 | tf_op jit(solution)/shard_map/ppermute | solution.py:582
  15.7 4.5 %collective-permute-start.4 = (f32[20,8,128]{2,1,0:T(8,128)S(1)}, f32[20,8,128]{2,1,0:T(8,128)S(1)}, u32[]{:S(2)}, u32[]{:S(2)}) collective-permute-start(f32[20,8,128]{2,1,0:T(8,128)S(1)} %get-tuple-element.37.own_ref), channel_id=1, source_target_pairs={{0,16},{16,0},{1,17},{17,1},{2,18},{18,2},{3,19},{19,3},{4,20},{20... | collective-permute-start | bytes 245768 | tf_op jit(solution)/shard_map/ppermute | solution.py:592

commit v8 on v7

--- a/solution.py
+++ b/solution.py
@@ -15,7 +15,7 @@
 SUB = 8
 NQ = 11
 ASSEMBLE_GROUP = 9
-OUT_ROWS = 8
+OUT_ROWS = 16
 
 VMEM = pl.BlockSpec(memory_space=pltpu.VMEM)
 

time: 21.5 us -> 21.5 us (level)
  transfers between devices with their start and end apart: 6 -> 6, of which waited for: 2 -> 2; matrix products, arithmetic and copies ran while one was open for 0% -> 0% of each run, Pallas kernels for 26% -> 25%
where the time goes in v8:
time: 21.5 us; the launch traced here: 21.4 us
  Pallas kernels  9.51 us (44%)
  starting transfers between devices  8.97 us (42%)
  waiting for transfers between devices  2.8 us (13%)
    ppermute x1, starting transfers between devices, on_device_pair(): near_halo = lax.ppermute(near, 'span', swap_pairs(n_span, 1))  5.11 us
    pallas_call x1, Pallas kernels, on_device_pair(): pl.pallas_call(functools.partial(assemble_kernel, rows, planes), name='as...  2.5 us
    pallas_call x2, Pallas kernels, on_device_pair(): pl.pallas_call(functools.partial(write_kernel, rows, planes, part), name=...  2.24 us
    ppermute x1, waiting for transfers between devices, on_device_pair(): solved = [(tip, lax.ppermute(tip, 'wall', across), T, s)]  1.78 us
    ppermute x1, starting transfers between devices, on_device_pair(): odd_halo = lax.ppermute(edge_cols, 'stream', swap_pairs(n_stream, 1))  1.64 us
    ppermute x1, starting transfers between devices, on_device_pair(): solved = [(tip, lax.ppermute(tip, 'wall', across), T, s)]  1.56 us
    pallas_call x1, Pallas kernels, on_device_pair(): pl.pallas_call(functools.partial(first_eliminate_kernel, rows, planes), n...  1.54 us
    pallas_call x1, Pallas kernels, on_device_pair(): pl.pallas_call(functools.partial(eliminate_kernel, rows, planes, part), n...  1.43 us
  transfers between devices with their start and end apart: 6, of which 2 were waited for; matrix products, arithmetic and copies ran while one was open for 0% of the time, Pallas kernels for 25%

profile of v8, /device:TPU:0, one launch (start us, length us, event | category | flops | bytes accessed | tf_op | source)
XLA Modules:
  0.0 21.4 jit_solution(73146145519602135)
XLA Ops:
  0.0 1.4 %pack.1 = (f32[512,128]{1,0:T(8,128)S(1)}, f32[3,512,128]{2,1,0:T(8,128)S(1)}, f32[512,128]{1,0:T(8,128)S(1)}, f32[512,128]{1,0:T(8,128)S(1)}, f32[5,32,128]{2,1,0:T(8,128)S(1)}, /*index=5*/f32[5,32,128]{2,1,0:T(8,128)S(1)}) custom-call(f32[512,128]{1,0:T(8,128)} %bitcast.5, f32[3,512,128]{2,1,0:T(8,128)} %bitcast.4, f32[512,128]{1,0:T(8,128)} %bitcast.6, ...), custom_call_target="tpu_custom_call" | custom-call | tf_op jit(solution)/shard_map/pack/pallas_call | solution.py:530
  1.4 5.1 %collective-permute-start = (f32[5,32,128]{2,1,0:T(8,128)S(1)}, f32[5,32,128]{2,1,0:T(8,128)S(1)}, u32[]{:S(2)}, u32[]{:S(2)}) collective-permute-start(f32[5,32,128]{2,1,0:T(8,128)S(1)} %get-tuple-element.32.near_ref), channel_id=1, source_target_pairs={{1,2},{2,1},{3,0},{0,3},{5,6},{6,5},{7,4},{4,7},{9,10},{10,9},{11,... | collective-permute-start | bytes 245768 | tf_op jit(solution)/shard_map/ppermute | solution.py:543
  6.5 0.0 collective-permute-start.1
  6.5 0.4 %columns.1 = (f32[5,8,128]{2,1,0:T(8,128)S(1)}, f32[5,544,128]{2,1,0:T(8,128)S(1)}) custom-call(f32[512,128]{1,0:T(8,128)S(1)} %get-tuple-element.25.phi_ref, f32[3,512,128]{2,1,0:T(8,128)S(1)} %get-tuple-element.24.conc_ref, f32[512,128]{1,0:T(8,128)S(1)} %get-tuple-element.26.eps_ref), custom_call_target="tpu_custom_call" | custom-call | tf_op jit(solution)/shard_map/columns/pallas_call | solution.py:545
  6.9 0.1 collective-permute-start.2
  7.0 1.6 %collective-permute-start.3 = (f32[5,8,128]{2,1,0:T(8,128)S(1)}, f32[5,8,128]{2,1,0:T(8,128)S(1)}, u32[]{:S(2)}, u32[]{:S(2)}) collective-permute-start(f32[5,8,128]{2,1,0:T(8,128)S(1)} %get-tuple-element.34.cols_ref), channel_id=1, source_target_pairs={{4,8},{8,4},{12,0},{0,12},{5,9},{9,5},{13,1},{1,13},{6,10},{10,6},... | collective-permute-start | bytes 61448 | tf_op jit(solution)/shard_map/ppermute | solution.py:553
  8.6 2.5 %assemble.1 = (f32[11,512,128]{2,1,0:T(8,128)S(1)}, f32[512,128]{1,0:T(8,128)S(1)}, f32[2,3,512,128]{3,2,1,0:T(8,128)S(1)}) custom-call(f32[512,128]{1,0:T(8,128)S(1)} %get-tuple-element.25.phi_ref, f32[3,512,128]{2,1,0:T(8,128)S(1)} %get-tuple-element.24.conc_ref, f32[512,128]{1,0:T(8,128)S(1)} %get-tuple-element.26.eps_ref, ...), custom_call_target="tpu_custom_call" | custom-call | flops 12000000 | bytes 6000000 | tf_op jit(solution)/shard_map/assemble/pallas_call | solution.py:556
  11.2 0.0 collective-permute-done.2.even_halo_ref
  11.2 0.0 collective-permute-done.3.odd_halo_ref
  11.2 0.0 collective-permute-done.near_halo_ref
  11.2 0.0 collective-permute-done.1.far_halo_ref
  11.2 1.5 %eliminate.2 = (f32[16,256,128]{2,1,0:T(8,128)S(1)}, f32[4,256,128]{2,1,0:T(8,128)S(1)}, f32[30,8,128]{2,1,0:T(8,128)S(1)}, f32[11,8,128]{2,1,0:T(8,128)S(1)}, f32[11,2,32,128]{3,2,1,0:T(8,128)S(1)}) custom-call(f32[512,128]{1,0:T(8,128)S(1)} %get-tuple-element.25.phi_ref, f32[3,512,128]{2,1,0:T(8,128)S(1)} %get-tuple-element.24.conc_ref, ...), custom_call_target="tpu_custom_call" | custom-call | tf_op jit(solution)/shard_map/eliminate/pallas_call | solution.py:571
  12.7 1.6 %collective-permute-start.5 = (f32[30,8,128]{2,1,0:T(8,128)S(1)}, f32[30,8,128]{2,1,0:T(8,128)S(1)}, u32[]{:S(2)}, u32[]{:S(2)}) collective-permute-start(f32[30,8,128]{2,1,0:T(8,128)S(1)} %get-tuple-element.38.own_ref.own_first_ref), channel_id=1, source_target_pairs={{0,16},{16,0},{1,17},{17,1},{2,18},{18,2},{3,19},{19,3},{4,20},{20... | collective-permute-start | bytes 368648 | tf_op jit(solution)/shard_map/ppermute | solution.py:582
  14.3 1.4 %eliminate.3 = (f32[16,256,128]{2,1,0:T(8,128)S(1)}, f32[4,256,128]{2,1,0:T(8,128)S(1)}, f32[20,8,128]{2,1,0:T(8,128)S(1)}) custom-call(f32[3,512,128]{2,1,0:T(8,128)S(1)} %get-tuple-element.24.conc_ref, f32[11,512,128]{2,1,0:T(8,128)S(1)} %get-tuple-element.29.acc_ref, f32[512,128]{1,0:T(8,128)S(1)} %get-tuple-element.30.fe_ref, ...), custom_call_target="tpu_custom_call" | custom-call | tf_op jit(solution)/shard_map/eliminate/pallas_call | solution.py:584
  15.7 0.6 %collective-permute-start.4 = (f32[20,8,128]{2,1,0:T(8,128)S(1)}, f32[20,8,128]{2,1,0:T(8,128)S(1)}, u32[]{:S(2)}, u32[]{:S(2)}) collective-permute-start(f32[20,8,128]{2,1,0:T(8,128)S(1)} %get-tuple-element.37.own_ref), channel_id=1, source_target_pairs={{0,16},{16,0},{1,17},{17,1},{2,18},{18,2},{3,19},{19,3},{4,20},{20... | collective-permute-start | bytes 245768 | tf_op jit(solution)/shard_map/ppermute | solution.py:592
  16.3 1.8 %collective-permute-done.5.near_ref.near_first_ref = f32[30,8,128]{2,1,0:T(8,128)S(1)} collective-permute-done((f32[30,8,128]{2,1,0:T(8,128)S(1)}, f32[30,8,128]{2,1,0:T(8,128)S(1)}, u32[]{:S(2)}, u32[]{:S(2)}) %collective-permute-start.5) | collective-permute-done | bytes 122912 | tf_op jit(solution)/shard_map/ppermute | solution.py:582
  18.1 1.1 %substitute.2.refs_0_ = f32[4,32,16,128]{3,2,1,0:T(8,128)} custom-call(f32[30,8,128]{2,1,0:T(8,128)S(1)} %get-tuple-element.38.own_ref.own_first_ref, f32[30,8,128]{2,1,0:T(8,128)S(1)} %collective-permute-done.5.near_ref.near_first_ref, f32[30,8,128]{2,1,0:T(8,128)S(1)} %get-tuple-element.38.own_ref.own_first_ref, ...), custom_call_target="tpu_custom_call" | custom-call | tf_op jit(solution)/shard_map/substitute/pallas_call | solution.py:598
  19.2 1.0 %collective-permute-done.4.near_ref = f32[20,8,128]{2,1,0:T(8,128)S(1)} collective-permute-done((f32[20,8,128]{2,1,0:T(8,128)S(1)}, f32[20,8,128]{2,1,0:T(8,128)S(1)}, u32[]{:S(2)}, u32[]{:S(2)}) %collective-permute-start.4) | collective-permute-done | bytes 81952 | tf_op jit(solution)/shard_map/ppermute | solution.py:592
  20.2 1.1 %substitute.3 = f32[4,32,16,128]{3,2,1,0:T(8,128)} custom-call(f32[20,8,128]{2,1,0:T(8,128)S(1)} %get-tuple-element.37.own_ref, f32[20,8,128]{2,1,0:T(8,128)S(1)} %collective-permute-done.4.near_ref, f32[30,8,128]{2,1,0:T(8,128)S(1)} %get-tuple-element.38.own_ref.own_first_ref, ...), custom_call_target="tpu_custom_call", output_to_operand_aliasing={{}: (6, {})} | custom-call | tf_op jit(solution)/shard_map/substitute/pallas_call | solution.py:598
Async XLA Ops:
  1.4 9.8 %collective-permute-start = (f32[5,32,128]{2,1,0:T(8,128)S(1)}, f32[5,32,128]{2,1,0:T(8,128)S(1)}, u32[]{:S(2)}, u32[]{:S(2)}) collective-permute-start(f32[5,32,128]{2,1,0:T(8,128)S(1)} %get-tuple-element.32.near_ref), channel_id=1, source_target_pairs={{1,2},{2,1},{3,0},{0,3},{5,6},{6,5},{7,4},{4,7},{9,10},{10,9},{11,... | collective-permute-start | bytes 245768 | tf_op jit(solution)/shard_map/ppermute | solution.py:543
  6.5 4.7 %collective-permute-start.1 = (f32[5,32,128]{2,1,0:T(8,128)S(1)}, f32[5,32,128]{2,1,0:T(8,128)S(1)}, u32[]{:S(2)}, u32[]{:S(2)}) collective-permute-start(f32[5,32,128]{2,1,0:T(8,128)S(1)} %get-tuple-element.33.far_ref), channel_id=1, source_target_pairs={{0,1},{1,0},{2,3},{3,2},{4,5},{5,4},{6,7},{7,6},{8,9},{9,8},{10,11... | collective-permute-start | bytes 245768 | tf_op jit(solution)/shard_map/ppermute | solution.py:544
  6.9 4.2 %collective-permute-start.2 = (f32[5,8,128]{2,1,0:T(8,128)S(1)}, f32[5,8,128]{2,1,0:T(8,128)S(1)}, u32[]{:S(2)}, u32[]{:S(2)}) collective-permute-start(f32[5,8,128]{2,1,0:T(8,128)S(1)} %get-tuple-element.34.cols_ref), channel_id=1, source_target_pairs={{0,4},{4,0},{8,12},{12,8},{1,5},{5,1},{9,13},{13,9},{2,6},{6,2},{1... | collective-permute-start | bytes 61448 | tf_op jit(solution)/shard_map/ppermute | solution.py:554
  7.0 4.2 %collective-permute-start.3 = (f32[5,8,128]{2,1,0:T(8,128)S(1)}, f32[5,8,128]{2,1,0:T(8,128)S(1)}, u32[]{:S(2)}, u32[]{:S(2)}) collective-permute-start(f32[5,8,128]{2,1,0:T(8,128)S(1)} %get-tuple-element.34.cols_ref), channel_id=1, source_target_pairs={{4,8},{8,4},{12,0},{0,12},{5,9},{9,5},{13,1},{1,13},{6,10},{10,6},... | collective-permute-start | bytes 61448 | tf_op jit(solution)/shard_map/ppermute | solution.py:553
  12.7 5.4 %collective-permute-start.5 = (f32[30,8,128]{2,1,0:T(8,128)S(1)}, f32[30,8,128]{2,1,0:T(8,128)S(1)}, u32[]{:S(2)}, u32[]{:S(2)}) collective-permute-start(f32[30,8,128]{2,1,0:T(8,128)S(1)} %get-tuple-element.38.own_ref.own_first_ref), channel_id=1, source_target_pairs={{0,16},{16,0},{1,17},{17,1},{2,18},{18,2},{3,19},{19,3},{4,20},{20... | collective-permute-start | bytes 368648 | tf_op jit(solution)/shard_map/ppermute | solution.py:582
  15.7 4.5 %collective-permute-start.4 = (f32[20,8,128]{2,1,0:T(8,128)S(1)}, f32[20,8,128]{2,1,0:T(8,128)S(1)}, u32[]{:S(2)}, u32[]{:S(2)}) collective-permute-start(f32[20,8,128]{2,1,0:T(8,128)S(1)} %get-tuple-element.37.own_ref), channel_id=1, source_target_pairs={{0,16},{16,0},{1,17},{17,1},{2,18},{18,2},{3,19},{19,3},{4,20},{20... | collective-permute-start | bytes 245768 | tf_op jit(solution)/shard_map/ppermute | solution.py:592
